TPU v7x, 32 devices: a whole 2x2x4 slice. The times are simulated.
32 devices in a mesh: label: 16 (over z, x, core), doc: 2 (over y).
Axes of the slice: x: 2, y: 2, z: 4, core: 2. Of those that a mesh axis runs over, the one named last changes fastest.
Arguments:
- tokens: bfloat16 [32, 128, 768], P(('label', 'doc')), may hold values from -6 to 6
- norm_gains: float32 [2, 768], replicated, may hold values from 0.1 to 1.9
- enc_weight: bfloat16 [768, 768], replicated, may hold values from -0.21875 to 0.21875
- head_weight: bfloat16 [16384, 768], P(('label', 'doc')), may hold values from -0.59765625 to 0.59765625
- head_bias: bfloat16 [16384], P(('label', 'doc')), may hold values from -12 to -7
- positives: int32 [32, 8], P(('label', 'doc')), may hold values from -1 to 16383, as said below
Outputs:
- row_grad: float32 [32, 768], P(('label', 'doc'))
- weight_grad: float32 [768, 768], replicated
- gain_grads: float32 [2, 768], replicated
Inputs may be any that keep to these rules, and one draw needn't show every extreme that they name: `positives`: each document lists 3 to 8 label ids at the front of its row and -1 in the remaining slots; an id may repeat within a row and then counts once.
All inputs are finite; a program needn't handle non-finite values.
Results may differ from a plain program's by a relative error of at most 0.0025.
The roundings to bfloat16 on the way count: a program that leaves them out, or rounds other values in their place, can miss the bound.
Values may be sent and summed in bfloat16 or wider, within the bound.
No kernel may reach another device: no remote copies, remote signals or barrier semaphores. Data moves between devices by JAX's collectives and lax.ppermute only.
A program may use at most 64 MiB of HBM per device.

v0:
```python
import jax
import jax.numpy as jnp
from jax import lax
from jax.sharding import PartitionSpec as P

epsilon = 1e-05


def normalize(values):
    center = values - jnp.mean(values, axis=-1, keepdims=True)
    inverse = lax.rsqrt(jnp.mean(center * center, axis=-1, keepdims=True) + epsilon)
    return (center * inverse, inverse)


def encode(tok_block, gains, enc_weight):
    width = tok_block.shape[-1]
    tok_flat = tok_block.reshape(-1, width).astype(jnp.float32)
    normed_in, _ = normalize(tok_flat)
    act_in = (normed_in * gains[0]).astype(jnp.bfloat16)
    pre_act = jnp.dot(act_in, enc_weight, preferred_element_type=jnp.float32)
    hidden = tok_flat + jax.nn.gelu(pre_act)
    pooled = jnp.mean(hidden.reshape(tok_block.shape[0], tok_block.shape[1], width), axis=1)
    normed_out, inv_out = normalize(pooled)
    return (normed_out * gains[1], (normed_in, act_in, pre_act, normed_out, inv_out))


def encode_back(cotangent, saved, gains, enc_weight, seq_len):
    normed_in, act_in, pre_act, normed_out, inv_out = saved
    gain_out_grad = jnp.sum(cotangent * normed_out, axis=0)
    d_normed = cotangent * gains[1]
    d_pooled = inv_out * (
        d_normed
        - jnp.mean(d_normed, axis=-1, keepdims=True)
        - normed_out * jnp.mean(d_normed * normed_out, axis=-1, keepdims=True)
    )
    spread_grad = jnp.broadcast_to(
        (d_pooled / seq_len)[:, None, :], (d_pooled.shape[0], seq_len, d_pooled.shape[1])
    ).reshape(pre_act.shape)
    _, gelu_back = jax.vjp(jax.nn.gelu, pre_act)
    d_pre = gelu_back(spread_grad)[0]
    weight_grad = lax.dot_general(
        act_in.astype(jnp.float32),
        d_pre,
        (((0,), (0,)), ((), ())),
        precision=lax.Precision.HIGHEST,
        preferred_element_type=jnp.float32,
    )
    d_act = lax.dot_general(
        d_pre,
        enc_weight.astype(jnp.float32),
        (((1,), (1,)), ((), ())),
        precision=lax.Precision.HIGHEST,
        preferred_element_type=jnp.float32,
    )
    gain_in_grad = jnp.sum(d_act * normed_in, axis=0)
    return (weight_grad, jnp.stack([gain_in_grad, gain_out_grad]))


def head_block(embed_bf, label_lists, weight_block, bias_block, first_label):
    logits = lax.dot_general(
        embed_bf, weight_block, (((1,), (1,)), ((), ())), preferred_element_type=jnp.float32
    )
    logits = logits + bias_block.astype(jnp.float32)[None, :]
    label_ids = first_label + jnp.arange(weight_block.shape[0], dtype=jnp.int32)
    target = jnp.any(label_lists[:, :, None] == label_ids[None, None, :], axis=1).astype(
        jnp.float32
    )
    d_logit = (jax.nn.sigmoid(logits) - target).astype(jnp.bfloat16)
    return jnp.dot(d_logit, weight_block, preferred_element_type=jnp.float32)


def shards(tokens, norm_gains, enc_weight, head_weight, head_bias, positives):
    doc_count, seq_len, width = tokens.shape
    embed, saved = encode(tokens, norm_gains, enc_weight)
    embed_bf = embed.astype(jnp.bfloat16)
    col_embed, col_lists = (
        lax.all_gather(embed_bf, "label", axis=0, tiled=True),
        lax.all_gather(positives, "label", axis=0, tiled=True),
    )
    span = head_weight.shape[0] * lax.axis_size("doc")
    label_base = lax.axis_index("label") * span
    partial_grad = head_block(
        col_embed,
        col_lists,
        lax.all_gather(head_weight, "doc", axis=0, tiled=True),
        lax.all_gather(head_bias, "doc", axis=0, tiled=True),
        label_base,
    )
    summed = lax.psum(partial_grad, "label")
    row_grad = lax.dynamic_slice_in_dim(summed, lax.axis_index("label") * doc_count, doc_count, 0)
    weight_part, gain_part = encode_back(row_grad, saved, norm_gains, enc_weight, seq_len)
    weight_grad, gain_grads = lax.psum((weight_part, gain_part), ("label", "doc"))
    return (row_grad, weight_grad, gain_grads)


def solution(mesh):
    placed = (
        P(("label", "doc"), None, None),
        P(),
        P(),
        P(("label", "doc"), None),
        P(("label", "doc")),
        P(("label", "doc"), None),
    )
    return jax.shard_map(
        shards,
        mesh=mesh,
        in_specs=placed,
        out_specs=(P(("label", "doc"), None), P(), P()),
        check_vma=False,
    )
```

profile of v0, /device:TPU:0, one launch (start us, length us, event | category | flops | bytes accessed | tf_op | source)
XLA Modules:
  0.0 270.5 jit_solution(18019750212588372802)
XLA Ops:
  7.2 0.0 copy-start
  7.2 0.0 all-gather.5.cloned.1.call-start
  7.2 0.7 all-gather.5.cloned.1.call-update
  7.9 0.0 copy-start.4
  7.9 0.0 copy-start.2
  7.9 0.0 all-reduce.2.cloned.1.call-start
  8.0 1.0 convert_reduce_fusion
  9.0 0.7 slice_reduce_fusion
  9.8 0.7 reshape.103
  10.4 5.2 %all-gather.1 = bf16[2,1,512]{2,1,0:T(2,128)(2,1)S(1)} all-gather(bf16[1,1,512]{2,1,0:T(2,128)(2,1)S(1)} %reshape.103), channel_id=1, replica_groups=mesh['label'=16,'doc'=2] {'doc'}, dimensions={0}, use_global_device_ids=true | all-gather | bytes 3072 | tf_op jit(solution)/shard_map/all_gather | solution.py:86
  15.7 1.1 fusion.14
  16.8 0.0 copy-done
  16.8 1.5 fusion.15
  18.3 0.6 multiply_reduce_fusion.1
  19.6 0.6 multiply_reduce_fusion
  20.9 0.0 copy-done.4
  20.9 22.1 %all-gather.2 = s32[16,1,8]{2,1,0:T(1,128)S(1)} all-gather(s32[1,1,8]{2,1,0:T(1,128)S(1)} %bitcast.39), channel_id=1, replica_groups=mesh['label'=16,'doc'=2] {'label'}, dimensions={0}, use_global_device_ids=true | all-gather | bytes 544 | tf_op jit(solution)/shard_map/all_gather | solution.py:78
  43.0 0.0 copy-done.2
  43.0 17.5 %all-gather = bf16[16,1,768]{2,1,0:T(2,128)(2,1)S(1)} all-gather(bf16[1,1,768]{2,1,0:T(2,128)(2,1)S(1)} %convert_bitcast_fusion.1), channel_id=1, replica_groups=mesh['label'=16,'doc'=2] {'label'}, dimensions={0}, use_global_device_ids=true | all-gather | bytes 26112 | tf_op jit(solution)/shard_map/all_gather | solution.py:77
  60.5 0.2 compare_reduce_fusion
  60.7 0.0 all-gather.5.cloned.1.call-done
  60.8 0.0 copy-start.1
  60.8 2.8 %fusion.7 = f32[16,768]{1,0:T(8,128)S(1)} fusion(bf16[1024,768]{1,0:T(8,128)(2,1)} %all-gather.5.cloned.1.call-done, pred[16,1024]{1,0:T(8,128)(4,1)S(1)} %compare_reduce_fusion, f32[1024]{0:T(1024)S(1)} %bitcast.38, bf16[16,1,768]{2,1,0:T(2,128)(2,1)S(1)} %all-gather), kind=kOutput, calls=%fused_computation.9 | convolution fusion | flops 50446336 | bytes 1667072 | tf_op jit(solution)/shard_map/dot_general | solution.py:69
  63.5 59.2 %psum.21 = f32[16,768]{1,0:T(8,128)S(1)} all-reduce(f32[16,768]{1,0:T(8,128)S(1)} %fusion.7), channel_id=1, replica_groups=mesh['label'=16,'doc'=2] {'label'}, use_global_device_ids=true, to_apply=%region_6.0 | all-reduce | flops 12288 | bytes 98304 | tf_op jit(solution)/shard_map/psum | solution.py:89
  122.8 0.0 copy-start.3
  122.8 0.6 fusion.37
  124.8 2.8 %fusion.31 = f32[768,768]{1,0:T(8,128)} fusion(bf16[1,128,768]{2,1,0:T(8,128)(2,1)S(1)} %copy-done.1, f32[768]{0:T(1024)S(1)} %slice_reduce_fusion, f32[128]{0:T(128)S(1)} %add_rsqrt_fusion, f32[128]{0:T(128)S(1)} %broadcast_multiply_fusion.1, f32[128,768]{1,0:T(8,128)S(1)} %get-tuple-element.9, f32[768]{0:T(1024)S(1)} %multiply_reduce_fusion.2, ...), kind=kOutput, calls=%fused_computation.52 | convolution fusion | flops 908230656 | bytes 2959360 | tf_op jit(solution)/shard_map/dot_general | solution.py:41
  127.6 0.0 all-reduce.2.cloned.1.call-update
  127.6 1.3 fusion
  129.0 37.3 %psum.23 = f32[2,768]{1,0:T(2,128)} all-reduce(f32[2,768]{1,0:T(2,128)S(1)} %pad_maximum_fusion), channel_id=1, replica_groups=mesh['label'=16,'doc'=2] {'label','doc'}, use_global_device_ids=true, to_apply=%region_11.0 | all-reduce | flops 1536 | bytes 12288 | tf_op jit(solution)/shard_map/psum | solution.py:92
  166.2 94.2 %all-reduce.2.cloned.1.call-done = f32[768,768]{1,0:T(8,128)} async-done(((f32[768,768]{1,0:T(8,128)}), f32[768,768]{1,0:T(8,128)}) %all-reduce.2.cloned.1.call-update) | async-done | bytes 2359312 | tf_op jit(solution)/shard_map/psum | solution.py:92
  260.4 3.2 %copy.25 = f32[768,768]{1,0:T(8,128)} copy(f32[768,768]{1,0:T(8,128)} %all-reduce.2.cloned.1.call-done) | data formatting | bytes 4718592
  (13 shorter events, 0.1 us)
Async XLA Ops:
  7.2 9.7 %copy-start = (bf16[768,768]{1,0:T(8,128)(2,1)S(1)}, bf16[768,768]{1,0:T(8,128)(2,1)}, u32[]{:S(2)}) copy-start(bf16[768,768]{1,0:T(8,128)(2,1)} %param.8) | copy-start | bytes 3538948
  7.2 53.6 %all-gather.5.cloned.1.call-start = ((), (), s32[]{:S(2)}) async-start(), calls=%async_computation | async-start | bytes 2359296 | tf_op jit(solution)/shard_map/all_gather | solution.py:85
  7.9 13.0 %copy-start.4 = (s32[1,8]{1,0:T(1,128)S(1)}, s32[1,8]{1,0:T(1,128)}, u32[]{:S(2)}) copy-start(s32[1,8]{1,0:T(1,128)} %param.11) | copy-start | bytes 100
  7.9 35.0 %copy-start.2 = (f32[2,768]{1,0:T(2,128)S(1)}, f32[2,768]{1,0:T(2,128)}, u32[]{:S(2)}) copy-start(f32[2,768]{1,0:T(2,128)} %param.7) | copy-start | bytes 18436
  7.9 252.5 %all-reduce.2.cloned.1.call-start = ((), (), s32[]{:S(2)}) async-start(), calls=%async_computation.1 | async-start | bytes 4718592 | tf_op jit(solution)/shard_map/psum | solution.py:92
  60.8 64.0 %copy-start.1 = (bf16[1,128,768]{2,1,0:T(8,128)(2,1)S(1)}, bf16[1,128,768]{2,1,0:T(8,128)(2,1)}, u32[]{:S(2)}) copy-start(bf16[1,128,768]{2,1,0:T(8,128)(2,1)} %param.6) | copy-start | bytes 589828
  122.8 4.8 %copy-start.3 = (f32[1,768]{1,0:T(1,128)}, f32[1,768]{1,0:T(1,128)S(1)}, u32[]{:S(2)}) copy-start(f32[1,768]{1,0:T(1,128)S(1)} %get-tuple-element.10) | copy-start | bytes 9220
Sparse Core Ops, SparseCore 0:
  9.6 29.8 all-gather.4
  127.8 132.6 all-reduce.1
where the time goes:
time: 271 us
  blocking collectives  141 us (52%)
  waiting for transfers between devices  95 us (35%)
  between operations  16.8 us (6%)
  matrix products  8.34 us (3%)
  local copies, waits for them, and re-layouts  4.65 us (2%)
  other arithmetic  4.28 us (2%)
    psum x1, waiting for transfers between devices, shards(): lax.psum((weight_part, gain_part), ('label', 'doc'))  94.2 us
    psum x1, blocking collectives, shards(): summed = lax.psum(partial_grad, 'label')  59.2 us
    psum x1, blocking collectives, shards(): lax.psum((weight_part, gain_part), ('label', 'doc'))  37.3 us
    all_gather x1, blocking collectives, shards(): lax.all_gather(positives, 'label', axis=0, tiled=True)  22.1 us
    all_gather x1, blocking collectives, shards(): lax.all_gather(embed_bf, 'label', axis=0, tiled=True)  17.5 us
  transfers between devices with their start and end apart: 2, of which 1 were waited for; matrix products, arithmetic and copies ran while one was open for 3% of the time, Pallas kernels for 0%

commit v1 on v0

v1 whole, which is shorter than its diff:
```python
import functools
import math

import jax
import jax.numpy as jnp
from jax import lax
from jax.experimental import pallas as pl
from jax.experimental.pallas import tpu as pltpu
from jax.sharding import PartitionSpec as P

epsilon = 1e-05
AXES = ("label", "doc")
PIECE_BITS = 8
PIECE = 1 << PIECE_BITS
DIGITS = 3
GATHER_LIMIT = 8 << 20
f32, bf16 = jnp.float32, jnp.bfloat16


def encode_rows(tok, gains, weight):
    mean = jnp.mean(tok, axis=-1, keepdims=True)
    center = tok - mean
    inverse = lax.rsqrt(jnp.mean(center * center, axis=-1, keepdims=True) + epsilon)
    act = (center * inverse * gains[0:1]).astype(bf16)
    pre = jnp.dot(act, weight, preferred_element_type=f32)
    scale = math.sqrt(2.0 / math.pi)
    square = pre * pre
    bend = jnp.tanh(pre * (scale + (scale * 0.044715) * square))
    half = 0.5 * pre
    gelu = half + half * bend
    tilt = 0.5 * bend + half * (1.0 - bend * bend) * (scale + (3.0 * scale * 0.044715) * square)
    return act, tilt, jnp.sum(tok + gelu, axis=0, keepdims=True), jnp.sum(act.astype(f32), axis=0, keepdims=True)


def norm_row(pooled):
    center = pooled - jnp.mean(pooled, axis=-1, keepdims=True)
    inverse = lax.rsqrt(jnp.mean(center * center, axis=-1, keepdims=True) + epsilon)
    return center * inverse, inverse


def place(device, core):
    return (device // (2 * core)) * core + device % core


def number():
    return lax.axis_index("label") * lax.axis_size("doc") + lax.axis_index("doc")


def encode_into(layout, toks, gains, weight, act_ref, tilt_ref, row_ref):
    at = 0
    for d, doc in enumerate(layout):
        seq = sum(rows for _, _, rows in doc)
        total, acts = 0.0, 0.0
        for operand, first, rows in doc:
            for start in range(0, rows, seq // 2):
                span = min(seq // 2, rows)
                tok = toks[operand][first + start : first + start + span, :].astype(f32)
                act, tilt, part, sums = encode_rows(tok, gains, weight)
                act_ref[at : at + span, :] = act
                tilt_ref[at : at + span, :] = tilt
                total, acts, at = total + part, acts + sums, at + span
        normed, inverse = norm_row(total * (1.0 / seq))
        row_ref[d, 0:1, :] = normed
        row_ref[d, 1:2, :] = jnp.broadcast_to(inverse, normed.shape)
        row_ref[d, 2:3, :] = acts
    return normed


def first_kernel(*refs):
    sources, (act_ref, tilt_ref, row_ref, embed_ref), held, (digits, sems) = refs[:4], refs[4:8], refs[8:12], refs[12:]
    copies = [pltpu.make_async_copy(a, b, sems.at[k]) for k, (a, b) in enumerate(zip(sources, held, strict=True))]
    for copy in copies:
        copy.start()
    for copy in copies:
        copy.wait()
    tok, gains_ref, weight_ref, listed_ref = held
    gains = gains_ref[...]
    seq, width = tok.shape
    slots = listed_ref.shape[1]
    normed = encode_into([[(0, 0, seq)]], [tok], gains, weight_ref[...], act_ref, tilt_ref, row_ref)
    embed = normed * gains[1:2]
    digits[...] = jnp.zeros_like(digits)
    shifted = listed_ref[...] + 1
    for k in range(DIGITS):
        digit = jnp.bitwise_and(jnp.right_shift(shifted, PIECE_BITS * (DIGITS - 1 - k)), PIECE - 1)
        digits[:, k * slots : (k + 1) * slots] = digit.astype(f32)
    lanes = [embed[:, k * 128 : (k + 1) * 128] for k in range(width // 128)] + [digits[...]]
    lanes += [jnp.zeros((1, 128), f32)] * (embed_ref.shape[1] - len(lanes))
    block = jnp.concatenate(lanes, axis=0).astype(bf16)
    embed_ref[...] = jnp.broadcast_to(block[None], embed_ref.shape)


def encode_kernel(layout, *refs):
    toks, (gains_ref, weight_ref, act_ref, tilt_ref, row_ref) = refs[:-5], refs[-5:]
    encode_into(layout, toks, gains_ref[...], weight_ref[...], act_ref, tilt_ref, row_ref)


def encode_shapes(rows, docs, width):
    return [
        jax.ShapeDtypeStruct((rows, width), bf16),
        jax.ShapeDtypeStruct((rows, width), f32),
        jax.ShapeDtypeStruct((docs, 8, width), f32),
    ]


def first_call(own, gains, weight, listed, copies):
    seq, width = own.shape
    sources = [own, gains, weight, listed]
    deep = -(-(width // 128 + 1) // 8) * 8
    return pl.pallas_call(
        first_kernel,
        out_shape=encode_shapes(seq, 1, width) + [jax.ShapeDtypeStruct((copies, deep, 128), bf16)],
        in_specs=[pl.BlockSpec(memory_space=pl.ANY)] * 4,
        scratch_shapes=[pltpu.VMEM(a.shape, a.dtype) for a in sources]
        + [pltpu.VMEM((1, 128), f32), pltpu.SemaphoreType.DMA((4,))],
        compiler_params=pltpu.CompilerParams(vmem_limit_bytes=10 << 20),
        name="first",
    )(*sources)


def encode_call(arrays, layout, gains, weight):
    rows = sum(piece[2] for doc in layout for piece in doc)
    return pl.pallas_call(
        functools.partial(encode_kernel, layout),
        out_shape=encode_shapes(rows, len(layout), gains.shape[1]),
        compiler_params=pltpu.CompilerParams(vmem_limit_bytes=14 << 20),
        name="encode",
    )(*arrays, gains, weight)


def join_kernel(pieces, *refs):
    out_ref = refs[-1]
    at = 0
    for operand, first, rows in pieces:
        out_ref[at : at + rows, :] = refs[operand][first : first + rows, :]
        at += rows


def join(parts, tied=()):
    arrays, pieces = [], []
    for array, first, rows in parts:
        known = [k for k, a in enumerate(arrays) if a is array]
        if not known:
            known = [len(arrays)]
            arrays.append(array)
        pieces.append((known[0], first, rows))
    vmem, anywhere = pl.BlockSpec(memory_space=pltpu.VMEM), pl.BlockSpec(memory_space=pl.ANY)
    return pl.pallas_call(
        functools.partial(join_kernel, pieces),
        out_shape=jax.ShapeDtypeStruct((sum(p[2] for p in pieces), arrays[0].shape[1]), arrays[0].dtype),
        in_specs=[vmem] * len(arrays) + [anywhere] * len(tied),
        compiler_params=pltpu.CompilerParams(vmem_limit_bytes=4 << 20),
        name="join",
    )(*arrays, *tied)


def add_kernel(count, *refs):
    parts = [ref[...] for ref in refs[:count]]
    while len(parts) > 1:
        parts = [parts[i] + parts[i + 1] for i in range(0, len(parts), 2)]
    refs[-1][...] = parts[0]


def add(parts, tied=()):
    vmem, anywhere = pl.BlockSpec(memory_space=pltpu.VMEM), pl.BlockSpec(memory_space=pl.ANY)
    return pl.pallas_call(
        functools.partial(add_kernel, len(parts)),
        out_shape=jax.ShapeDtypeStruct(parts[0].shape, parts[0].dtype),
        in_specs=[vmem] * len(parts) + [anywhere] * len(tied),
        compiler_params=pltpu.CompilerParams(vmem_limit_bytes=4 << 20),
        name="add",
    )(*parts, *tied)


def head_kernel(slots, rows_ref, weight_ref, bias_ref, mine_ref, other_ref, rows, part):
    labels, width = weight_ref.shape
    lanes = width // 128 + 1
    me, core = number(), lax.axis_size("doc")
    rows[...] = rows_ref[...].astype(f32)
    weight = weight_ref[...]
    embed = jnp.concatenate([rows[:, k, :] for k in range(lanes - 1)], axis=1)
    logits = lax.dot_general(
        embed.astype(bf16), weight, (((1,), (1,)), ((), ())), preferred_element_type=f32
    ) + bias_ref[...].astype(f32).reshape(1, labels)
    digits = rows[:, lanes - 1, :]
    ids = digits[:, :slots] * (PIECE * PIECE) + digits[:, slots : 2 * slots] * PIECE + digits[:, 2 * slots : 3 * slots]
    own = lax.broadcasted_iota(jnp.int32, logits.shape, 1) + (me * labels + 1)
    listed = ids.astype(jnp.int32)
    hit = own == listed[:, 0:1]
    for k in range(1, slots):
        hit = jnp.logical_or(hit, own == listed[:, k : k + 1])
    d_logit = (jax.nn.sigmoid(logits) - jnp.where(hit, 1.0, 0.0)).astype(bf16)
    part[...] = jnp.dot(d_logit, weight, preferred_element_type=f32)
    half = part.shape[0] // 2
    kind = lax.rem(me // core, 2)
    mine_ref[...] = part[pl.ds(pl.multiple_of(kind * half, half), half), :]
    other_ref[...] = part[pl.ds(pl.multiple_of((1 - kind) * half, half), half), :]


def back_kernel(seq, masks, *refs):
    grad_ref, gains_ref, weight_ref = refs[:3]
    groups = [refs[3 + 3 * g : 6 + 3 * g] for g in range(len(masks))]
    out_ref, sums_ref, own_ref, act, d_pre, saved, spreads = refs[3 + 3 * len(masks) :]
    me, core = number(), lax.axis_size("doc")
    places = [[place(me ^ m, core) for m in group] for group in masks]
    own_ref[...] = grad_ref[pl.ds(place(me, core), 1), :]
    width = gains_ref.shape[1]
    for (_, _, row_ref), group in zip(groups, places, strict=True):
        for d, at in enumerate(group):
            saved[at] = row_ref[d]
    row, normed, inverse, sums = grad_ref[...], saved[:, 0, :], saved[:, 1, :], saved[:, 2, :]
    d_normed = row * gains_ref[1:2, :]
    spread = (
        inverse
        * (
            d_normed
            - jnp.mean(d_normed, axis=-1, keepdims=True)
            - normed * jnp.mean(d_normed * normed, axis=-1, keepdims=True)
        )
        * (1.0 / seq)
    )
    spreads[...] = spread
    for (act_ref, tilt_ref, _), group in zip(groups, places, strict=True):
        for d, at in enumerate(group):
            to = pl.ds(pl.multiple_of(at * seq, seq), seq)
            act[to, :] = act_ref[d * seq : (d + 1) * seq, :]
            d_pre[to, :] = (tilt_ref[d * seq : (d + 1) * seq, :] * spreads[pl.ds(at, 1), :]).astype(bf16)
    half = 0.5 * spread
    sums_top, half_top = sums.astype(bf16), half.astype(bf16)
    sums_low = (sums - sums_top.astype(f32)).astype(bf16)
    half_low = (half - half_top.astype(f32)).astype(bf16)
    even = lax.dot_general(
        jnp.concatenate([sums_top, sums_top, sums_low], axis=0),
        jnp.concatenate([half_top, half_low, half_top], axis=0),
        (((0,), (0,)), ((), ())),
        preferred_element_type=f32,
    )
    total = even + lax.dot_general(act[...], d_pre[...], (((0,), (0,)), ((), ())), preferred_element_type=f32)
    out_ref[...] = total.astype(bf16)
    weighed = total * weight_ref[...].astype(f32)
    lanes = weighed[:, :128]
    for k in range(1, width // 128):
        lanes = lanes + weighed[:, k * 128 : (k + 1) * 128]
    sums_ref[0:1, :] = jnp.sum(lanes.T, axis=0, keepdims=True) / gains_ref[0:1, :]
    sums_ref[1:2, :] = jnp.sum(row * normed, axis=0, keepdims=True)


def final_kernel(mine_ref, other_ref, sums_ref, more_ref, weight_ref, gains_ref):
    weight_ref[...] = mine_ref[...].astype(f32) + other_ref[...].astype(f32)
    gains_ref[...] = sums_ref[...] + more_ref[...]


def final_call(mine, other, sums, more):
    rows, width = mine.shape
    steps = 4 if rows % 64 == 0 else 1
    part = pl.BlockSpec((rows // steps, width), lambda i: (i, 0))
    whole = pl.BlockSpec(sums.shape, lambda i: (0, 0))
    return pl.pallas_call(
        final_kernel,
        grid=(steps,),
        out_shape=[jax.ShapeDtypeStruct(mine.shape, f32), jax.ShapeDtypeStruct(sums.shape, f32)],
        in_specs=[part, part, whole, whole],
        out_specs=[part, whole],
        compiler_params=pltpu.CompilerParams(vmem_limit_bytes=12 << 20),
        name="final",
    )(mine, other, sums, more)


def swap(value, mask, count):
    return lax.ppermute(value, AXES, [(i, i ^ mask) for i in range(count)])


def combos(bits):
    masks = [0]
    for bit in bits:
        masks += [m | bit for m in masks]
    return masks


def gathered(tokens, norm_gains, enc_weight, head_weight, head_bias, positives):
    n_doc, count = lax.axis_size("doc"), lax.axis_size(AXES)
    seq, width = tokens.shape[1:]
    slots = positives.shape[1]
    core = n_doc
    bits = [1 << b for b in range(count.bit_length() - 1) if 1 << b != core]
    x, y, z, far = bits
    hop = functools.partial(swap, count=count)
    half, h = count // 2, seq // 2
    by_core = [i for i in range(count) if not i & core] + [i for i in range(count) if i & core]

    own = tokens.reshape(seq, width)
    held = {0: [(own, 0, seq)]}

    def exchange(plan, tied=()):
        come = {}
        for to, wanted in plan.items():
            parts = []
            for doc, low, high in wanted:
                at = 0
                for array, first, rows in held[doc]:
                    start, stop = max(low, at), min(high, at + rows)
                    if start < stop:
                        parts.append((array, first + start - at, stop - start))
                    at += rows
            come[to] = hop(parts[0][0] if not tied else join(parts, tied), to)
        new = {}
        for to, wanted in plan.items():
            at = 0
            for doc, low, high in wanted:
                new.setdefault(doc ^ to, []).append((low, come[to], at, high - low))
                at += high - low
        fresh = {}
        for doc, pieces in new.items():
            fresh[doc] = [piece[1:] for piece in sorted(pieces, key=lambda piece: piece[0])]
        held.update(fresh)
        return list(fresh), list(come.values())

    groups, masks = [], []

    def encode_held(docs):
        arrays, layout = [], []
        for doc in docs:
            pieces = []
            for array, first, rows in held[doc]:
                known = [k for k, a in enumerate(arrays) if a is array]
                if not known:
                    known = [len(arrays)]
                    arrays.append(array)
                pieces.append((known[0], first, rows))
            layout.append(pieces)
        groups.append(encode_call(arrays, layout, norm_gains, enc_weight))
        masks.append(docs)
        return groups[-1][2]

    docs_0, come_0 = exchange({x: [(0, 0, seq)], y: [(0, 0, seq)], z: [(0, 0, seq)], far: [(0, 0, seq)]})

    *group, copies = first_call(own, norm_gains, enc_weight, positives, count)
    groups.append(group)
    masks.append([0])
    rows = lax.all_to_all(copies, AXES, split_axis=0, concat_axis=0, tiled=True, axis_index_groups=[by_core])

    def cube(base):
        return {
            x: [(base | y, 0, h), (base | z, 0, h)],
            y: [(base | x, h, seq), (base | z, 0, h)],
            z: [(base | x, h, seq), (base | y, h, seq)],
        }

    def corner(base):
        return {x: [(base | y | z, 0, h)], y: [(base | x | z, h, seq)]}

    mine, other = pl.pallas_call(
        functools.partial(head_kernel, slots),
        out_shape=[jax.ShapeDtypeStruct((half, width), f32)] * 2,
        scratch_shapes=[pltpu.VMEM(rows.shape, f32), pltpu.VMEM((count, width), f32)],
        compiler_params=pltpu.CompilerParams(vmem_limit_bytes=10 << 20),
        name="head",
    )(rows, head_weight, head_bias)

    plan = cube(0)
    docs_1, _ = exchange({to: [(far, 0, seq)] + plan[to] for to in plan}, [rows])
    tied = encode_held(docs_0)
    total = add([mine, hop(other, core)])
    total = add([total] + [hop(total, m) for m in (x, y, x | y)], [tied])
    plan, last = cube(far), corner(0)
    docs_2, _ = exchange({to: plan[to] + last.get(to, []) for to in plan}, [total])
    tied = encode_held(docs_1)
    total = add([total] + [hop(total, m) for m in (z, far, z | far)], [tied])
    docs_3, _ = exchange(corner(far), [tied])
    encode_held(docs_2)
    encode_held(docs_3)

    operands = [array for group in groups for array in group]
    part, sums, row_grad = pl.pallas_call(
        functools.partial(back_kernel, seq, masks),
        out_shape=[
            jax.ShapeDtypeStruct((width, width), bf16),
            jax.ShapeDtypeStruct((2, width), f32),
            jax.ShapeDtypeStruct((1, width), f32),
        ],
        scratch_shapes=[
            pltpu.VMEM((half * seq, width), bf16),
            pltpu.VMEM((half * seq, width), bf16),
            pltpu.VMEM((half, 8, width), f32),
            pltpu.VMEM((half, width), f32),
        ],
        compiler_params=pltpu.CompilerParams(vmem_limit_bytes=32 << 20),
        name="back",
    )(total, norm_gains, enc_weight, *operands)
    weight_grad, gain_grads = final_call(part, hop(part, core), sums, hop(sums, core))
    return row_grad, weight_grad, gain_grads


def normalize(values):
    center = values - jnp.mean(values, axis=-1, keepdims=True)
    inverse = lax.rsqrt(jnp.mean(center * center, axis=-1, keepdims=True) + epsilon)
    return (center * inverse, inverse)


def encode(tok_block, gains, enc_weight):
    width = tok_block.shape[-1]
    tok_flat = tok_block.reshape(-1, width).astype(f32)
    normed_in, _ = normalize(tok_flat)
    act_in = (normed_in * gains[0]).astype(bf16)
    pre_act = jnp.dot(act_in, enc_weight, preferred_element_type=f32)
    hidden = tok_flat + jax.nn.gelu(pre_act)
    pooled = jnp.mean(hidden.reshape(tok_block.shape[0], tok_block.shape[1], width), axis=1)
    normed_out, inv_out = normalize(pooled)
    return (normed_out * gains[1], (normed_in, act_in, pre_act, normed_out, inv_out))


def encode_back(cotangent, saved, gains, enc_weight, seq_len):
    normed_in, act_in, pre_act, normed_out, inv_out = saved
    gain_out_grad = jnp.sum(cotangent * normed_out, axis=0)
    d_normed = cotangent * gains[1]
    d_pooled = inv_out * (
        d_normed
        - jnp.mean(d_normed, axis=-1, keepdims=True)
        - normed_out * jnp.mean(d_normed * normed_out, axis=-1, keepdims=True)
    )
    spread_grad = jnp.broadcast_to(
        (d_pooled / seq_len)[:, None, :], (d_pooled.shape[0], seq_len, d_pooled.shape[1])
    ).reshape(pre_act.shape)
    _, gelu_back = jax.vjp(jax.nn.gelu, pre_act)
    d_pre = gelu_back(spread_grad)[0]
    weight_grad = lax.dot_general(
        act_in.astype(f32), d_pre, (((0,), (0,)), ((), ())), precision=lax.Precision.HIGHEST, preferred_element_type=f32
    )
    d_act = lax.dot_general(
        d_pre, enc_weight.astype(f32), (((1,), (1,)), ((), ())), precision=lax.Precision.HIGHEST, preferred_element_type=f32
    )
    gain_in_grad = jnp.sum(d_act * normed_in, axis=0)
    return (weight_grad, jnp.stack([gain_in_grad, gain_out_grad]))


def head_block(embed_bf, label_lists, weight_block, bias_block, first_label):
    logits = lax.dot_general(embed_bf, weight_block, (((1,), (1,)), ((), ())), preferred_element_type=f32)
    logits = logits + bias_block.astype(f32)[None, :]
    label_ids = first_label + jnp.arange(weight_block.shape[0], dtype=jnp.int32)
    target = jnp.any(label_lists[:, :, None] == label_ids[None, None, :], axis=1).astype(f32)
    d_logit = (jax.nn.sigmoid(logits) - target).astype(bf16)
    return jnp.dot(d_logit, weight_block, preferred_element_type=f32)


def spread_out(tokens, norm_gains, enc_weight, head_weight, head_bias, positives):
    doc_count, seq_len, width = tokens.shape
    embed, saved = encode(tokens, norm_gains, enc_weight)
    col_embed, col_lists = (
        lax.all_gather(embed.astype(bf16), "label", axis=0, tiled=True),
        lax.all_gather(positives, "label", axis=0, tiled=True),
    )
    span = head_weight.shape[0] * lax.axis_size("doc")
    partial_grad = head_block(
        col_embed,
        col_lists,
        lax.all_gather(head_weight, "doc", axis=0, tiled=True),
        lax.all_gather(head_bias, "doc", axis=0, tiled=True),
        lax.axis_index("label") * span,
    )
    summed = lax.psum(partial_grad, "label")
    row_grad = lax.dynamic_slice_in_dim(summed, lax.axis_index("label") * doc_count, doc_count, 0)
    weight_part, gain_part = encode_back(row_grad, saved, norm_gains, enc_weight, seq_len)
    weight_grad, gain_grads = lax.psum((weight_part, gain_part), AXES)
    return (row_grad, weight_grad, gain_grads)


def shards(tokens, *rest):
    count = lax.axis_size(AXES)
    powers = all(size & (size - 1) == 0 for size in (count, lax.axis_size("doc")))
    fits = tokens.size * tokens.dtype.itemsize * (count // 2) <= GATHER_LIMIT
    plan = gathered if fits and powers and count == 32 and tokens.shape[0] == 1 else spread_out
    return plan(tokens, *rest)


def solution(mesh):
    placed = (
        P(AXES, None, None),
        P(),
        P(),
        P(AXES, None),
        P(AXES),
        P(AXES, None),
    )
    return jax.shard_map(
        shards,
        mesh=mesh,
        in_specs=placed,
        out_specs=(P(AXES, None), P(), P()),
        check_vma=False,
    )
```

time: 271 us -> 68.9 us (0.25)
  blocking collectives: 141 us -> 9.02 us
  waiting for transfers between devices: 95 us -> 11.9 us
  starting transfers between devices: 0.08 us -> 25.2 us
  Pallas kernels: 0 us -> 18.3 us
  between operations: 16.8 us -> 0.81 us
  matrix products: 8.34 us -> 0 us
  other arithmetic: 4.28 us -> 0 us
    psum x2 -> x0, blocking collectives: 96.5 us -> none  [the longest x1 59.2 us: shards(): summed = lax.psum(partial_grad, 'label')]
    psum x1 -> x0, waiting for transfers between devices: 94.2 us -> none  [shards(): lax.psum((weight_part, gain_part), ('label', 'doc'))]
    all_gather x3 -> x0, blocking collectives: 44.8 us -> none  [the longest x1 22.1 us: shards(): lax.all_gather(positives, 'label', axis=0, tiled=True)]
    ppermute x0 -> x21, starting transfers between devices: none -> 25.2 us  [swap(): return lax.ppermute(value, AXES, [(i, i ^ mask) for i in range(count)])]
    pallas_call x0 -> x19, Pallas kernels: none -> 18.3 us  [the longest x4 9.21 us: encode_call(): pl.pallas_call(functools.partial(encode_kernel, layout), out_shape=encode...]
    ppermute x0 -> x21, waiting for transfers between devices: none -> 11.9 us  [swap(): return lax.ppermute(value, AXES, [(i, i ^ mask) for i in range(count)])]
    all_to_all x0 -> x1, blocking collectives: none -> 9.02 us  [gathered(): lax.all_to_all(copies, AXES, split_axis=0, concat_axis=0, tiled=True, axi...]
    dot_general x4 -> x0, matrix products: 8.34 us -> none  [the longest x1 2.83 us: encode_back(): lax.dot_general(act_in.astype(jnp.float32), d_pre, (((0,), (0,)), ((), ()...]
  transfers between devices with their start and end apart: 2 -> 21, of which waited for: 1 -> 6; matrix products, arithmetic and copies ran while one was open for 3% -> 0% of each run, Pallas kernels for 0% -> 15%
where the time goes in v1:
time: 68.9 us; the launch traced here: 68.7 us
  starting transfers between devices  25.2 us (37%)
  Pallas kernels  18.3 us (27%)
  waiting for transfers between devices  11.9 us (17%)
  blocking collectives  9.02 us (13%)
  local copies, waits for them, and re-layouts  3.56 us (5%)
  between operations  0.81 us (1%)
    ppermute x21, starting transfers between devices, swap(): return lax.ppermute(value, AXES, [(i, i ^ mask) for i in range(count)])  25.2 us
    ppermute x21, waiting for transfers between devices, swap(): return lax.ppermute(value, AXES, [(i, i ^ mask) for i in range(count)])  11.9 us
    pallas_call x4, Pallas kernels, encode_call(): pl.pallas_call(functools.partial(encode_kernel, layout), out_shape=encode...  9.21 us
    all_to_all x1, blocking collectives, gathered(): lax.all_to_all(copies, AXES, split_axis=0, concat_axis=0, tiled=True, axi...  9.02 us
    pallas_call x1, Pallas kernels, gathered(): pl.pallas_call(functools.partial(back_kernel, seq, masks), out_shape=[jax...  4.76 us
    unnamed x16, local copies, waits for them, and re-layouts  3.56 us
    pallas_call x1, Pallas kernels, final_call(): pl.pallas_call(final_kernel, grid=(steps,), out_shape=[jax.ShapeDtypeStru...  1.95 us
    pallas_call x1, Pallas kernels, first_call(): pl.pallas_call(first_kernel, out_shape=encode_shapes(seq, 1, width) + [ja...  1.46 us
  transfers between devices with their start and end apart: 21, of which 6 were waited for; matrix products, arithmetic and copies ran while one was open for 0% of the time, Pallas kernels for 15%

profile of v1, /device:TPU:0, one launch (start us, length us, event | category | flops | bytes accessed | tf_op | source)
XLA Modules:
  0.0 68.7 jit_solution(12088181180655386273)
XLA Ops:
  0.6 4.1 %collective-permute-start.7 = (bf16[128,768]{1,0:T(8,128)(2,1)}, bf16[128,768]{1,0:T(8,128)(2,1)S(1)}, u32[]{:S(2)}, u32[]{:S(2)}) collective-permute-start(bf16[128,768]{1,0:T(8,128)(2,1)} %bitcast.1), channel_id=1, source_target_pairs={{0,16},{1,17},{2,18},{3,19},{4,20},{5,21},{6,22},{7,23},{8,24},{9,... | collective-permute-start | bytes 589832 | tf_op jit(solution)/shard_map/ppermute | solution.py:270
  4.7 1.5 %collective-permute-start.5 = (bf16[128,768]{1,0:T(8,128)(2,1)}, bf16[128,768]{1,0:T(8,128)(2,1)S(1)}, u32[]{:S(2)}, u32[]{:S(2)}) collective-permute-start(bf16[128,768]{1,0:T(8,128)(2,1)} %bitcast.2), channel_id=1, source_target_pairs={{0,4},{1,5},{2,6},{3,7},{4,0},{5,1},{6,2},{7,3},{8,12},{9,13},{10,... | collective-permute-start | bytes 589832 | tf_op jit(solution)/shard_map/ppermute | solution.py:270
  6.2 1.6 %collective-permute-start.6 = (bf16[128,768]{1,0:T(8,128)(2,1)}, bf16[128,768]{1,0:T(8,128)(2,1)S(1)}, u32[]{:S(2)}, u32[]{:S(2)}) collective-permute-start(bf16[128,768]{1,0:T(8,128)(2,1)} %bitcast.3), channel_id=1, source_target_pairs={{0,8},{1,9},{2,10},{3,11},{4,12},{5,13},{6,14},{7,15},{8,0},{9,1},... | collective-permute-start | bytes 589832 | tf_op jit(solution)/shard_map/ppermute | solution.py:270
  7.8 1.5 %collective-permute-start.4 = (bf16[128,768]{1,0:T(8,128)(2,1)}, bf16[128,768]{1,0:T(8,128)(2,1)S(1)}, u32[]{:S(2)}, u32[]{:S(2)}) collective-permute-start(bf16[128,768]{1,0:T(8,128)(2,1)} %bitcast.4), channel_id=1, source_target_pairs={{0,1},{1,0},{2,3},{3,2},{4,5},{5,4},{6,7},{7,6},{8,9},{9,8},{10,11... | collective-permute-start | bytes 589832 | tf_op jit(solution)/shard_map/ppermute | solution.py:270
  9.3 1.3 %copy-done = bf16[768,768]{1,0:T(8,128)(2,1)S(1)} copy-done((bf16[768,768]{1,0:T(8,128)(2,1)S(1)}, bf16[768,768]{1,0:T(8,128)(2,1)}, u32[]{:S(2)}) %copy-start) | copy-done | bytes 1179672
  11.3 0.9 %copy-done.5 = bf16[1,128,768]{2,1,0:T(8,128)(2,1)S(1)} copy-done((bf16[1,128,768]{2,1,0:T(8,128)(2,1)S(1)}, bf16[1,128,768]{2,1,0:T(8,128)(2,1)}, u32[]{:S(2)}) %copy-start.5) | copy-done | bytes 196632
  12.9 1.5 %first.1 = (bf16[128,768]{1,0:T(8,128)(2,1)S(1)}, f32[128,768]{1,0:T(8,128)S(1)}, f32[1,8,768]{2,1,0:T(8,128)S(1)}, bf16[32,8,128]{2,1,0:T(8,128)(2,1)S(1)}) custom-call(bf16[128,768]{1,0:T(8,128)(2,1)S(1)} %bitcast.5, f32[2,768]{1,0:T(2,128)S(1)} %copy-done.3, bf16[768,768]{1,0:T(8,128)(2,1)S(1)} %copy-done, s32[1,8]{1,0:T(1,128)S(1)} %copy-done.7), custom_call_target="tpu_custom_call" | custom-call | tf_op jit(solution)/shard_map/first/pallas_call | solution.py:110
  14.3 9.0 %all_to_all.5.rows_ref.refs_3_ = bf16[32,8,128]{2,1,0:T(8,128)(2,1)S(1)} all-to-all(bf16[32,8,128]{2,1,0:T(8,128)(2,1)S(1)} %get-tuple-element.26), channel_id=1, replica_groups={{0,1,4,5,8,9,12,13,16,17,20,21,24,25,28,29,2,3,6,7,10,11,14,15,18,19,22..., dimensions={0} | all-to-all | bytes 131072 | tf_op jit(solution)/shard_map/all_to_all | solution.py:340
  23.4 0.8 %collective-permute-start.11 = (bf16[256,768]{1,0:T(8,128)(2,1)S(1)}, bf16[256,768]{1,0:T(8,128)(2,1)S(1)}, u32[]{:S(2)}, u32[]{:S(2)}) collective-permute-start(bf16[256,768]{1,0:T(8,128)(2,1)S(1)} %join.8), channel_id=1, source_target_pairs={{0,1},{1,0},{2,3},{3,2},{4,5},{5,4},{6,7},{7,6},{8,9},{9,8},{10,11... | collective-permute-start | bytes 1179656 | tf_op jit(solution)/shard_map/ppermute | solution.py:270
  24.9 0.7 %collective-permute-start.12 = (bf16[256,768]{1,0:T(8,128)(2,1)S(1)}, bf16[256,768]{1,0:T(8,128)(2,1)S(1)}, u32[]{:S(2)}, u32[]{:S(2)}) collective-permute-start(bf16[256,768]{1,0:T(8,128)(2,1)S(1)} %join.9), channel_id=1, source_target_pairs={{0,4},{1,5},{2,6},{3,7},{4,0},{5,1},{6,2},{7,3},{8,12},{9,13},{10,... | collective-permute-start | bytes 1179656 | tf_op jit(solution)/shard_map/ppermute | solution.py:270
  25.6 0.7 %head.1 = (f32[16,768]{1,0:T(8,128)S(1)}, f32[16,768]{1,0:T(8,128)S(1)}) custom-call(bf16[32,8,128]{2,1,0:T(8,128)(2,1)S(1)} %all_to_all.5.rows_ref.refs_3_, bf16[512,768]{1,0:T(8,128)(2,1)S(1)} %copy-done.2, bf16[512]{0:T(512)(128)(2,1)S(1)} %copy-done.6), custom_call_target="tpu_custom_call" | custom-call | tf_op jit(solution)/shard_map/head/pallas_call | solution.py:352
  26.4 1.2 %collective-permute-done.refs_1_ = f32[16,768]{1,0:T(8,128)S(1)} collective-permute-done((f32[16,768]{1,0:T(8,128)S(1)}, f32[16,768]{1,0:T(8,128)S(1)}, u32[]{:S(2)}, u32[]{:S(2)}) %collective-permute-start) | collective-permute-done | bytes 49184 | tf_op jit(solution)/shard_map/ppermute | solution.py:270
  27.6 1.5 %collective-permute-start.1 = (f32[16,768]{1,0:T(8,128)S(1)}, f32[16,768]{1,0:T(8,128)S(1)}, u32[]{:S(2)}, u32[]{:S(2)}) collective-permute-start(f32[16,768]{1,0:T(8,128)S(1)} %add.3.refs_0_), channel_id=1, source_target_pairs={{0,1},{1,0},{2,3},{3,2},{4,5},{5,4},{6,7},{7,6},{8,9},{9,8},{10,11... | collective-permute-start | bytes 147464 | tf_op jit(solution)/shard_map/ppermute | solution.py:270
  29.1 1.6 %collective-permute-start.2 = (f32[16,768]{1,0:T(8,128)S(1)}, f32[16,768]{1,0:T(8,128)S(1)}, u32[]{:S(2)}, u32[]{:S(2)}) collective-permute-start(f32[16,768]{1,0:T(8,128)S(1)} %add.3.refs_0_), channel_id=1, source_target_pairs={{0,4},{1,5},{2,6},{3,7},{4,0},{5,1},{6,2},{7,3},{8,12},{9,13},{10,... | collective-permute-start | bytes 147464 | tf_op jit(solution)/shard_map/ppermute | solution.py:270
  30.7 4.6 %collective-permute-done.1.refs_1_ = f32[16,768]{1,0:T(8,128)S(1)} collective-permute-done((f32[16,768]{1,0:T(8,128)S(1)}, f32[16,768]{1,0:T(8,128)S(1)}, u32[]{:S(2)}, u32[]{:S(2)}) %collective-permute-start.1) | collective-permute-done | bytes 49184 | tf_op jit(solution)/shard_map/ppermute | solution.py:270
  35.3 1.1 %collective-permute-start.3 = (f32[16,768]{1,0:T(8,128)S(1)}, f32[16,768]{1,0:T(8,128)S(1)}, u32[]{:S(2)}, u32[]{:S(2)}) collective-permute-start(f32[16,768]{1,0:T(8,128)S(1)} %add.3.refs_0_), channel_id=1, source_target_pairs={{0,5},{1,4},{2,7},{3,6},{4,1},{5,0},{6,3},{7,2},{8,13},{9,12},{10,... | collective-permute-start | bytes 147464 | tf_op jit(solution)/shard_map/ppermute | solution.py:270
  36.4 2.4 %encode.4 = (bf16[512,768]{1,0:T(8,128)(2,1)S(1)}, f32[512,768]{1,0:T(8,128)S(1)}, f32[4,8,768]{2,1,0:T(8,128)S(1)}) custom-call(bf16[128,768]{1,0:T(8,128)(2,1)S(1)} %collective-permute-done.4.refs_0_.refs_1_, bf16[128,768]{1,0:T(8,128)(2,1)S(1)} %collective-permute-done.5.refs_1_.refs_2_, bf16[128,768]{1,0:T(8,128)(2,1)S(1)} %collective-permute-done.6.refs_2_, ...), custom_call_target="tpu_custom_call" | custom-call | tf_op jit(solution)/shard_map/encode/pallas_call | solution.py:123
  38.8 1.5 %collective-permute-done.3.refs_3_ = f32[16,768]{1,0:T(8,128)S(1)} collective-permute-done((f32[16,768]{1,0:T(8,128)S(1)}, f32[16,768]{1,0:T(8,128)S(1)}, u32[]{:S(2)}, u32[]{:S(2)}) %collective-permute-start.3) | collective-permute-done | bytes 49184 | tf_op jit(solution)/shard_map/ppermute | solution.py:270
  40.3 1.3 %collective-permute-start.15 = (bf16[192,768]{1,0:T(8,128)(2,1)S(1)}, bf16[192,768]{1,0:T(8,128)(2,1)S(1)}, u32[]{:S(2)}, u32[]{:S(2)}) collective-permute-start(bf16[192,768]{1,0:T(8,128)(2,1)S(1)} %join.12), channel_id=1, source_target_pairs={{0,4},{1,5},{2,6},{3,7},{4,0},{5,1},{6,2},{7,3},{8,12},{9,13},{10,... | collective-permute-start | bytes 884744 | tf_op jit(solution)/shard_map/ppermute | solution.py:270
  42.1 0.8 %collective-permute-start.14 = (bf16[192,768]{1,0:T(8,128)(2,1)S(1)}, bf16[192,768]{1,0:T(8,128)(2,1)S(1)}, u32[]{:S(2)}, u32[]{:S(2)}) collective-permute-start(bf16[192,768]{1,0:T(8,128)(2,1)S(1)} %join.11), channel_id=1, source_target_pairs={{0,1},{1,0},{2,3},{3,2},{4,5},{5,4},{6,7},{7,6},{8,9},{9,8},{10,11... | collective-permute-start | bytes 884744 | tf_op jit(solution)/shard_map/ppermute | solution.py:270
  42.9 1.4 %collective-permute-start.10 = (f32[16,768]{1,0:T(8,128)S(1)}, f32[16,768]{1,0:T(8,128)S(1)}, u32[]{:S(2)}, u32[]{:S(2)}) collective-permute-start(f32[16,768]{1,0:T(8,128)S(1)} %add.4.refs_0_.refs_2_), channel_id=1, source_target_pairs={{0,24},{1,25},{2,26},{3,27},{4,28},{5,29},{6,30},{7,31},{8,16},{9,... | collective-permute-start | bytes 147464 | tf_op jit(solution)/shard_map/ppermute | solution.py:270
  44.3 3.5 %encode.5 = (bf16[768,768]{1,0:T(8,128)(2,1)S(1)}, f32[768,768]{1,0:T(8,128)S(1)}, f32[6,8,768]{2,1,0:T(8,128)S(1)}) custom-call(bf16[256,768]{1,0:T(8,128)(2,1)S(1)} %collective-permute-done.11.refs_0_, bf16[256,768]{1,0:T(8,128)(2,1)S(1)} %collective-permute-done.12.refs_1_.refs_0_, bf16[256,768]{1,0:T(8,128)(2,1)S(1)} %collective-permute-done.13.refs_2_.refs_1_, ...), custom_call_target="tpu_custom_call" | custom-call | tf_op jit(solution)/shard_map/encode/pallas_call | solution.py:123
  47.8 1.2 %collective-permute-start.18 = (bf16[64,768]{1,0:T(8,128)(2,1)S(1)}, bf16[64,768]{1,0:T(8,128)(2,1)S(1)}, u32[]{:S(2)}, u32[]{:S(2)}) collective-permute-start(bf16[64,768]{1,0:T(8,128)(2,1)S(1)} %join.15), channel_id=1, source_target_pairs={{0,4},{1,5},{2,6},{3,7},{4,0},{5,1},{6,2},{7,3},{8,12},{9,13},{10,... | collective-permute-start | bytes 294920 | tf_op jit(solution)/shard_map/ppermute | solution.py:270
  49.1 1.3 %collective-permute-start.17 = (bf16[64,768]{1,0:T(8,128)(2,1)S(1)}, bf16[64,768]{1,0:T(8,128)(2,1)S(1)}, u32[]{:S(2)}, u32[]{:S(2)}) collective-permute-start(bf16[64,768]{1,0:T(8,128)(2,1)S(1)} %join.14), channel_id=1, source_target_pairs={{0,1},{1,0},{2,3},{3,2},{4,5},{5,4},{6,7},{7,6},{8,9},{9,8},{10,11... | collective-permute-start | bytes 294920 | tf_op jit(solution)/shard_map/ppermute | solution.py:270
  50.7 2.8 %collective-permute-start.9 = (f32[16,768]{1,0:T(8,128)S(1)}, f32[16,768]{1,0:T(8,128)S(1)}, u32[]{:S(2)}, u32[]{:S(2)}) collective-permute-start(f32[16,768]{1,0:T(8,128)S(1)} %add.4.refs_0_.refs_2_), channel_id=1, source_target_pairs={{0,16},{1,17},{2,18},{3,19},{4,20},{5,21},{6,22},{7,23},{8,24},{9,... | collective-permute-start | bytes 147464 | tf_op jit(solution)/shard_map/ppermute | solution.py:270
  53.5 0.9 %collective-permute-done.8.refs_1_ = f32[16,768]{1,0:T(8,128)S(1)} collective-permute-done((f32[16,768]{1,0:T(8,128)S(1)}, f32[16,768]{1,0:T(8,128)S(1)}, u32[]{:S(2)}, u32[]{:S(2)}) %collective-permute-start.8) | collective-permute-done | bytes 49184 | tf_op jit(solution)/shard_map/ppermute | solution.py:270
  54.4 1.3 %collective-permute-done.9.refs_2_ = f32[16,768]{1,0:T(8,128)S(1)} collective-permute-done((f32[16,768]{1,0:T(8,128)S(1)}, f32[16,768]{1,0:T(8,128)S(1)}, u32[]{:S(2)}, u32[]{:S(2)}) %collective-permute-start.9) | collective-permute-done | bytes 49184 | tf_op jit(solution)/shard_map/ppermute | solution.py:270
  55.8 2.4 %encode.6 = (bf16[512,768]{1,0:T(8,128)(2,1)S(1)}, f32[512,768]{1,0:T(8,128)S(1)}, f32[4,8,768]{2,1,0:T(8,128)S(1)}) custom-call(bf16[192,768]{1,0:T(8,128)(2,1)S(1)} %collective-permute-done.14.refs_0_, bf16[192,768]{1,0:T(8,128)(2,1)S(1)} %collective-permute-done.15.refs_1_.refs_0_, bf16[128,768]{1,0:T(8,128)(2,1)S(1)} %collective-permute-done.16.refs_2_.refs_0_, ...), custom_call_target="tpu_custom_call" | custom-call | tf_op jit(solution)/shard_map/encode/pallas_call | solution.py:123
  58.2 0.9 %encode.7 = (bf16[128,768]{1,0:T(8,128)(2,1)S(1)}, f32[128,768]{1,0:T(8,128)S(1)}, f32[1,8,768]{2,1,0:T(8,128)S(1)}) custom-call(bf16[64,768]{1,0:T(8,128)(2,1)S(1)} %collective-permute-done.17.refs_0_, bf16[64,768]{1,0:T(8,128)(2,1)S(1)} %collective-permute-done.18.refs_1_, f32[2,768]{1,0:T(2,128)S(1)} %copy-done.4, bf16[768,768]{1,0:T(8,128)(2,1)S(1)} %copy-done.1), custom_call_target="tpu_custom_call" | custom-call | tf_op jit(solution)/shard_map/encode/pallas_call | solution.py:123
  59.1 4.8 %back.1 = (bf16[768,768]{1,0:T(8,128)(2,1)S(1)}, f32[2,768]{1,0:T(2,128)S(1)}, f32[1,768]{1,0:T(1,128)}) custom-call(f32[16,768]{1,0:T(8,128)S(1)} %add.5.refs_0_, f32[2,768]{1,0:T(2,128)S(1)} %copy-done.4, bf16[768,768]{1,0:T(8,128)(2,1)S(1)} %copy-done.1, bf16[128,768]{1,0:T(8,128)(2,1)S(1)} %get-tuple-element.31.refs_3_, ...), custom_call_target="tpu_custom_call" | custom-call | tf_op jit(solution)/shard_map/back/pallas_call | solution.py:374
  64.4 2.3 %collective-permute-done.20.more_ref = f32[2,768]{1,0:T(2,128)S(1)} collective-permute-done((f32[2,768]{1,0:T(2,128)S(1)}, f32[2,768]{1,0:T(2,128)S(1)}, u32[]{:S(2)}, u32[]{:S(2)}) %collective-permute-start.20) | collective-permute-done | bytes 6176 | tf_op jit(solution)/shard_map/ppermute | solution.py:270
  66.7 2.0 %final.1 = (f32[768,768]{1,0:T(8,128)}, f32[2,768]{1,0:T(2,128)}) custom-call(bf16[768,768]{1,0:T(8,128)(2,1)S(1)} %get-tuple-element.45.mine_ref, bf16[768,768]{1,0:T(8,128)(2,1)S(1)} %collective-permute-done.19.other_ref, f32[2,768]{1,0:T(2,128)S(1)} %get-tuple-element.46.sums_ref, f32[2,768]{1,0:T(2,128)S(1)} %collective-permute-done.20.more_ref), custom_call_target="tpu_custom_call" | custom-call | tf_op jit(solution)/shard_map/final/pallas_call | solution.py:258
  (46 shorter events, 3.5 us)
Async XLA Ops:
  0.6 22.7 %collective-permute-start.7 = (bf16[128,768]{1,0:T(8,128)(2,1)}, bf16[128,768]{1,0:T(8,128)(2,1)S(1)}, u32[]{:S(2)}, u32[]{:S(2)}) collective-permute-start(bf16[128,768]{1,0:T(8,128)(2,1)} %bitcast.1), channel_id=1, source_target_pairs={{0,16},{1,17},{2,18},{3,19},{4,20},{5,21},{6,22},{7,23},{8,24},{9,... | collective-permute-start | bytes 589832 | tf_op jit(solution)/shard_map/ppermute | solution.py:270
  4.7 18.6 %collective-permute-start.5 = (bf16[128,768]{1,0:T(8,128)(2,1)}, bf16[128,768]{1,0:T(8,128)(2,1)S(1)}, u32[]{:S(2)}, u32[]{:S(2)}) collective-permute-start(bf16[128,768]{1,0:T(8,128)(2,1)} %bitcast.2), channel_id=1, source_target_pairs={{0,4},{1,5},{2,6},{3,7},{4,0},{5,1},{6,2},{7,3},{8,12},{9,13},{10,... | collective-permute-start | bytes 589832 | tf_op jit(solution)/shard_map/ppermute | solution.py:270
  6.2 17.1 %collective-permute-start.6 = (bf16[128,768]{1,0:T(8,128)(2,1)}, bf16[128,768]{1,0:T(8,128)(2,1)S(1)}, u32[]{:S(2)}, u32[]{:S(2)}) collective-permute-start(bf16[128,768]{1,0:T(8,128)(2,1)} %bitcast.3), channel_id=1, source_target_pairs={{0,8},{1,9},{2,10},{3,11},{4,12},{5,13},{6,14},{7,15},{8,0},{9,1},... | collective-permute-start | bytes 589832 | tf_op jit(solution)/shard_map/ppermute | solution.py:270
  7.8 16.5 %collective-permute-start.4 = (bf16[128,768]{1,0:T(8,128)(2,1)}, bf16[128,768]{1,0:T(8,128)(2,1)S(1)}, u32[]{:S(2)}, u32[]{:S(2)}) collective-permute-start(bf16[128,768]{1,0:T(8,128)(2,1)} %bitcast.4), channel_id=1, source_target_pairs={{0,1},{1,0},{2,3},{3,2},{4,5},{5,4},{6,7},{7,6},{8,9},{9,8},{10,11... | collective-permute-start | bytes 589832 | tf_op jit(solution)/shard_map/ppermute | solution.py:270
  9.3 1.3 %copy-start = (bf16[768,768]{1,0:T(8,128)(2,1)S(1)}, bf16[768,768]{1,0:T(8,128)(2,1)}, u32[]{:S(2)}) copy-start(bf16[768,768]{1,0:T(8,128)(2,1)} %refs_2_.5) | copy-start | bytes 3538948
  10.6 0.7 %copy-start.3 = (f32[2,768]{1,0:T(2,128)S(1)}, f32[2,768]{1,0:T(2,128)}, u32[]{:S(2)}) copy-start(f32[2,768]{1,0:T(2,128)} %refs_1_.3) | copy-start | bytes 18436
  11.3 0.9 %copy-start.5 = (bf16[1,128,768]{2,1,0:T(8,128)(2,1)S(1)}, bf16[1,128,768]{2,1,0:T(8,128)(2,1)}, u32[]{:S(2)}) copy-start(bf16[1,128,768]{2,1,0:T(8,128)(2,1)} %param.6) | copy-start | bytes 589828
  12.2 0.7 copy-start.7
  23.4 2.3 %copy-start.2 = (bf16[512,768]{1,0:T(8,128)(2,1)S(1)}, bf16[512,768]{1,0:T(8,128)(2,1)}, u32[]{:S(2)}) copy-start(bf16[512,768]{1,0:T(8,128)(2,1)} %weight_ref.1) | copy-start | bytes 2359300
  23.4 2.3 %copy-start.6 = (bf16[512]{0:T(512)(128)(2,1)S(1)}, bf16[512]{0:T(512)(128)(2,1)}, u32[]{:S(2)}) copy-start(bf16[512]{0:T(512)(128)(2,1)} %bias_ref.1) | copy-start | bytes 3076
  23.4 13.0 %copy-start.1 = (bf16[768,768]{1,0:T(8,128)(2,1)S(1)}, bf16[768,768]{1,0:T(8,128)(2,1)}, u32[]{:S(2)}) copy-start(bf16[768,768]{1,0:T(8,128)(2,1)} %refs_2_.5) | copy-start | bytes 3538948
  23.4 13.0 %copy-start.4 = (f32[2,768]{1,0:T(2,128)S(1)}, f32[2,768]{1,0:T(2,128)}, u32[]{:S(2)}) copy-start(f32[2,768]{1,0:T(2,128)} %refs_1_.3) | copy-start | bytes 18436
  23.4 16.9 %collective-permute-start.11 = (bf16[256,768]{1,0:T(8,128)(2,1)S(1)}, bf16[256,768]{1,0:T(8,128)(2,1)S(1)}, u32[]{:S(2)}, u32[]{:S(2)}) collective-permute-start(bf16[256,768]{1,0:T(8,128)(2,1)S(1)} %join.8), channel_id=1, source_target_pairs={{0,1},{1,0},{2,3},{3,2},{4,5},{5,4},{6,7},{7,6},{8,9},{9,8},{10,11... | collective-permute-start | bytes 1179656 | tf_op jit(solution)/shard_map/ppermute | solution.py:270
  24.3 16.0 %collective-permute-start.13 = (bf16[256,768]{1,0:T(8,128)(2,1)S(1)}, bf16[256,768]{1,0:T(8,128)(2,1)S(1)}, u32[]{:S(2)}, u32[]{:S(2)}) collective-permute-start(bf16[256,768]{1,0:T(8,128)(2,1)S(1)} %join.10), channel_id=1, source_target_pairs={{0,8},{1,9},{2,10},{3,11},{4,12},{5,13},{6,14},{7,15},{8,0},{9,1},... | collective-permute-start | bytes 1179656 | tf_op jit(solution)/shard_map/ppermute | solution.py:270
  24.9 16.8 %collective-permute-start.12 = (bf16[256,768]{1,0:T(8,128)(2,1)S(1)}, bf16[256,768]{1,0:T(8,128)(2,1)S(1)}, u32[]{:S(2)}, u32[]{:S(2)}) collective-permute-start(bf16[256,768]{1,0:T(8,128)(2,1)S(1)} %join.9), channel_id=1, source_target_pairs={{0,4},{1,5},{2,6},{3,7},{4,0},{5,1},{6,2},{7,3},{8,12},{9,13},{10,... | collective-permute-start | bytes 1179656 | tf_op jit(solution)/shard_map/ppermute | solution.py:270
  26.3 1.3 %collective-permute-start = (f32[16,768]{1,0:T(8,128)S(1)}, f32[16,768]{1,0:T(8,128)S(1)}, u32[]{:S(2)}, u32[]{:S(2)}) collective-permute-start(f32[16,768]{1,0:T(8,128)S(1)} %get-tuple-element.28), channel_id=1, source_target_pairs={{0,2},{1,3},{2,0},{3,1},{4,6},{5,7},{6,4},{7,5},{8,10},{9,11},{10,... | collective-permute-start | bytes 147464 | tf_op jit(solution)/shard_map/ppermute | solution.py:270
  27.6 7.7 %collective-permute-start.1 = (f32[16,768]{1,0:T(8,128)S(1)}, f32[16,768]{1,0:T(8,128)S(1)}, u32[]{:S(2)}, u32[]{:S(2)}) collective-permute-start(f32[16,768]{1,0:T(8,128)S(1)} %add.3.refs_0_), channel_id=1, source_target_pairs={{0,1},{1,0},{2,3},{3,2},{4,5},{5,4},{6,7},{7,6},{8,9},{9,8},{10,11... | collective-permute-start | bytes 147464 | tf_op jit(solution)/shard_map/ppermute | solution.py:270
  29.1 9.7 %collective-permute-start.2 = (f32[16,768]{1,0:T(8,128)S(1)}, f32[16,768]{1,0:T(8,128)S(1)}, u32[]{:S(2)}, u32[]{:S(2)}) collective-permute-start(f32[16,768]{1,0:T(8,128)S(1)} %add.3.refs_0_), channel_id=1, source_target_pairs={{0,4},{1,5},{2,6},{3,7},{4,0},{5,1},{6,2},{7,3},{8,12},{9,13},{10,... | collective-permute-start | bytes 147464 | tf_op jit(solution)/shard_map/ppermute | solution.py:270
  35.3 5.0 %collective-permute-start.3 = (f32[16,768]{1,0:T(8,128)S(1)}, f32[16,768]{1,0:T(8,128)S(1)}, u32[]{:S(2)}, u32[]{:S(2)}) collective-permute-start(f32[16,768]{1,0:T(8,128)S(1)} %add.3.refs_0_), channel_id=1, source_target_pairs={{0,5},{1,4},{2,7},{3,6},{4,1},{5,0},{6,3},{7,2},{8,13},{9,12},{10,... | collective-permute-start | bytes 147464 | tf_op jit(solution)/shard_map/ppermute | solution.py:270
  40.3 8.7 %collective-permute-start.15 = (bf16[192,768]{1,0:T(8,128)(2,1)S(1)}, bf16[192,768]{1,0:T(8,128)(2,1)S(1)}, u32[]{:S(2)}, u32[]{:S(2)}) collective-permute-start(bf16[192,768]{1,0:T(8,128)(2,1)S(1)} %join.12), channel_id=1, source_target_pairs={{0,4},{1,5},{2,6},{3,7},{4,0},{5,1},{6,2},{7,3},{8,12},{9,13},{10,... | collective-permute-start | bytes 884744 | tf_op jit(solution)/shard_map/ppermute | solution.py:270
  41.7 6.1 %collective-permute-start.16 = (bf16[128,768]{1,0:T(8,128)(2,1)S(1)}, bf16[128,768]{1,0:T(8,128)(2,1)S(1)}, u32[]{:S(2)}, u32[]{:S(2)}) collective-permute-start(bf16[128,768]{1,0:T(8,128)(2,1)S(1)} %join.13), channel_id=1, source_target_pairs={{0,8},{1,9},{2,10},{3,11},{4,12},{5,13},{6,14},{7,15},{8,0},{9,1},... | collective-permute-start | bytes 589832 | tf_op jit(solution)/shard_map/ppermute | solution.py:270
  42.1 13.6 %collective-permute-start.14 = (bf16[192,768]{1,0:T(8,128)(2,1)S(1)}, bf16[192,768]{1,0:T(8,128)(2,1)S(1)}, u32[]{:S(2)}, u32[]{:S(2)}) collective-permute-start(bf16[192,768]{1,0:T(8,128)(2,1)S(1)} %join.11), channel_id=1, source_target_pairs={{0,1},{1,0},{2,3},{3,2},{4,5},{5,4},{6,7},{7,6},{8,9},{9,8},{10,11... | collective-permute-start | bytes 884744 | tf_op jit(solution)/shard_map/ppermute | solution.py:270
  42.9 7.8 %collective-permute-start.10 = (f32[16,768]{1,0:T(8,128)S(1)}, f32[16,768]{1,0:T(8,128)S(1)}, u32[]{:S(2)}, u32[]{:S(2)}) collective-permute-start(f32[16,768]{1,0:T(8,128)S(1)} %add.4.refs_0_.refs_2_), channel_id=1, source_target_pairs={{0,24},{1,25},{2,26},{3,27},{4,28},{5,29},{6,30},{7,31},{8,16},{9,... | collective-permute-start | bytes 147464 | tf_op jit(solution)/shard_map/ppermute | solution.py:270
  47.8 10.3 %collective-permute-start.18 = (bf16[64,768]{1,0:T(8,128)(2,1)S(1)}, bf16[64,768]{1,0:T(8,128)(2,1)S(1)}, u32[]{:S(2)}, u32[]{:S(2)}) collective-permute-start(bf16[64,768]{1,0:T(8,128)(2,1)S(1)} %join.15), channel_id=1, source_target_pairs={{0,4},{1,5},{2,6},{3,7},{4,0},{5,1},{6,2},{7,3},{8,12},{9,13},{10,... | collective-permute-start | bytes 294920 | tf_op jit(solution)/shard_map/ppermute | solution.py:270
  49.1 9.1 %collective-permute-start.17 = (bf16[64,768]{1,0:T(8,128)(2,1)S(1)}, bf16[64,768]{1,0:T(8,128)(2,1)S(1)}, u32[]{:S(2)}, u32[]{:S(2)}) collective-permute-start(bf16[64,768]{1,0:T(8,128)(2,1)S(1)} %join.14), channel_id=1, source_target_pairs={{0,1},{1,0},{2,3},{3,2},{4,5},{5,4},{6,7},{7,6},{8,9},{9,8},{10,11... | collective-permute-start | bytes 294920 | tf_op jit(solution)/shard_map/ppermute | solution.py:270
  50.3 4.1 %collective-permute-start.8 = (f32[16,768]{1,0:T(8,128)S(1)}, f32[16,768]{1,0:T(8,128)S(1)}, u32[]{:S(2)}, u32[]{:S(2)}) collective-permute-start(f32[16,768]{1,0:T(8,128)S(1)} %add.4.refs_0_.refs_2_), channel_id=1, source_target_pairs={{0,8},{1,9},{2,10},{3,11},{4,12},{5,13},{6,14},{7,15},{8,0},{9,1},... | collective-permute-start | bytes 147464 | tf_op jit(solution)/shard_map/ppermute | solution.py:270
  50.7 5.0 %collective-permute-start.9 = (f32[16,768]{1,0:T(8,128)S(1)}, f32[16,768]{1,0:T(8,128)S(1)}, u32[]{:S(2)}, u32[]{:S(2)}) collective-permute-start(f32[16,768]{1,0:T(8,128)S(1)} %add.4.refs_0_.refs_2_), channel_id=1, source_target_pairs={{0,16},{1,17},{2,18},{3,19},{4,20},{5,21},{6,22},{7,23},{8,24},{9,... | collective-permute-start | bytes 147464 | tf_op jit(solution)/shard_map/ppermute | solution.py:270
  63.9 2.9 %collective-permute-start.19 = (bf16[768,768]{1,0:T(8,128)(2,1)S(1)}, bf16[768,768]{1,0:T(8,128)(2,1)S(1)}, u32[]{:S(2)}, u32[]{:S(2)}) collective-permute-start(bf16[768,768]{1,0:T(8,128)(2,1)S(1)} %get-tuple-element.45.mine_ref), channel_id=1, source_target_pairs={{0,2},{1,3},{2,0},{3,1},{4,6},{5,7},{6,4},{7,5},{8,10},{9,11},{10,... | collective-permute-start | bytes 3538952 | tf_op jit(solution)/shard_map/ppermute | solution.py:270
  63.9 2.9 %collective-permute-start.20 = (f32[2,768]{1,0:T(2,128)S(1)}, f32[2,768]{1,0:T(2,128)S(1)}, u32[]{:S(2)}, u32[]{:S(2)}) collective-permute-start(f32[2,768]{1,0:T(2,128)S(1)} %get-tuple-element.46.sums_ref), channel_id=1, source_target_pairs={{0,2},{1,3},{2,0},{3,1},{4,6},{5,7},{6,4},{7,5},{8,10},{9,11},{10,... | collective-permute-start | bytes 18440 | tf_op jit(solution)/shard_map/ppermute | solution.py:270

commit v2 on v1

--- a/solution.py
+++ b/solution.py
@@ -14,12 +14,13 @@
 PIECE = 1 << PIECE_BITS
 DIGITS = 3
 GATHER_LIMIT = 8 << 20
+FIRST_LIMIT = 10 << 20
 f32, bf16 = jnp.float32, jnp.bfloat16
 
 
 def encode_rows(tok, gains, weight):
-    mean = jnp.mean(tok, axis=-1, keepdims=True)
-    center = tok - mean
+    values = tok.astype(f32)
+    center = values - jnp.mean(values, axis=-1, keepdims=True)
     inverse = lax.rsqrt(jnp.mean(center * center, axis=-1, keepdims=True) + epsilon)
     act = (center * inverse * gains[0:1]).astype(bf16)
     pre = jnp.dot(act, weight, preferred_element_type=f32)
@@ -27,9 +28,10 @@
     square = pre * pre
     bend = jnp.tanh(pre * (scale + (scale * 0.044715) * square))
     half = 0.5 * pre
-    gelu = half + half * bend
-    tilt = 0.5 * bend + half * (1.0 - bend * bend) * (scale + (3.0 * scale * 0.044715) * square)
-    return act, tilt, jnp.sum(tok + gelu, axis=0, keepdims=True), jnp.sum(act.astype(f32), axis=0, keepdims=True)
+    bent = half * bend
+    tilt = 0.5 * bend + (half - bent * bend) * (scale + (3.0 * scale * 0.044715) * square)
+    total = jnp.sum(values + (half + bent), axis=0, keepdims=True)
+    return act, tilt, total, jnp.sum(act.astype(f32), axis=0, keepdims=True)
 
 
 def norm_row(pooled):
@@ -54,7 +56,7 @@
         for operand, first, rows in doc:
             for start in range(0, rows, seq // 2):
                 span = min(seq // 2, rows)
-                tok = toks[operand][first + start : first + start + span, :].astype(f32)
+                tok = toks[operand][first + start : first + start + span, :]
                 act, tilt, part, sums = encode_rows(tok, gains, weight)
                 act_ref[at : at + span, :] = act
                 tilt_ref[at : at + span, :] = tilt
@@ -110,10 +112,10 @@
     return pl.pallas_call(
         first_kernel,
         out_shape=encode_shapes(seq, 1, width) + [jax.ShapeDtypeStruct((copies, deep, 128), bf16)],
-        in_specs=[pl.BlockSpec(memory_space=pl.ANY)] * 4,
+        in_specs=[pl.BlockSpec(memory_space=pltpu.HBM)] * 4,
         scratch_shapes=[pltpu.VMEM(a.shape, a.dtype) for a in sources]
         + [pltpu.VMEM((1, 128), f32), pltpu.SemaphoreType.DMA((4,))],
-        compiler_params=pltpu.CompilerParams(vmem_limit_bytes=10 << 20),
+        compiler_params=pltpu.CompilerParams(vmem_limit_bytes=FIRST_LIMIT),
         name="first",
     )(*sources)
 
@@ -170,6 +172,20 @@
         compiler_params=pltpu.CompilerParams(vmem_limit_bytes=4 << 20),
         name="add",
     )(*parts, *tied)
+
+
+def mark_kernel(*refs):
+    refs[-1][...] = jnp.zeros_like(refs[-1])
+
+
+def mark(arrays):
+    return pl.pallas_call(
+        mark_kernel,
+        out_shape=jax.ShapeDtypeStruct((8, 128), f32),
+        in_specs=[pl.BlockSpec(memory_space=pl.ANY)] * len(arrays),
+        compiler_params=pltpu.CompilerParams(vmem_limit_bytes=1 << 20),
+        name="mark",
+    )(*arrays)
 
 
 def head_kernel(slots, rows_ref, weight_ref, bias_ref, mine_ref, other_ref, rows, part):
@@ -200,7 +216,7 @@
 def back_kernel(seq, masks, *refs):
     grad_ref, gains_ref, weight_ref = refs[:3]
     groups = [refs[3 + 3 * g : 6 + 3 * g] for g in range(len(masks))]
-    out_ref, sums_ref, own_ref, act, d_pre, saved, spreads = refs[3 + 3 * len(masks) :]
+    out_ref, own_ref, act, d_pre, saved, spreads = refs[3 + 3 * len(masks) :]
     me, core = number(), lax.axis_size("doc")
     places = [[place(me ^ m, core) for m in group] for group in masks]
     own_ref[...] = grad_ref[pl.ds(place(me, core), 1), :]
@@ -225,10 +241,10 @@
             to = pl.ds(pl.multiple_of(at * seq, seq), seq)
             act[to, :] = act_ref[d * seq : (d + 1) * seq, :]
             d_pre[to, :] = (tilt_ref[d * seq : (d + 1) * seq, :] * spreads[pl.ds(at, 1), :]).astype(bf16)
-    half = 0.5 * spread
-    sums_top, half_top = sums.astype(bf16), half.astype(bf16)
+    even = 0.5 * spread
+    sums_top, half_top = sums.astype(bf16), even.astype(bf16)
     sums_low = (sums - sums_top.astype(f32)).astype(bf16)
-    half_low = (half - half_top.astype(f32)).astype(bf16)
+    half_low = (even - half_top.astype(f32)).astype(bf16)
     even = lax.dot_general(
         jnp.concatenate([sums_top, sums_top, sums_low], axis=0),
         jnp.concatenate([half_top, half_low, half_top], axis=0),
@@ -236,34 +252,49 @@
         preferred_element_type=f32,
     )
     total = even + lax.dot_general(act[...], d_pre[...], (((0,), (0,)), ((), ())), preferred_element_type=f32)
-    out_ref[...] = total.astype(bf16)
+    out_ref[:width, :] = total.astype(bf16)
     weighed = total * weight_ref[...].astype(f32)
     lanes = weighed[:, :128]
     for k in range(1, width // 128):
         lanes = lanes + weighed[:, k * 128 : (k + 1) * 128]
-    sums_ref[0:1, :] = jnp.sum(lanes.T, axis=0, keepdims=True) / gains_ref[0:1, :]
-    sums_ref[1:2, :] = jnp.sum(row * normed, axis=0, keepdims=True)
-
-
-def final_kernel(mine_ref, other_ref, sums_ref, more_ref, weight_ref, gains_ref):
-    weight_ref[...] = mine_ref[...].astype(f32) + other_ref[...].astype(f32)
-    gains_ref[...] = sums_ref[...] + more_ref[...]
-
-
-def final_call(mine, other, sums, more):
-    rows, width = mine.shape
-    steps = 4 if rows % 64 == 0 else 1
-    part = pl.BlockSpec((rows // steps, width), lambda i: (i, 0))
-    whole = pl.BlockSpec(sums.shape, lambda i: (0, 0))
+    gain_in = jnp.sum(lanes.T, axis=0, keepdims=True) / gains_ref[0:1, :]
+    gain_out = jnp.sum(row * normed, axis=0, keepdims=True)
+    rest, terms = jnp.concatenate([gain_in, gain_out], axis=0), []
+    for _ in range(3):
+        terms.append(rest.astype(bf16).astype(f32))
+        rest = rest - terms[-1]
+    terms.append(jnp.zeros((16 - 2 * len(terms), width), f32))
+    out_ref[width:, :] = jnp.concatenate(terms, axis=0).astype(bf16)
+
+
+def final_kernel(steps, mine_ref, other_ref, weight_ref, gains_ref, total, sems):
+    rows = weight_ref.shape[0]
+    span = rows // steps
+    copies = []
+    for k in range(steps):
+        part = pl.ds(k * span, span)
+        total[part, :] = mine_ref[part, :].astype(f32) + other_ref[part, :].astype(f32)
+        copies.append(pltpu.make_async_copy(total.at[part, :], weight_ref.at[part, :], sems.at[k]))
+        copies[-1].start()
+    mine, other = mine_ref[rows:, :].astype(f32), other_ref[rows:, :].astype(f32)
+    gains_ref[...] = (mine[0:2] + mine[2:4] + mine[4:6]) + (other[0:2] + other[2:4] + other[4:6])
+    for copy in copies:
+        copy.wait()
+
+
+def final_call(mine, other):
+    width = mine.shape[1]
+    steps = 8 if width % 128 == 0 else 1
+    vmem, hbm = pl.BlockSpec(memory_space=pltpu.VMEM), pl.BlockSpec(memory_space=pltpu.HBM)
     return pl.pallas_call(
-        final_kernel,
-        grid=(steps,),
-        out_shape=[jax.ShapeDtypeStruct(mine.shape, f32), jax.ShapeDtypeStruct(sums.shape, f32)],
-        in_specs=[part, part, whole, whole],
-        out_specs=[part, whole],
+        functools.partial(final_kernel, steps),
+        out_shape=[jax.ShapeDtypeStruct((width, width), f32), jax.ShapeDtypeStruct((2, width), f32)],
+        in_specs=[vmem] * 2,
+        out_specs=[hbm, vmem],
+        scratch_shapes=[pltpu.VMEM((width, width), f32), pltpu.SemaphoreType.DMA((steps,))],
         compiler_params=pltpu.CompilerParams(vmem_limit_bytes=12 << 20),
         name="final",
-    )(mine, other, sums, more)
+    )(mine, other)
 
 
 def swap(value, mask, count):
@@ -332,23 +363,24 @@
         masks.append(docs)
         return groups[-1][2]
 
-    docs_0, come_0 = exchange({x: [(0, 0, seq)], y: [(0, 0, seq)], z: [(0, 0, seq)], far: [(0, 0, seq)]})
-
+    whole = (0, 0, seq)
+    docs_0, _ = exchange({far: [whole], z: [whole], x: [whole], y: [whole]})
     *group, copies = first_call(own, norm_gains, enc_weight, positives, count)
     groups.append(group)
     masks.append([0])
     rows = lax.all_to_all(copies, AXES, split_axis=0, concat_axis=0, tiled=True, axis_index_groups=[by_core])
 
-    def cube(base):
+    def spread(full, corners):
+        wanted = [(doc, 0, seq) for doc in full]
         return {
-            x: [(base | y, 0, h), (base | z, 0, h)],
-            y: [(base | x, h, seq), (base | z, 0, h)],
-            z: [(base | x, h, seq), (base | y, h, seq)],
+            x: wanted + [(y | doc, 0, h) for doc in corners],
+            y: wanted + [(x | doc, h, seq) for doc in corners],
         }
 
-    def corner(base):
-        return {x: [(base | y | z, 0, h)], y: [(base | x | z, h, seq)]}
-
+    early = mark([held[far][0][0]])
+    plan = spread([z, far], [0])
+    plan[z] = [(far, 0, seq)]
+    docs_1, _ = exchange(plan, [groups[0][2], early])
     mine, other = pl.pallas_call(
         functools.partial(head_kernel, slots),
         out_shape=[jax.ShapeDtypeStruct((half, width), f32)] * 2,
@@ -357,25 +389,27 @@
         name="head",
     )(rows, head_weight, head_bias)
 
-    plan = cube(0)
-    docs_1, _ = exchange({to: [(far, 0, seq)] + plan[to] for to in plan}, [rows])
+    total = add([mine, hop(other, core)])
+    plan = spread([z | far], [z, far])
+    docs_2, _ = exchange(plan, [total])
     tied = encode_held(docs_0)
-    total = add([mine, hop(other, core)])
-    total = add([total] + [hop(total, m) for m in (x, y, x | y)], [tied])
-    plan, last = cube(far), corner(0)
-    docs_2, _ = exchange({to: plan[to] + last.get(to, []) for to in plan}, [total])
-    tied = encode_held(docs_1)
-    total = add([total] + [hop(total, m) for m in (z, far, z | far)], [tied])
-    docs_3, _ = exchange(corner(far), [tied])
-    encode_held(docs_2)
+    total = add([total, hop(total, z)], [tied])
+    tied = encode_held(docs_1[:4])
+    total = add([total, hop(total, far)], [tied])
+    plan = spread([], [z | far])
+    docs_3, _ = exchange(plan, [total])
+    rest = docs_1[4:]
+    tied = [encode_held(rest)] if rest else []
+    total = add([total, hop(total, x)], tied)
+    tied = encode_held(docs_2)
+    total = add([total, hop(total, y)], [tied])
     encode_held(docs_3)
 
     operands = [array for group in groups for array in group]
-    part, sums, row_grad = pl.pallas_call(
+    part, row_grad = pl.pallas_call(
         functools.partial(back_kernel, seq, masks),
         out_shape=[
-            jax.ShapeDtypeStruct((width, width), bf16),
-            jax.ShapeDtypeStruct((2, width), f32),
+            jax.ShapeDtypeStruct((width + 16, width), bf16),
             jax.ShapeDtypeStruct((1, width), f32),
         ],
         scratch_shapes=[
@@ -387,7 +421,7 @@
         compiler_params=pltpu.CompilerParams(vmem_limit_bytes=32 << 20),
         name="back",
     )(total, norm_gains, enc_weight, *operands)
-    weight_grad, gain_grads = final_call(part, hop(part, core), sums, hop(sums, core))
+    weight_grad, gain_grads = final_call(part, hop(part, core))
     return row_grad, weight_grad, gain_grads
 
 

time: 68.9 us -> 62.9 us (0.913)
  waiting for transfers between devices: 11.9 us -> 5.59 us
  starting transfers between devices: 25.2 us -> 23.8 us
  blocking collectives: 9.02 us -> 10.2 us
    ppermute x21 -> x17, waiting for transfers between devices: 11.9 us -> 5.59 us  [swap(): return lax.ppermute(value, AXES, [(i, i ^ mask) for i in range(count)])]
    ppermute x21 -> x17, starting transfers between devices: 25.2 us -> 23.8 us  [swap(): return lax.ppermute(value, AXES, [(i, i ^ mask) for i in range(count)])]
    all_to_all x1, blocking collectives: 9.02 us -> 10.2 us  [gathered(): lax.all_to_all(copies, AXES, split_axis=0, concat_axis=0, tiled=True, axi...]
    pallas_call x4 -> x5, Pallas kernels: 9.21 us -> 9.42 us  [encode_call(): pl.pallas_call(functools.partial(encode_kernel, layout), out_shape=encode...]
    pallas_call x1 -> x2, Pallas kernels: 1.95 us -> 2.09 us  [the longest x1 2.09 us: final_call(): pl.pallas_call(functools.partial(final_kernel, steps), out_shape=[jax.Sha...]
  transfers between devices with their start and end apart: 21 -> 17, of which waited for: 6 -> 4; matrix products, arithmetic and copies ran while one was open for 0% -> 0% of each run, Pallas kernels for 15% -> 17%
where the time goes in v2:
time: 62.9 us; the launch traced here: 62.6 us
  starting transfers between devices  23.8 us (38%)
  Pallas kernels  18.6 us (30%)
  blocking collectives  10.2 us (16%)
  waiting for transfers between devices  5.59 us (9%)
  local copies, waits for them, and re-layouts  3.56 us (6%)
  between operations  0.82 us (1%)
    ppermute x17, starting transfers between devices, swap(): return lax.ppermute(value, AXES, [(i, i ^ mask) for i in range(count)])  23.8 us
    all_to_all x1, blocking collectives, gathered(): lax.all_to_all(copies, AXES, split_axis=0, concat_axis=0, tiled=True, axi...  10.2 us
    pallas_call x5, Pallas kernels, encode_call(): pl.pallas_call(functools.partial(encode_kernel, layout), out_shape=encode...  9.42 us
    ppermute x17, waiting for transfers between devices, swap(): return lax.ppermute(value, AXES, [(i, i ^ mask) for i in range(count)])  5.59 us
    pallas_call x1, Pallas kernels, gathered(): pl.pallas_call(functools.partial(back_kernel, seq, masks), out_shape=[jax...  4.77 us
    unnamed x16, local copies, waits for them, and re-layouts  3.56 us
    pallas_call x1, Pallas kernels, final_call(): pl.pallas_call(functools.partial(final_kernel, steps), out_shape=[jax.Sha...  2.09 us
    pallas_call x1, Pallas kernels, first_call(): pl.pallas_call(first_kernel, out_shape=encode_shapes(seq, 1, width) + [ja...  1.46 us
  transfers between devices with their start and end apart: 17, of which 4 were waited for; matrix products, arithmetic and copies ran while one was open for 0% of the time, Pallas kernels for 17%

profile of v2, /device:TPU:0, one launch (start us, length us, event | category | flops | bytes accessed | tf_op | source)
XLA Modules:
  0.0 62.6 jit_solution(16385562677642852656)
XLA Ops:
  0.6 4.1 %collective-permute-start.2 = (bf16[128,768]{1,0:T(8,128)(2,1)}, bf16[128,768]{1,0:T(8,128)(2,1)S(1)}, u32[]{:S(2)}, u32[]{:S(2)}) collective-permute-start(bf16[128,768]{1,0:T(8,128)(2,1)} %bitcast.1), channel_id=1, source_target_pairs={{0,16},{1,17},{2,18},{3,19},{4,20},{5,21},{6,22},{7,23},{8,24},{9,... | collective-permute-start | bytes 589832 | tf_op jit(solution)/shard_map/ppermute | solution.py:301
  4.7 1.5 %collective-permute-start.5 = (bf16[128,768]{1,0:T(8,128)(2,1)}, bf16[128,768]{1,0:T(8,128)(2,1)S(1)}, u32[]{:S(2)}, u32[]{:S(2)}) collective-permute-start(bf16[128,768]{1,0:T(8,128)(2,1)} %bitcast.2), channel_id=1, source_target_pairs={{0,4},{1,5},{2,6},{3,7},{4,0},{5,1},{6,2},{7,3},{8,12},{9,13},{10,... | collective-permute-start | bytes 589832 | tf_op jit(solution)/shard_map/ppermute | solution.py:301
  6.2 1.6 %collective-permute-start.3 = (bf16[128,768]{1,0:T(8,128)(2,1)}, bf16[128,768]{1,0:T(8,128)(2,1)S(1)}, u32[]{:S(2)}, u32[]{:S(2)}) collective-permute-start(bf16[128,768]{1,0:T(8,128)(2,1)} %bitcast.3), channel_id=1, source_target_pairs={{0,8},{1,9},{2,10},{3,11},{4,12},{5,13},{6,14},{7,15},{8,0},{9,1},... | collective-permute-start | bytes 589832 | tf_op jit(solution)/shard_map/ppermute | solution.py:301
  7.8 1.5 %collective-permute-start.4 = (bf16[128,768]{1,0:T(8,128)(2,1)}, bf16[128,768]{1,0:T(8,128)(2,1)S(1)}, u32[]{:S(2)}, u32[]{:S(2)}) collective-permute-start(bf16[128,768]{1,0:T(8,128)(2,1)} %bitcast.4), channel_id=1, source_target_pairs={{0,1},{1,0},{2,3},{3,2},{4,5},{5,4},{6,7},{7,6},{8,9},{9,8},{10,11... | collective-permute-start | bytes 589832 | tf_op jit(solution)/shard_map/ppermute | solution.py:301
  9.3 1.3 %copy-done = bf16[768,768]{1,0:T(8,128)(2,1)S(1)} copy-done((bf16[768,768]{1,0:T(8,128)(2,1)S(1)}, bf16[768,768]{1,0:T(8,128)(2,1)}, u32[]{:S(2)}) %copy-start) | copy-done | bytes 1179672
  10.6 0.7 %copy-done.3 = f32[2,768]{1,0:T(2,128)S(1)} copy-done((f32[2,768]{1,0:T(2,128)S(1)}, f32[2,768]{1,0:T(2,128)}, u32[]{:S(2)}) %copy-start.3) | copy-done | bytes 6168
  11.3 0.9 %copy-done.5 = bf16[1,128,768]{2,1,0:T(8,128)(2,1)S(1)} copy-done((bf16[1,128,768]{2,1,0:T(8,128)(2,1)S(1)}, bf16[1,128,768]{2,1,0:T(8,128)(2,1)}, u32[]{:S(2)}) %copy-start.5) | copy-done | bytes 196632
  12.2 0.7 %copy-done.7 = s32[1,8]{1,0:T(1,128)S(1)} copy-done((s32[1,8]{1,0:T(1,128)S(1)}, s32[1,8]{1,0:T(1,128)}, u32[]{:S(2)}) %copy-start.7) | copy-done | bytes 56
  12.9 1.5 %first.1 = (bf16[128,768]{1,0:T(8,128)(2,1)S(1)}, f32[128,768]{1,0:T(8,128)S(1)}, f32[1,8,768]{2,1,0:T(8,128)S(1)}, bf16[32,8,128]{2,1,0:T(8,128)(2,1)S(1)}) custom-call(bf16[128,768]{1,0:T(8,128)(2,1)S(1)} %bitcast.5, f32[2,768]{1,0:T(2,128)S(1)} %copy-done.3, bf16[768,768]{1,0:T(8,128)(2,1)S(1)} %copy-done, s32[1,8]{1,0:T(1,128)S(1)} %copy-done.7), custom_call_target="tpu_custom_call" | custom-call | tf_op jit(solution)/shard_map/first/pallas_call | solution.py:112
  14.4 1.2 %collective-permute-done.3.refs_1_.refs_0_ = bf16[128,768]{1,0:T(8,128)(2,1)S(1)} collective-permute-done((bf16[128,768]{1,0:T(8,128)(2,1)}, bf16[128,768]{1,0:T(8,128)(2,1)S(1)}, u32[]{:S(2)}, u32[]{:S(2)}) %collective-permute-start.3) | collective-permute-done | bytes 196640 | tf_op jit(solution)/shard_map/ppermute | solution.py:301
  15.6 1.6 %collective-permute-start.7 = (bf16[320,768]{1,0:T(8,128)(2,1)S(1)}, bf16[320,768]{1,0:T(8,128)(2,1)S(1)}, u32[]{:S(2)}, u32[]{:S(2)}) collective-permute-start(bf16[320,768]{1,0:T(8,128)(2,1)S(1)} %join.7), channel_id=1, source_target_pairs={{0,1},{1,0},{2,3},{3,2},{4,5},{5,4},{6,7},{7,6},{8,9},{9,8},{10,11... | collective-permute-start | bytes 1474568 | tf_op jit(solution)/shard_map/ppermute | solution.py:301
  17.3 0.6 collective-permute-start.8
  17.9 1.2 %collective-permute-start.10 = (bf16[128,768]{1,0:T(8,128)(2,1)S(1)}, bf16[128,768]{1,0:T(8,128)(2,1)S(1)}, u32[]{:S(2)}, u32[]{:S(2)}) collective-permute-start(bf16[128,768]{1,0:T(8,128)(2,1)S(1)} %join.9), channel_id=1, source_target_pairs={{0,8},{1,9},{2,10},{3,11},{4,12},{5,13},{6,14},{7,15},{8,0},{9,1},... | collective-permute-start | bytes 589832 | tf_op jit(solution)/shard_map/ppermute | solution.py:301
  19.1 10.2 %all_to_all.5.rows_ref = bf16[32,8,128]{2,1,0:T(8,128)(2,1)S(1)} all-to-all(bf16[32,8,128]{2,1,0:T(8,128)(2,1)S(1)} %get-tuple-element.28), channel_id=1, replica_groups={{0,1,4,5,8,9,12,13,16,17,20,21,24,25,28,29,2,3,6,7,10,11,14,15,18,19,22..., dimensions={0} | all-to-all | bytes 131072 | tf_op jit(solution)/shard_map/all_to_all | solution.py:371
  29.4 0.7 %head.1 = (f32[16,768]{1,0:T(8,128)S(1)}, f32[16,768]{1,0:T(8,128)S(1)}) custom-call(bf16[32,8,128]{2,1,0:T(8,128)(2,1)S(1)} %all_to_all.5.rows_ref, bf16[512,768]{1,0:T(8,128)(2,1)S(1)} %copy-done.2, bf16[512]{0:T(512)(128)(2,1)S(1)} %copy-done.6), custom_call_target="tpu_custom_call" | custom-call | tf_op jit(solution)/shard_map/head/pallas_call | solution.py:384
  30.2 1.2 %collective-permute-done.refs_1_ = f32[16,768]{1,0:T(8,128)S(1)} collective-permute-done((f32[16,768]{1,0:T(8,128)S(1)}, f32[16,768]{1,0:T(8,128)S(1)}, u32[]{:S(2)}, u32[]{:S(2)}) %collective-permute-start) | collective-permute-done | bytes 49184 | tf_op jit(solution)/shard_map/ppermute | solution.py:301
  31.5 0.9 %collective-permute-start.13 = (bf16[256,768]{1,0:T(8,128)(2,1)S(1)}, bf16[256,768]{1,0:T(8,128)(2,1)S(1)}, u32[]{:S(2)}, u32[]{:S(2)}) collective-permute-start(bf16[256,768]{1,0:T(8,128)(2,1)S(1)} %join.11), channel_id=1, source_target_pairs={{0,4},{1,5},{2,6},{3,7},{4,0},{5,1},{6,2},{7,3},{8,12},{9,13},{10,... | collective-permute-start | bytes 1179656 | tf_op jit(solution)/shard_map/ppermute | solution.py:301
  32.4 1.2 %collective-permute-start.12 = (bf16[256,768]{1,0:T(8,128)(2,1)S(1)}, bf16[256,768]{1,0:T(8,128)(2,1)S(1)}, u32[]{:S(2)}, u32[]{:S(2)}) collective-permute-start(bf16[256,768]{1,0:T(8,128)(2,1)S(1)} %join.10), channel_id=1, source_target_pairs={{0,1},{1,0},{2,3},{3,2},{4,5},{5,4},{6,7},{7,6},{8,9},{9,8},{10,11... | collective-permute-start | bytes 1179656 | tf_op jit(solution)/shard_map/ppermute | solution.py:301
  33.6 1.8 %collective-permute-start.1 = (f32[16,768]{1,0:T(8,128)S(1)}, f32[16,768]{1,0:T(8,128)S(1)}, u32[]{:S(2)}, u32[]{:S(2)}) collective-permute-start(f32[16,768]{1,0:T(8,128)S(1)} %add.5.refs_0_.refs_2_), channel_id=1, source_target_pairs={{0,8},{1,9},{2,10},{3,11},{4,12},{5,13},{6,14},{7,15},{8,0},{9,1},... | collective-permute-start | bytes 147464 | tf_op jit(solution)/shard_map/ppermute | solution.py:301
  35.4 2.4 %encode.5 = (bf16[512,768]{1,0:T(8,128)(2,1)S(1)}, f32[512,768]{1,0:T(8,128)S(1)}, f32[4,8,768]{2,1,0:T(8,128)S(1)}) custom-call(bf16[128,768]{1,0:T(8,128)(2,1)S(1)} %collective-permute-done.2.refs_0_.refs_1_, bf16[128,768]{1,0:T(8,128)(2,1)S(1)} %collective-permute-done.3.refs_1_.refs_0_, bf16[128,768]{1,0:T(8,128)(2,1)S(1)} %collective-permute-done.4.refs_2_, ...), custom_call_target="tpu_custom_call" | custom-call | tf_op jit(solution)/shard_map/encode/pallas_call | solution.py:125
  37.8 3.3 %collective-permute-start.6 = (f32[16,768]{1,0:T(8,128)S(1)}, f32[16,768]{1,0:T(8,128)S(1)}, u32[]{:S(2)}, u32[]{:S(2)}) collective-permute-start(f32[16,768]{1,0:T(8,128)S(1)} %add.6.refs_0_), channel_id=1, source_target_pairs={{0,16},{1,17},{2,18},{3,19},{4,20},{5,21},{6,22},{7,23},{8,24},{9,... | collective-permute-start | bytes 147464 | tf_op jit(solution)/shard_map/ppermute | solution.py:301
  41.1 2.4 %encode.6 = (bf16[512,768]{1,0:T(8,128)(2,1)S(1)}, f32[512,768]{1,0:T(8,128)S(1)}, f32[4,8,768]{2,1,0:T(8,128)S(1)}) custom-call(bf16[320,768]{1,0:T(8,128)(2,1)S(1)} %collective-permute-done.7.refs_0_.refs_1_, bf16[320,768]{1,0:T(8,128)(2,1)S(1)} %collective-permute-done.8.refs_1_.refs_0_, f32[2,768]{1,0:T(2,128)S(1)} %copy-done.4, ...), custom_call_target="tpu_custom_call" | custom-call | tf_op jit(solution)/shard_map/encode/pallas_call | solution.py:125
  43.5 0.6 collective-permute-start.9
  44.1 1.6 %collective-permute-start.14 = (bf16[64,768]{1,0:T(8,128)(2,1)S(1)}, bf16[64,768]{1,0:T(8,128)(2,1)S(1)}, u32[]{:S(2)}, u32[]{:S(2)}) collective-permute-start(bf16[64,768]{1,0:T(8,128)(2,1)S(1)} %join.12), channel_id=1, source_target_pairs={{0,1},{1,0},{2,3},{3,2},{4,5},{5,4},{6,7},{7,6},{8,9},{9,8},{10,11... | collective-permute-start | bytes 294920 | tf_op jit(solution)/shard_map/ppermute | solution.py:301
  45.7 0.6 %collective-permute-start.15 = (bf16[64,768]{1,0:T(8,128)(2,1)S(1)}, bf16[64,768]{1,0:T(8,128)(2,1)S(1)}, u32[]{:S(2)}, u32[]{:S(2)}) collective-permute-start(bf16[64,768]{1,0:T(8,128)(2,1)S(1)} %join.13), channel_id=1, source_target_pairs={{0,4},{1,5},{2,6},{3,7},{4,0},{5,1},{6,2},{7,3},{8,12},{9,13},{10,... | collective-permute-start | bytes 294920 | tf_op jit(solution)/shard_map/ppermute | solution.py:301
  46.4 1.4 %encode.7 = (bf16[256,768]{1,0:T(8,128)(2,1)S(1)}, f32[256,768]{1,0:T(8,128)S(1)}, f32[2,8,768]{2,1,0:T(8,128)S(1)}) custom-call(bf16[320,768]{1,0:T(8,128)(2,1)S(1)} %collective-permute-done.8.refs_1_.refs_0_, bf16[128,768]{1,0:T(8,128)(2,1)S(1)} %collective-permute-done.10.refs_1_.refs_0_, f32[2,768]{1,0:T(2,128)S(1)} %copy-done.4, ...), custom_call_target="tpu_custom_call" | custom-call | tf_op jit(solution)/shard_map/encode/pallas_call | solution.py:125
  47.8 1.5 %collective-permute-start.11 = (f32[16,768]{1,0:T(8,128)S(1)}, f32[16,768]{1,0:T(8,128)S(1)}, u32[]{:S(2)}, u32[]{:S(2)}) collective-permute-start(f32[16,768]{1,0:T(8,128)S(1)} %add.8.refs_0_), channel_id=1, source_target_pairs={{0,4},{1,5},{2,6},{3,7},{4,0},{5,1},{6,2},{7,3},{8,12},{9,13},{10,... | collective-permute-start | bytes 147464 | tf_op jit(solution)/shard_map/ppermute | solution.py:301
  49.3 2.4 %encode.8 = (bf16[512,768]{1,0:T(8,128)(2,1)S(1)}, f32[512,768]{1,0:T(8,128)S(1)}, f32[4,8,768]{2,1,0:T(8,128)S(1)}) custom-call(bf16[256,768]{1,0:T(8,128)(2,1)S(1)} %collective-permute-done.12.refs_0_, bf16[256,768]{1,0:T(8,128)(2,1)S(1)} %collective-permute-done.13.refs_1_.refs_0_, f32[2,768]{1,0:T(2,128)S(1)} %copy-done.4, bf16[768,768]{1,0:T(8,128)(2,1)S(1)} %copy-done.1), custom_call_target="tpu_custom_call" | custom-call | tf_op jit(solution)/shard_map/encode/pallas_call | solution.py:125
  51.9 0.9 %encode.9 = (bf16[128,768]{1,0:T(8,128)(2,1)S(1)}, f32[128,768]{1,0:T(8,128)S(1)}, f32[1,8,768]{2,1,0:T(8,128)S(1)}) custom-call(bf16[64,768]{1,0:T(8,128)(2,1)S(1)} %collective-permute-done.14.refs_0_, bf16[64,768]{1,0:T(8,128)(2,1)S(1)} %collective-permute-done.15.refs_1_, f32[2,768]{1,0:T(2,128)S(1)} %copy-done.4, bf16[768,768]{1,0:T(8,128)(2,1)S(1)} %copy-done.1), custom_call_target="tpu_custom_call" | custom-call | tf_op jit(solution)/shard_map/encode/pallas_call | solution.py:125
  52.9 4.8 %back.1 = (bf16[784,768]{1,0:T(8,128)(2,1)S(1)}, f32[1,768]{1,0:T(1,128)}) custom-call(f32[16,768]{1,0:T(8,128)S(1)} %add.9.refs_0_, f32[2,768]{1,0:T(2,128)S(1)} %copy-done.4, bf16[768,768]{1,0:T(8,128)(2,1)S(1)} %copy-done.1, bf16[128,768]{1,0:T(8,128)(2,1)S(1)} %get-tuple-element.36.refs_3_, f32[128,768]{1,0:T(8,128)S(1)} %get-tuple-element.37.refs_4_, ...), custom_call_target="tpu_custom_call" | custom-call | tf_op jit(solution)/shard_map/back/pallas_call | solution.py:409
  57.7 2.9 %collective-permute-done.16.other_ref = bf16[784,768]{1,0:T(8,128)(2,1)S(1)} collective-permute-done((bf16[784,768]{1,0:T(8,128)(2,1)S(1)}, bf16[784,768]{1,0:T(8,128)(2,1)S(1)}, u32[]{:S(2)}, u32[]{:S(2)}) %collective-permute-start.16) | collective-permute-done | bytes 1204256 | tf_op jit(solution)/shard_map/ppermute | solution.py:301
  60.5 2.1 %final.1 = (f32[768,768]{1,0:T(8,128)}, f32[2,768]{1,0:T(2,128)}) custom-call(bf16[784,768]{1,0:T(8,128)(2,1)S(1)} %get-tuple-element.50.mine_ref, bf16[784,768]{1,0:T(8,128)(2,1)S(1)} %collective-permute-done.16.other_ref), custom_call_target="tpu_custom_call" | custom-call | tf_op jit(solution)/shard_map/final/pallas_call | solution.py:289
  (41 shorter events, 0.6 us)
Async XLA Ops:
  0.6 13.7 %collective-permute-start.2 = (bf16[128,768]{1,0:T(8,128)(2,1)}, bf16[128,768]{1,0:T(8,128)(2,1)S(1)}, u32[]{:S(2)}, u32[]{:S(2)}) collective-permute-start(bf16[128,768]{1,0:T(8,128)(2,1)} %bitcast.1), channel_id=1, source_target_pairs={{0,16},{1,17},{2,18},{3,19},{4,20},{5,21},{6,22},{7,23},{8,24},{9,... | collective-permute-start | bytes 589832 | tf_op jit(solution)/shard_map/ppermute | solution.py:301
  4.7 9.6 %collective-permute-start.5 = (bf16[128,768]{1,0:T(8,128)(2,1)}, bf16[128,768]{1,0:T(8,128)(2,1)S(1)}, u32[]{:S(2)}, u32[]{:S(2)}) collective-permute-start(bf16[128,768]{1,0:T(8,128)(2,1)} %bitcast.2), channel_id=1, source_target_pairs={{0,4},{1,5},{2,6},{3,7},{4,0},{5,1},{6,2},{7,3},{8,12},{9,13},{10,... | collective-permute-start | bytes 589832 | tf_op jit(solution)/shard_map/ppermute | solution.py:301
  6.2 9.3 %collective-permute-start.3 = (bf16[128,768]{1,0:T(8,128)(2,1)}, bf16[128,768]{1,0:T(8,128)(2,1)S(1)}, u32[]{:S(2)}, u32[]{:S(2)}) collective-permute-start(bf16[128,768]{1,0:T(8,128)(2,1)} %bitcast.3), channel_id=1, source_target_pairs={{0,8},{1,9},{2,10},{3,11},{4,12},{5,13},{6,14},{7,15},{8,0},{9,1},... | collective-permute-start | bytes 589832 | tf_op jit(solution)/shard_map/ppermute | solution.py:301
  7.8 9.4 %collective-permute-start.4 = (bf16[128,768]{1,0:T(8,128)(2,1)}, bf16[128,768]{1,0:T(8,128)(2,1)S(1)}, u32[]{:S(2)}, u32[]{:S(2)}) collective-permute-start(bf16[128,768]{1,0:T(8,128)(2,1)} %bitcast.4), channel_id=1, source_target_pairs={{0,1},{1,0},{2,3},{3,2},{4,5},{5,4},{6,7},{7,6},{8,9},{9,8},{10,11... | collective-permute-start | bytes 589832 | tf_op jit(solution)/shard_map/ppermute | solution.py:301
  9.3 1.3 %copy-start = (bf16[768,768]{1,0:T(8,128)(2,1)S(1)}, bf16[768,768]{1,0:T(8,128)(2,1)}, u32[]{:S(2)}) copy-start(bf16[768,768]{1,0:T(8,128)(2,1)} %refs_2_.11) | copy-start | bytes 3538948
  10.6 0.7 %copy-start.3 = (f32[2,768]{1,0:T(2,128)S(1)}, f32[2,768]{1,0:T(2,128)}, u32[]{:S(2)}) copy-start(f32[2,768]{1,0:T(2,128)} %refs_1_.3) | copy-start | bytes 18436
  11.3 0.9 %copy-start.5 = (bf16[1,128,768]{2,1,0:T(8,128)(2,1)S(1)}, bf16[1,128,768]{2,1,0:T(8,128)(2,1)}, u32[]{:S(2)}) copy-start(bf16[1,128,768]{2,1,0:T(8,128)(2,1)} %param.6) | copy-start | bytes 589828
  12.2 0.7 %copy-start.7 = (s32[1,8]{1,0:T(1,128)S(1)}, s32[1,8]{1,0:T(1,128)}, u32[]{:S(2)}) copy-start(s32[1,8]{1,0:T(1,128)} %refs_3_.5) | copy-start | bytes 100
  14.3 15.1 %copy-start.2 = (bf16[512,768]{1,0:T(8,128)(2,1)S(1)}, bf16[512,768]{1,0:T(8,128)(2,1)}, u32[]{:S(2)}) copy-start(bf16[512,768]{1,0:T(8,128)(2,1)} %weight_ref.1) | copy-start | bytes 2359300
  14.3 15.0 %copy-start.6 = (bf16[512]{0:T(512)(128)(2,1)S(1)}, bf16[512]{0:T(512)(128)(2,1)}, u32[]{:S(2)}) copy-start(bf16[512]{0:T(512)(128)(2,1)} %bias_ref.1) | copy-start | bytes 3076
  15.6 15.8 %collective-permute-start.7 = (bf16[320,768]{1,0:T(8,128)(2,1)S(1)}, bf16[320,768]{1,0:T(8,128)(2,1)S(1)}, u32[]{:S(2)}, u32[]{:S(2)}) collective-permute-start(bf16[320,768]{1,0:T(8,128)(2,1)S(1)} %join.7), channel_id=1, source_target_pairs={{0,1},{1,0},{2,3},{3,2},{4,5},{5,4},{6,7},{7,6},{8,9},{9,8},{10,11... | collective-permute-start | bytes 1474568 | tf_op jit(solution)/shard_map/ppermute | solution.py:301
  17.3 15.1 %collective-permute-start.8 = (bf16[320,768]{1,0:T(8,128)(2,1)S(1)}, bf16[320,768]{1,0:T(8,128)(2,1)S(1)}, u32[]{:S(2)}, u32[]{:S(2)}) collective-permute-start(bf16[320,768]{1,0:T(8,128)(2,1)S(1)} %join.8), channel_id=1, source_target_pairs={{0,4},{1,5},{2,6},{3,7},{4,0},{5,1},{6,2},{7,3},{8,12},{9,13},{10,... | collective-permute-start | bytes 1474568 | tf_op jit(solution)/shard_map/ppermute | solution.py:301
  17.9 13.5 %collective-permute-start.10 = (bf16[128,768]{1,0:T(8,128)(2,1)S(1)}, bf16[128,768]{1,0:T(8,128)(2,1)S(1)}, u32[]{:S(2)}, u32[]{:S(2)}) collective-permute-start(bf16[128,768]{1,0:T(8,128)(2,1)S(1)} %join.9), channel_id=1, source_target_pairs={{0,8},{1,9},{2,10},{3,11},{4,12},{5,13},{6,14},{7,15},{8,0},{9,1},... | collective-permute-start | bytes 589832 | tf_op jit(solution)/shard_map/ppermute | solution.py:301
  29.4 6.0 %copy-start.1 = (bf16[768,768]{1,0:T(8,128)(2,1)S(1)}, bf16[768,768]{1,0:T(8,128)(2,1)}, u32[]{:S(2)}) copy-start(bf16[768,768]{1,0:T(8,128)(2,1)} %refs_2_.11) | copy-start | bytes 3538948
  29.4 6.0 %copy-start.4 = (f32[2,768]{1,0:T(2,128)S(1)}, f32[2,768]{1,0:T(2,128)}, u32[]{:S(2)}) copy-start(f32[2,768]{1,0:T(2,128)} %refs_1_.3) | copy-start | bytes 18436
  30.1 1.3 %collective-permute-start = (f32[16,768]{1,0:T(8,128)S(1)}, f32[16,768]{1,0:T(8,128)S(1)}, u32[]{:S(2)}, u32[]{:S(2)}) collective-permute-start(f32[16,768]{1,0:T(8,128)S(1)} %get-tuple-element.30), channel_id=1, source_target_pairs={{0,2},{1,3},{2,0},{3,1},{4,6},{5,7},{6,4},{7,5},{8,10},{9,11},{10,... | collective-permute-start | bytes 147464 | tf_op jit(solution)/shard_map/ppermute | solution.py:301
  31.5 12.7 %collective-permute-start.13 = (bf16[256,768]{1,0:T(8,128)(2,1)S(1)}, bf16[256,768]{1,0:T(8,128)(2,1)S(1)}, u32[]{:S(2)}, u32[]{:S(2)}) collective-permute-start(bf16[256,768]{1,0:T(8,128)(2,1)S(1)} %join.11), channel_id=1, source_target_pairs={{0,4},{1,5},{2,6},{3,7},{4,0},{5,1},{6,2},{7,3},{8,12},{9,13},{10,... | collective-permute-start | bytes 1179656 | tf_op jit(solution)/shard_map/ppermute | solution.py:301
  32.4 13.3 %collective-permute-start.12 = (bf16[256,768]{1,0:T(8,128)(2,1)S(1)}, bf16[256,768]{1,0:T(8,128)(2,1)S(1)}, u32[]{:S(2)}, u32[]{:S(2)}) collective-permute-start(bf16[256,768]{1,0:T(8,128)(2,1)S(1)} %join.10), channel_id=1, source_target_pairs={{0,1},{1,0},{2,3},{3,2},{4,5},{5,4},{6,7},{7,6},{8,9},{9,8},{10,11... | collective-permute-start | bytes 1179656 | tf_op jit(solution)/shard_map/ppermute | solution.py:301
  33.6 4.2 %collective-permute-start.1 = (f32[16,768]{1,0:T(8,128)S(1)}, f32[16,768]{1,0:T(8,128)S(1)}, u32[]{:S(2)}, u32[]{:S(2)}) collective-permute-start(f32[16,768]{1,0:T(8,128)S(1)} %add.5.refs_0_.refs_2_), channel_id=1, source_target_pairs={{0,8},{1,9},{2,10},{3,11},{4,12},{5,13},{6,14},{7,15},{8,0},{9,1},... | collective-permute-start | bytes 147464 | tf_op jit(solution)/shard_map/ppermute | solution.py:301
  37.8 5.7 %collective-permute-start.6 = (f32[16,768]{1,0:T(8,128)S(1)}, f32[16,768]{1,0:T(8,128)S(1)}, u32[]{:S(2)}, u32[]{:S(2)}) collective-permute-start(f32[16,768]{1,0:T(8,128)S(1)} %add.6.refs_0_), channel_id=1, source_target_pairs={{0,16},{1,17},{2,18},{3,19},{4,20},{5,21},{6,22},{7,23},{8,24},{9,... | collective-permute-start | bytes 147464 | tf_op jit(solution)/shard_map/ppermute | solution.py:301
  43.5 4.2 %collective-permute-start.9 = (f32[16,768]{1,0:T(8,128)S(1)}, f32[16,768]{1,0:T(8,128)S(1)}, u32[]{:S(2)}, u32[]{:S(2)}) collective-permute-start(f32[16,768]{1,0:T(8,128)S(1)} %add.7.refs_0_.refs_1_), channel_id=1, source_target_pairs={{0,1},{1,0},{2,3},{3,2},{4,5},{5,4},{6,7},{7,6},{8,9},{9,8},{10,11... | collective-permute-start | bytes 147464 | tf_op jit(solution)/shard_map/ppermute | solution.py:301
  44.1 7.8 %collective-permute-start.14 = (bf16[64,768]{1,0:T(8,128)(2,1)S(1)}, bf16[64,768]{1,0:T(8,128)(2,1)S(1)}, u32[]{:S(2)}, u32[]{:S(2)}) collective-permute-start(bf16[64,768]{1,0:T(8,128)(2,1)S(1)} %join.12), channel_id=1, source_target_pairs={{0,1},{1,0},{2,3},{3,2},{4,5},{5,4},{6,7},{7,6},{8,9},{9,8},{10,11... | collective-permute-start | bytes 294920 | tf_op jit(solution)/shard_map/ppermute | solution.py:301
  45.7 6.2 %collective-permute-start.15 = (bf16[64,768]{1,0:T(8,128)(2,1)S(1)}, bf16[64,768]{1,0:T(8,128)(2,1)S(1)}, u32[]{:S(2)}, u32[]{:S(2)}) collective-permute-start(bf16[64,768]{1,0:T(8,128)(2,1)S(1)} %join.13), channel_id=1, source_target_pairs={{0,4},{1,5},{2,6},{3,7},{4,0},{5,1},{6,2},{7,3},{8,12},{9,13},{10,... | collective-permute-start | bytes 294920 | tf_op jit(solution)/shard_map/ppermute | solution.py:301
  47.8 4.2 %collective-permute-start.11 = (f32[16,768]{1,0:T(8,128)S(1)}, f32[16,768]{1,0:T(8,128)S(1)}, u32[]{:S(2)}, u32[]{:S(2)}) collective-permute-start(f32[16,768]{1,0:T(8,128)S(1)} %add.8.refs_0_), channel_id=1, source_target_pairs={{0,4},{1,5},{2,6},{3,7},{4,0},{5,1},{6,2},{7,3},{8,12},{9,13},{10,... | collective-permute-start | bytes 147464 | tf_op jit(solution)/shard_map/ppermute | solution.py:301
  57.6 2.9 %collective-permute-start.16 = (bf16[784,768]{1,0:T(8,128)(2,1)S(1)}, bf16[784,768]{1,0:T(8,128)(2,1)S(1)}, u32[]{:S(2)}, u32[]{:S(2)}) collective-permute-start(bf16[784,768]{1,0:T(8,128)(2,1)S(1)} %get-tuple-element.50.mine_ref), channel_id=1, source_target_pairs={{0,2},{1,3},{2,0},{3,1},{4,6},{5,7},{6,4},{7,5},{8,10},{9,11},{10,... | collective-permute-start | bytes 3612680 | tf_op jit(solution)/shard_map/ppermute | solution.py:301

commit v3 on v2

--- a/solution.py
+++ b/solution.py
@@ -18,20 +18,21 @@
 f32, bf16 = jnp.float32, jnp.bfloat16
 
 
-def encode_rows(tok, gains, weight):
+def enter(tok, gains):
     values = tok.astype(f32)
     center = values - jnp.mean(values, axis=-1, keepdims=True)
     inverse = lax.rsqrt(jnp.mean(center * center, axis=-1, keepdims=True) + epsilon)
     act = (center * inverse * gains[0:1]).astype(bf16)
-    pre = jnp.dot(act, weight, preferred_element_type=f32)
+    return act, jnp.sum(act.astype(f32), axis=0, keepdims=True)
+
+
+def bend(tok, pre):
     scale = math.sqrt(2.0 / math.pi)
     square = pre * pre
-    bend = jnp.tanh(pre * (scale + (scale * 0.044715) * square))
-    half = 0.5 * pre
-    bent = half * bend
-    tilt = 0.5 * bend + (half - bent * bend) * (scale + (3.0 * scale * 0.044715) * square)
-    total = jnp.sum(values + (half + bent), axis=0, keepdims=True)
-    return act, tilt, total, jnp.sum(act.astype(f32), axis=0, keepdims=True)
+    half = 0.5 * jnp.tanh(pre * (scale + (scale * 0.044715) * square))
+    gelu = pre * (0.5 + half)
+    tilt = half + gelu * (0.5 - half) * (2.0 * scale + (6.0 * scale * 0.044715) * square)
+    return tilt, jnp.sum(tok.astype(f32) + gelu, axis=0, keepdims=True)
 
 
 def norm_row(pooled):
@@ -49,22 +50,29 @@
 
 
 def encode_into(layout, toks, gains, weight, act_ref, tilt_ref, row_ref):
-    at = 0
-    for d, doc in enumerate(layout):
-        seq = sum(rows for _, _, rows in doc)
-        total, acts = 0.0, 0.0
+    seq = sum(rows for _, _, rows in layout[0])
+    span = seq // 2
+    halves = []
+    for doc in layout:
         for operand, first, rows in doc:
-            for start in range(0, rows, seq // 2):
-                span = min(seq // 2, rows)
-                tok = toks[operand][first + start : first + start + span, :]
-                act, tilt, part, sums = encode_rows(tok, gains, weight)
-                act_ref[at : at + span, :] = act
-                tilt_ref[at : at + span, :] = tilt
-                total, acts, at = total + part, acts + sums, at + span
-        normed, inverse = norm_row(total * (1.0 / seq))
+            halves += [(operand, first + start) for start in range(0, rows, span)]
+    acts = []
+    for k, (operand, first) in enumerate(halves):
+        act, sums = enter(toks[operand][first : first + span, :], gains)
+        act_ref[k * span : (k + 1) * span, :] = act
+        acts.append(sums)
+    totals = []
+    for k, (operand, first) in enumerate(halves):
+        if k % 2 == 0:
+            pre = jnp.dot(act_ref[k * span : (k + 2) * span, :], weight, preferred_element_type=f32)
+        tilt, sums = bend(toks[operand][first : first + span, :], pre[k % 2 * span : (k % 2 + 1) * span])
+        tilt_ref[k * span : (k + 1) * span, :] = tilt
+        totals.append(sums)
+    for d in range(len(layout)):
+        normed, inverse = norm_row((totals[2 * d] + totals[2 * d + 1]) * (1.0 / seq))
         row_ref[d, 0:1, :] = normed
         row_ref[d, 1:2, :] = jnp.broadcast_to(inverse, normed.shape)
-        row_ref[d, 2:3, :] = acts
+        row_ref[d, 2:3, :] = acts[2 * d] + acts[2 * d + 1]
     return normed
 
 

time: 62.9 us -> 62 us (0.986)
  Pallas kernels: 18.6 us -> 17 us
  waiting for transfers between devices: 5.59 us -> 6.72 us
    pallas_call x5, Pallas kernels: 9.42 us -> 7.97 us  [encode_call(): pl.pallas_call(functools.partial(encode_kernel, layout), out_shape=encode...]
    ppermute x17, waiting for transfers between devices: 5.59 us -> 6.72 us  [swap(): return lax.ppermute(value, AXES, [(i, i ^ mask) for i in range(count)])]
  transfers between devices with their start and end apart: 17 -> 17, of which waited for: 4 -> 7; matrix products, arithmetic and copies ran while one was open for 0% -> 0% of each run, Pallas kernels for 17% -> 15%
where the time goes in v3:
time: 62 us; the launch traced here: 61.8 us
  starting transfers between devices  23.5 us (38%)
  Pallas kernels  17 us (27%)
  blocking collectives  10.2 us (16%)
  waiting for transfers between devices  6.72 us (11%)
  local copies, waits for them, and re-layouts  3.56 us (6%)
  between operations  0.78 us (1%)
    ppermute x17, starting transfers between devices, swap(): return lax.ppermute(value, AXES, [(i, i ^ mask) for i in range(count)])  23.5 us
    all_to_all x1, blocking collectives, gathered(): lax.all_to_all(copies, AXES, split_axis=0, concat_axis=0, tiled=True, axi...  10.2 us
    pallas_call x5, Pallas kernels, encode_call(): pl.pallas_call(functools.partial(encode_kernel, layout), out_shape=encode...  7.97 us
    ppermute x17, waiting for transfers between devices, swap(): return lax.ppermute(value, AXES, [(i, i ^ mask) for i in range(count)])  6.72 us
    pallas_call x1, Pallas kernels, gathered(): pl.pallas_call(functools.partial(back_kernel, seq, masks), out_shape=[jax...  4.77 us
    unnamed x16, local copies, waits for them, and re-layouts  3.56 us
    pallas_call x1, Pallas kernels, final_call(): pl.pallas_call(functools.partial(final_kernel, steps), out_shape=[jax.Sha...  2.09 us
    pallas_call x1, Pallas kernels, first_call(): pl.pallas_call(first_kernel, out_shape=encode_shapes(seq, 1, width) + [ja...  1.29 us
  transfers between devices with their start and end apart: 17, of which 7 were waited for; matrix products, arithmetic and copies ran while one was open for 0% of the time, Pallas kernels for 15%

profile of v3, /device:TPU:0, one launch (start us, length us, event | category | flops | bytes accessed | tf_op | source)
XLA Modules:
  0.0 61.8 jit_solution(4081818650607291436)
XLA Ops:
  0.6 4.1 %collective-permute-start.2 = (bf16[128,768]{1,0:T(8,128)(2,1)}, bf16[128,768]{1,0:T(8,128)(2,1)S(1)}, u32[]{:S(2)}, u32[]{:S(2)}) collective-permute-start(bf16[128,768]{1,0:T(8,128)(2,1)} %bitcast.1), channel_id=1, source_target_pairs={{0,16},{1,17},{2,18},{3,19},{4,20},{5,21},{6,22},{7,23},{8,24},{9,... | collective-permute-start | bytes 589832 | tf_op jit(solution)/shard_map/ppermute | solution.py:309
  4.7 1.5 %collective-permute-start.5 = (bf16[128,768]{1,0:T(8,128)(2,1)}, bf16[128,768]{1,0:T(8,128)(2,1)S(1)}, u32[]{:S(2)}, u32[]{:S(2)}) collective-permute-start(bf16[128,768]{1,0:T(8,128)(2,1)} %bitcast.2), channel_id=1, source_target_pairs={{0,4},{1,5},{2,6},{3,7},{4,0},{5,1},{6,2},{7,3},{8,12},{9,13},{10,... | collective-permute-start | bytes 589832 | tf_op jit(solution)/shard_map/ppermute | solution.py:309
  6.2 1.6 %collective-permute-start.3 = (bf16[128,768]{1,0:T(8,128)(2,1)}, bf16[128,768]{1,0:T(8,128)(2,1)S(1)}, u32[]{:S(2)}, u32[]{:S(2)}) collective-permute-start(bf16[128,768]{1,0:T(8,128)(2,1)} %bitcast.3), channel_id=1, source_target_pairs={{0,8},{1,9},{2,10},{3,11},{4,12},{5,13},{6,14},{7,15},{8,0},{9,1},... | collective-permute-start | bytes 589832 | tf_op jit(solution)/shard_map/ppermute | solution.py:309
  7.8 1.5 %collective-permute-start.4 = (bf16[128,768]{1,0:T(8,128)(2,1)}, bf16[128,768]{1,0:T(8,128)(2,1)S(1)}, u32[]{:S(2)}, u32[]{:S(2)}) collective-permute-start(bf16[128,768]{1,0:T(8,128)(2,1)} %bitcast.4), channel_id=1, source_target_pairs={{0,1},{1,0},{2,3},{3,2},{4,5},{5,4},{6,7},{7,6},{8,9},{9,8},{10,11... | collective-permute-start | bytes 589832 | tf_op jit(solution)/shard_map/ppermute | solution.py:309
  9.3 1.3 %copy-done = bf16[768,768]{1,0:T(8,128)(2,1)S(1)} copy-done((bf16[768,768]{1,0:T(8,128)(2,1)S(1)}, bf16[768,768]{1,0:T(8,128)(2,1)}, u32[]{:S(2)}) %copy-start) | copy-done | bytes 1179672
  10.6 0.7 %copy-done.3 = f32[2,768]{1,0:T(2,128)S(1)} copy-done((f32[2,768]{1,0:T(2,128)S(1)}, f32[2,768]{1,0:T(2,128)}, u32[]{:S(2)}) %copy-start.3) | copy-done | bytes 6168
  11.3 0.9 %copy-done.5 = bf16[1,128,768]{2,1,0:T(8,128)(2,1)S(1)} copy-done((bf16[1,128,768]{2,1,0:T(8,128)(2,1)S(1)}, bf16[1,128,768]{2,1,0:T(8,128)(2,1)}, u32[]{:S(2)}) %copy-start.5) | copy-done | bytes 196632
  12.2 0.7 %copy-done.7 = s32[1,8]{1,0:T(1,128)S(1)} copy-done((s32[1,8]{1,0:T(1,128)S(1)}, s32[1,8]{1,0:T(1,128)}, u32[]{:S(2)}) %copy-start.7) | copy-done | bytes 56
  12.9 1.3 %first.1 = (bf16[128,768]{1,0:T(8,128)(2,1)S(1)}, f32[128,768]{1,0:T(8,128)S(1)}, f32[1,8,768]{2,1,0:T(8,128)S(1)}, bf16[32,8,128]{2,1,0:T(8,128)(2,1)S(1)}) custom-call(bf16[128,768]{1,0:T(8,128)(2,1)S(1)} %bitcast.5, f32[2,768]{1,0:T(2,128)S(1)} %copy-done.3, bf16[768,768]{1,0:T(8,128)(2,1)S(1)} %copy-done, s32[1,8]{1,0:T(1,128)S(1)} %copy-done.7), custom_call_target="tpu_custom_call" | custom-call | tf_op jit(solution)/shard_map/first/pallas_call | solution.py:120
  14.2 1.4 %collective-permute-done.3.refs_1_.refs_0_ = bf16[128,768]{1,0:T(8,128)(2,1)S(1)} collective-permute-done((bf16[128,768]{1,0:T(8,128)(2,1)}, bf16[128,768]{1,0:T(8,128)(2,1)S(1)}, u32[]{:S(2)}, u32[]{:S(2)}) %collective-permute-start.3) | collective-permute-done | bytes 196640 | tf_op jit(solution)/shard_map/ppermute | solution.py:309
  15.6 1.6 %collective-permute-start.7 = (bf16[320,768]{1,0:T(8,128)(2,1)S(1)}, bf16[320,768]{1,0:T(8,128)(2,1)S(1)}, u32[]{:S(2)}, u32[]{:S(2)}) collective-permute-start(bf16[320,768]{1,0:T(8,128)(2,1)S(1)} %join.7), channel_id=1, source_target_pairs={{0,1},{1,0},{2,3},{3,2},{4,5},{5,4},{6,7},{7,6},{8,9},{9,8},{10,11... | collective-permute-start | bytes 1474568 | tf_op jit(solution)/shard_map/ppermute | solution.py:309
  17.9 1.2 %collective-permute-start.10 = (bf16[128,768]{1,0:T(8,128)(2,1)S(1)}, bf16[128,768]{1,0:T(8,128)(2,1)S(1)}, u32[]{:S(2)}, u32[]{:S(2)}) collective-permute-start(bf16[128,768]{1,0:T(8,128)(2,1)S(1)} %join.9), channel_id=1, source_target_pairs={{0,8},{1,9},{2,10},{3,11},{4,12},{5,13},{6,14},{7,15},{8,0},{9,1},... | collective-permute-start | bytes 589832 | tf_op jit(solution)/shard_map/ppermute | solution.py:309
  19.1 10.2 %all_to_all.5.rows_ref = bf16[32,8,128]{2,1,0:T(8,128)(2,1)S(1)} all-to-all(bf16[32,8,128]{2,1,0:T(8,128)(2,1)S(1)} %get-tuple-element.28), channel_id=1, replica_groups={{0,1,4,5,8,9,12,13,16,17,20,21,24,25,28,29,2,3,6,7,10,11,14,15,18,19,22..., dimensions={0} | all-to-all | bytes 131072 | tf_op jit(solution)/shard_map/all_to_all | solution.py:379
  29.4 0.7 %head.1 = (f32[16,768]{1,0:T(8,128)S(1)}, f32[16,768]{1,0:T(8,128)S(1)}) custom-call(bf16[32,8,128]{2,1,0:T(8,128)(2,1)S(1)} %all_to_all.5.rows_ref, bf16[512,768]{1,0:T(8,128)(2,1)S(1)} %copy-done.2, bf16[512]{0:T(512)(128)(2,1)S(1)} %copy-done.6), custom_call_target="tpu_custom_call" | custom-call | tf_op jit(solution)/shard_map/head/pallas_call | solution.py:392
  30.2 1.2 %collective-permute-done.refs_1_ = f32[16,768]{1,0:T(8,128)S(1)} collective-permute-done((f32[16,768]{1,0:T(8,128)S(1)}, f32[16,768]{1,0:T(8,128)S(1)}, u32[]{:S(2)}, u32[]{:S(2)}) %collective-permute-start) | collective-permute-done | bytes 49184 | tf_op jit(solution)/shard_map/ppermute | solution.py:309
  31.5 0.9 %collective-permute-start.13 = (bf16[256,768]{1,0:T(8,128)(2,1)S(1)}, bf16[256,768]{1,0:T(8,128)(2,1)S(1)}, u32[]{:S(2)}, u32[]{:S(2)}) collective-permute-start(bf16[256,768]{1,0:T(8,128)(2,1)S(1)} %join.11), channel_id=1, source_target_pairs={{0,4},{1,5},{2,6},{3,7},{4,0},{5,1},{6,2},{7,3},{8,12},{9,13},{10,... | collective-permute-start | bytes 1179656 | tf_op jit(solution)/shard_map/ppermute | solution.py:309
  32.4 1.2 %collective-permute-start.12 = (bf16[256,768]{1,0:T(8,128)(2,1)S(1)}, bf16[256,768]{1,0:T(8,128)(2,1)S(1)}, u32[]{:S(2)}, u32[]{:S(2)}) collective-permute-start(bf16[256,768]{1,0:T(8,128)(2,1)S(1)} %join.10), channel_id=1, source_target_pairs={{0,1},{1,0},{2,3},{3,2},{4,5},{5,4},{6,7},{7,6},{8,9},{9,8},{10,11... | collective-permute-start | bytes 1179656 | tf_op jit(solution)/shard_map/ppermute | solution.py:309
  33.6 1.8 %collective-permute-start.1 = (f32[16,768]{1,0:T(8,128)S(1)}, f32[16,768]{1,0:T(8,128)S(1)}, u32[]{:S(2)}, u32[]{:S(2)}) collective-permute-start(f32[16,768]{1,0:T(8,128)S(1)} %add.5.refs_0_.refs_2_), channel_id=1, source_target_pairs={{0,8},{1,9},{2,10},{3,11},{4,12},{5,13},{6,14},{7,15},{8,0},{9,1},... | collective-permute-start | bytes 147464 | tf_op jit(solution)/shard_map/ppermute | solution.py:309
  35.4 2.0 %encode.5 = (bf16[512,768]{1,0:T(8,128)(2,1)S(1)}, f32[512,768]{1,0:T(8,128)S(1)}, f32[4,8,768]{2,1,0:T(8,128)S(1)}) custom-call(bf16[128,768]{1,0:T(8,128)(2,1)S(1)} %collective-permute-done.2.refs_0_.refs_1_, bf16[128,768]{1,0:T(8,128)(2,1)S(1)} %collective-permute-done.3.refs_1_.refs_0_, bf16[128,768]{1,0:T(8,128)(2,1)S(1)} %collective-permute-done.4.refs_2_, ...), custom_call_target="tpu_custom_call" | custom-call | tf_op jit(solution)/shard_map/encode/pallas_call | solution.py:133
  37.7 3.1 %collective-permute-start.6 = (f32[16,768]{1,0:T(8,128)S(1)}, f32[16,768]{1,0:T(8,128)S(1)}, u32[]{:S(2)}, u32[]{:S(2)}) collective-permute-start(f32[16,768]{1,0:T(8,128)S(1)} %add.6.refs_0_), channel_id=1, source_target_pairs={{0,16},{1,17},{2,18},{3,19},{4,20},{5,21},{6,22},{7,23},{8,24},{9,... | collective-permute-start | bytes 147464 | tf_op jit(solution)/shard_map/ppermute | solution.py:309
  40.8 2.0 %encode.6 = (bf16[512,768]{1,0:T(8,128)(2,1)S(1)}, f32[512,768]{1,0:T(8,128)S(1)}, f32[4,8,768]{2,1,0:T(8,128)S(1)}) custom-call(bf16[320,768]{1,0:T(8,128)(2,1)S(1)} %collective-permute-done.7.refs_0_.refs_1_, bf16[320,768]{1,0:T(8,128)(2,1)S(1)} %collective-permute-done.8.refs_1_.refs_0_, f32[2,768]{1,0:T(2,128)S(1)} %copy-done.4, ...), custom_call_target="tpu_custom_call" | custom-call | tf_op jit(solution)/shard_map/encode/pallas_call | solution.py:133
  42.9 0.8 %collective-permute-start.9 = (f32[16,768]{1,0:T(8,128)S(1)}, f32[16,768]{1,0:T(8,128)S(1)}, u32[]{:S(2)}, u32[]{:S(2)}) collective-permute-start(f32[16,768]{1,0:T(8,128)S(1)} %add.7.refs_0_.refs_1_), channel_id=1, source_target_pairs={{0,1},{1,0},{2,3},{3,2},{4,5},{5,4},{6,7},{7,6},{8,9},{9,8},{10,11... | collective-permute-start | bytes 147464 | tf_op jit(solution)/shard_map/ppermute | solution.py:309
  43.7 1.4 %collective-permute-start.14 = (bf16[64,768]{1,0:T(8,128)(2,1)S(1)}, bf16[64,768]{1,0:T(8,128)(2,1)S(1)}, u32[]{:S(2)}, u32[]{:S(2)}) collective-permute-start(bf16[64,768]{1,0:T(8,128)(2,1)S(1)} %join.12), channel_id=1, source_target_pairs={{0,1},{1,0},{2,3},{3,2},{4,5},{5,4},{6,7},{7,6},{8,9},{9,8},{10,11... | collective-permute-start | bytes 294920 | tf_op jit(solution)/shard_map/ppermute | solution.py:309
  45.1 0.7 %collective-permute-start.15 = (bf16[64,768]{1,0:T(8,128)(2,1)S(1)}, bf16[64,768]{1,0:T(8,128)(2,1)S(1)}, u32[]{:S(2)}, u32[]{:S(2)}) collective-permute-start(bf16[64,768]{1,0:T(8,128)(2,1)S(1)} %join.13), channel_id=1, source_target_pairs={{0,4},{1,5},{2,6},{3,7},{4,0},{5,1},{6,2},{7,3},{8,12},{9,13},{10,... | collective-permute-start | bytes 294920 | tf_op jit(solution)/shard_map/ppermute | solution.py:309
  45.8 1.1 %encode.7 = (bf16[256,768]{1,0:T(8,128)(2,1)S(1)}, f32[256,768]{1,0:T(8,128)S(1)}, f32[2,8,768]{2,1,0:T(8,128)S(1)}) custom-call(bf16[320,768]{1,0:T(8,128)(2,1)S(1)} %collective-permute-done.8.refs_1_.refs_0_, bf16[128,768]{1,0:T(8,128)(2,1)S(1)} %collective-permute-done.10.refs_1_.refs_0_, f32[2,768]{1,0:T(2,128)S(1)} %copy-done.4, ...), custom_call_target="tpu_custom_call" | custom-call | tf_op jit(solution)/shard_map/encode/pallas_call | solution.py:133
  47.1 1.3 %collective-permute-start.11 = (f32[16,768]{1,0:T(8,128)S(1)}, f32[16,768]{1,0:T(8,128)S(1)}, u32[]{:S(2)}, u32[]{:S(2)}) collective-permute-start(f32[16,768]{1,0:T(8,128)S(1)} %add.8.refs_0_), channel_id=1, source_target_pairs={{0,4},{1,5},{2,6},{3,7},{4,0},{5,1},{6,2},{7,3},{8,12},{9,13},{10,... | collective-permute-start | bytes 147464 | tf_op jit(solution)/shard_map/ppermute | solution.py:309
  48.4 2.0 %encode.8 = (bf16[512,768]{1,0:T(8,128)(2,1)S(1)}, f32[512,768]{1,0:T(8,128)S(1)}, f32[4,8,768]{2,1,0:T(8,128)S(1)}) custom-call(bf16[256,768]{1,0:T(8,128)(2,1)S(1)} %collective-permute-done.12.refs_0_, bf16[256,768]{1,0:T(8,128)(2,1)S(1)} %collective-permute-done.13.refs_1_.refs_0_, f32[2,768]{1,0:T(2,128)S(1)} %copy-done.4, bf16[768,768]{1,0:T(8,128)(2,1)S(1)} %copy-done.1), custom_call_target="tpu_custom_call" | custom-call | tf_op jit(solution)/shard_map/encode/pallas_call | solution.py:133
  50.4 0.8 %collective-permute-done.11.refs_1_ = f32[16,768]{1,0:T(8,128)S(1)} collective-permute-done((f32[16,768]{1,0:T(8,128)S(1)}, f32[16,768]{1,0:T(8,128)S(1)}, u32[]{:S(2)}, u32[]{:S(2)}) %collective-permute-start.11) | collective-permute-done | bytes 49184 | tf_op jit(solution)/shard_map/ppermute | solution.py:309
  51.3 0.8 %encode.9 = (bf16[128,768]{1,0:T(8,128)(2,1)S(1)}, f32[128,768]{1,0:T(8,128)S(1)}, f32[1,8,768]{2,1,0:T(8,128)S(1)}) custom-call(bf16[64,768]{1,0:T(8,128)(2,1)S(1)} %collective-permute-done.14.refs_0_, bf16[64,768]{1,0:T(8,128)(2,1)S(1)} %collective-permute-done.15.refs_1_, f32[2,768]{1,0:T(2,128)S(1)} %copy-done.4, bf16[768,768]{1,0:T(8,128)(2,1)S(1)} %copy-done.1), custom_call_target="tpu_custom_call" | custom-call | tf_op jit(solution)/shard_map/encode/pallas_call | solution.py:133
  52.0 4.8 %back.1 = (bf16[784,768]{1,0:T(8,128)(2,1)S(1)}, f32[1,768]{1,0:T(1,128)}) custom-call(f32[16,768]{1,0:T(8,128)S(1)} %add.9.refs_0_, f32[2,768]{1,0:T(2,128)S(1)} %copy-done.4, bf16[768,768]{1,0:T(8,128)(2,1)S(1)} %copy-done.1, bf16[128,768]{1,0:T(8,128)(2,1)S(1)} %get-tuple-element.36.refs_3_, f32[128,768]{1,0:T(8,128)S(1)} %get-tuple-element.37.refs_4_, ...), custom_call_target="tpu_custom_call" | custom-call | tf_op jit(solution)/shard_map/back/pallas_call | solution.py:417
  56.8 2.9 %collective-permute-done.16.other_ref = bf16[784,768]{1,0:T(8,128)(2,1)S(1)} collective-permute-done((bf16[784,768]{1,0:T(8,128)(2,1)S(1)}, bf16[784,768]{1,0:T(8,128)(2,1)S(1)}, u32[]{:S(2)}, u32[]{:S(2)}) %collective-permute-start.16) | collective-permute-done | bytes 1204256 | tf_op jit(solution)/shard_map/ppermute | solution.py:309
  59.7 2.1 %final.1 = (f32[768,768]{1,0:T(8,128)}, f32[2,768]{1,0:T(2,128)}) custom-call(bf16[784,768]{1,0:T(8,128)(2,1)S(1)} %get-tuple-element.50.mine_ref, bf16[784,768]{1,0:T(8,128)(2,1)S(1)} %collective-permute-done.16.other_ref), custom_call_target="tpu_custom_call" | custom-call | tf_op jit(solution)/shard_map/final/pallas_call | solution.py:297
  (41 shorter events, 1.4 us)
Async XLA Ops:
  0.6 13.6 %collective-permute-start.2 = (bf16[128,768]{1,0:T(8,128)(2,1)}, bf16[128,768]{1,0:T(8,128)(2,1)S(1)}, u32[]{:S(2)}, u32[]{:S(2)}) collective-permute-start(bf16[128,768]{1,0:T(8,128)(2,1)} %bitcast.1), channel_id=1, source_target_pairs={{0,16},{1,17},{2,18},{3,19},{4,20},{5,21},{6,22},{7,23},{8,24},{9,... | collective-permute-start | bytes 589832 | tf_op jit(solution)/shard_map/ppermute | solution.py:309
  4.7 9.5 %collective-permute-start.5 = (bf16[128,768]{1,0:T(8,128)(2,1)}, bf16[128,768]{1,0:T(8,128)(2,1)S(1)}, u32[]{:S(2)}, u32[]{:S(2)}) collective-permute-start(bf16[128,768]{1,0:T(8,128)(2,1)} %bitcast.2), channel_id=1, source_target_pairs={{0,4},{1,5},{2,6},{3,7},{4,0},{5,1},{6,2},{7,3},{8,12},{9,13},{10,... | collective-permute-start | bytes 589832 | tf_op jit(solution)/shard_map/ppermute | solution.py:309
  6.2 9.3 %collective-permute-start.3 = (bf16[128,768]{1,0:T(8,128)(2,1)}, bf16[128,768]{1,0:T(8,128)(2,1)S(1)}, u32[]{:S(2)}, u32[]{:S(2)}) collective-permute-start(bf16[128,768]{1,0:T(8,128)(2,1)} %bitcast.3), channel_id=1, source_target_pairs={{0,8},{1,9},{2,10},{3,11},{4,12},{5,13},{6,14},{7,15},{8,0},{9,1},... | collective-permute-start | bytes 589832 | tf_op jit(solution)/shard_map/ppermute | solution.py:309
  7.8 9.4 %collective-permute-start.4 = (bf16[128,768]{1,0:T(8,128)(2,1)}, bf16[128,768]{1,0:T(8,128)(2,1)S(1)}, u32[]{:S(2)}, u32[]{:S(2)}) collective-permute-start(bf16[128,768]{1,0:T(8,128)(2,1)} %bitcast.4), channel_id=1, source_target_pairs={{0,1},{1,0},{2,3},{3,2},{4,5},{5,4},{6,7},{7,6},{8,9},{9,8},{10,11... | collective-permute-start | bytes 589832 | tf_op jit(solution)/shard_map/ppermute | solution.py:309
  9.3 1.3 %copy-start = (bf16[768,768]{1,0:T(8,128)(2,1)S(1)}, bf16[768,768]{1,0:T(8,128)(2,1)}, u32[]{:S(2)}) copy-start(bf16[768,768]{1,0:T(8,128)(2,1)} %refs_2_.11) | copy-start | bytes 3538948
  10.6 0.7 %copy-start.3 = (f32[2,768]{1,0:T(2,128)S(1)}, f32[2,768]{1,0:T(2,128)}, u32[]{:S(2)}) copy-start(f32[2,768]{1,0:T(2,128)} %refs_1_.3) | copy-start | bytes 18436
  11.3 0.9 %copy-start.5 = (bf16[1,128,768]{2,1,0:T(8,128)(2,1)S(1)}, bf16[1,128,768]{2,1,0:T(8,128)(2,1)}, u32[]{:S(2)}) copy-start(bf16[1,128,768]{2,1,0:T(8,128)(2,1)} %param.6) | copy-start | bytes 589828
  12.2 0.7 %copy-start.7 = (s32[1,8]{1,0:T(1,128)S(1)}, s32[1,8]{1,0:T(1,128)}, u32[]{:S(2)}) copy-start(s32[1,8]{1,0:T(1,128)} %refs_3_.5) | copy-start | bytes 100
  14.2 15.2 %copy-start.2 = (bf16[512,768]{1,0:T(8,128)(2,1)S(1)}, bf16[512,768]{1,0:T(8,128)(2,1)}, u32[]{:S(2)}) copy-start(bf16[512,768]{1,0:T(8,128)(2,1)} %weight_ref.1) | copy-start | bytes 2359300
  14.2 15.2 %copy-start.6 = (bf16[512]{0:T(512)(128)(2,1)S(1)}, bf16[512]{0:T(512)(128)(2,1)}, u32[]{:S(2)}) copy-start(bf16[512]{0:T(512)(128)(2,1)} %bias_ref.1) | copy-start | bytes 3076
  15.6 15.8 %collective-permute-start.7 = (bf16[320,768]{1,0:T(8,128)(2,1)S(1)}, bf16[320,768]{1,0:T(8,128)(2,1)S(1)}, u32[]{:S(2)}, u32[]{:S(2)}) collective-permute-start(bf16[320,768]{1,0:T(8,128)(2,1)S(1)} %join.7), channel_id=1, source_target_pairs={{0,1},{1,0},{2,3},{3,2},{4,5},{5,4},{6,7},{7,6},{8,9},{9,8},{10,11... | collective-permute-start | bytes 1474568 | tf_op jit(solution)/shard_map/ppermute | solution.py:309
  17.3 15.1 %collective-permute-start.8 = (bf16[320,768]{1,0:T(8,128)(2,1)S(1)}, bf16[320,768]{1,0:T(8,128)(2,1)S(1)}, u32[]{:S(2)}, u32[]{:S(2)}) collective-permute-start(bf16[320,768]{1,0:T(8,128)(2,1)S(1)} %join.8), channel_id=1, source_target_pairs={{0,4},{1,5},{2,6},{3,7},{4,0},{5,1},{6,2},{7,3},{8,12},{9,13},{10,... | collective-permute-start | bytes 1474568 | tf_op jit(solution)/shard_map/ppermute | solution.py:309
  17.9 13.5 %collective-permute-start.10 = (bf16[128,768]{1,0:T(8,128)(2,1)S(1)}, bf16[128,768]{1,0:T(8,128)(2,1)S(1)}, u32[]{:S(2)}, u32[]{:S(2)}) collective-permute-start(bf16[128,768]{1,0:T(8,128)(2,1)S(1)} %join.9), channel_id=1, source_target_pairs={{0,8},{1,9},{2,10},{3,11},{4,12},{5,13},{6,14},{7,15},{8,0},{9,1},... | collective-permute-start | bytes 589832 | tf_op jit(solution)/shard_map/ppermute | solution.py:309
  29.4 6.0 %copy-start.1 = (bf16[768,768]{1,0:T(8,128)(2,1)S(1)}, bf16[768,768]{1,0:T(8,128)(2,1)}, u32[]{:S(2)}) copy-start(bf16[768,768]{1,0:T(8,128)(2,1)} %refs_2_.11) | copy-start | bytes 3538948
  29.4 6.0 %copy-start.4 = (f32[2,768]{1,0:T(2,128)S(1)}, f32[2,768]{1,0:T(2,128)}, u32[]{:S(2)}) copy-start(f32[2,768]{1,0:T(2,128)} %refs_1_.3) | copy-start | bytes 18436
  30.1 1.3 %collective-permute-start = (f32[16,768]{1,0:T(8,128)S(1)}, f32[16,768]{1,0:T(8,128)S(1)}, u32[]{:S(2)}, u32[]{:S(2)}) collective-permute-start(f32[16,768]{1,0:T(8,128)S(1)} %get-tuple-element.30), channel_id=1, source_target_pairs={{0,2},{1,3},{2,0},{3,1},{4,6},{5,7},{6,4},{7,5},{8,10},{9,11},{10,... | collective-permute-start | bytes 147464 | tf_op jit(solution)/shard_map/ppermute | solution.py:309
  31.5 12.2 %collective-permute-start.13 = (bf16[256,768]{1,0:T(8,128)(2,1)S(1)}, bf16[256,768]{1,0:T(8,128)(2,1)S(1)}, u32[]{:S(2)}, u32[]{:S(2)}) collective-permute-start(bf16[256,768]{1,0:T(8,128)(2,1)S(1)} %join.11), channel_id=1, source_target_pairs={{0,4},{1,5},{2,6},{3,7},{4,0},{5,1},{6,2},{7,3},{8,12},{9,13},{10,... | collective-permute-start | bytes 1179656 | tf_op jit(solution)/shard_map/ppermute | solution.py:309
  32.4 12.7 %collective-permute-start.12 = (bf16[256,768]{1,0:T(8,128)(2,1)S(1)}, bf16[256,768]{1,0:T(8,128)(2,1)S(1)}, u32[]{:S(2)}, u32[]{:S(2)}) collective-permute-start(bf16[256,768]{1,0:T(8,128)(2,1)S(1)} %join.10), channel_id=1, source_target_pairs={{0,1},{1,0},{2,3},{3,2},{4,5},{5,4},{6,7},{7,6},{8,9},{9,8},{10,11... | collective-permute-start | bytes 1179656 | tf_op jit(solution)/shard_map/ppermute | solution.py:309
  33.6 4.1 %collective-permute-start.1 = (f32[16,768]{1,0:T(8,128)S(1)}, f32[16,768]{1,0:T(8,128)S(1)}, u32[]{:S(2)}, u32[]{:S(2)}) collective-permute-start(f32[16,768]{1,0:T(8,128)S(1)} %add.5.refs_0_.refs_2_), channel_id=1, source_target_pairs={{0,8},{1,9},{2,10},{3,11},{4,12},{5,13},{6,14},{7,15},{8,0},{9,1},... | collective-permute-start | bytes 147464 | tf_op jit(solution)/shard_map/ppermute | solution.py:309
  37.7 5.2 %collective-permute-start.6 = (f32[16,768]{1,0:T(8,128)S(1)}, f32[16,768]{1,0:T(8,128)S(1)}, u32[]{:S(2)}, u32[]{:S(2)}) collective-permute-start(f32[16,768]{1,0:T(8,128)S(1)} %add.6.refs_0_), channel_id=1, source_target_pairs={{0,16},{1,17},{2,18},{3,19},{4,20},{5,21},{6,22},{7,23},{8,24},{9,... | collective-permute-start | bytes 147464 | tf_op jit(solution)/shard_map/ppermute | solution.py:309
  42.9 4.1 %collective-permute-start.9 = (f32[16,768]{1,0:T(8,128)S(1)}, f32[16,768]{1,0:T(8,128)S(1)}, u32[]{:S(2)}, u32[]{:S(2)}) collective-permute-start(f32[16,768]{1,0:T(8,128)S(1)} %add.7.refs_0_.refs_1_), channel_id=1, source_target_pairs={{0,1},{1,0},{2,3},{3,2},{4,5},{5,4},{6,7},{7,6},{8,9},{9,8},{10,11... | collective-permute-start | bytes 147464 | tf_op jit(solution)/shard_map/ppermute | solution.py:309
  43.7 7.5 %collective-permute-start.14 = (bf16[64,768]{1,0:T(8,128)(2,1)S(1)}, bf16[64,768]{1,0:T(8,128)(2,1)S(1)}, u32[]{:S(2)}, u32[]{:S(2)}) collective-permute-start(bf16[64,768]{1,0:T(8,128)(2,1)S(1)} %join.12), channel_id=1, source_target_pairs={{0,1},{1,0},{2,3},{3,2},{4,5},{5,4},{6,7},{7,6},{8,9},{9,8},{10,11... | collective-permute-start | bytes 294920 | tf_op jit(solution)/shard_map/ppermute | solution.py:309
  45.1 6.1 %collective-permute-start.15 = (bf16[64,768]{1,0:T(8,128)(2,1)S(1)}, bf16[64,768]{1,0:T(8,128)(2,1)S(1)}, u32[]{:S(2)}, u32[]{:S(2)}) collective-permute-start(bf16[64,768]{1,0:T(8,128)(2,1)S(1)} %join.13), channel_id=1, source_target_pairs={{0,4},{1,5},{2,6},{3,7},{4,0},{5,1},{6,2},{7,3},{8,12},{9,13},{10,... | collective-permute-start | bytes 294920 | tf_op jit(solution)/shard_map/ppermute | solution.py:309
  47.1 4.2 %collective-permute-start.11 = (f32[16,768]{1,0:T(8,128)S(1)}, f32[16,768]{1,0:T(8,128)S(1)}, u32[]{:S(2)}, u32[]{:S(2)}) collective-permute-start(f32[16,768]{1,0:T(8,128)S(1)} %add.8.refs_0_), channel_id=1, source_target_pairs={{0,4},{1,5},{2,6},{3,7},{4,0},{5,1},{6,2},{7,3},{8,12},{9,13},{10,... | collective-permute-start | bytes 147464 | tf_op jit(solution)/shard_map/ppermute | solution.py:309
  56.8 2.9 %collective-permute-start.16 = (bf16[784,768]{1,0:T(8,128)(2,1)S(1)}, bf16[784,768]{1,0:T(8,128)(2,1)S(1)}, u32[]{:S(2)}, u32[]{:S(2)}) collective-permute-start(bf16[784,768]{1,0:T(8,128)(2,1)S(1)} %get-tuple-element.50.mine_ref), channel_id=1, source_target_pairs={{0,2},{1,3},{2,0},{3,1},{4,6},{5,7},{6,4},{7,5},{8,10},{9,11},{10,... | collective-permute-start | bytes 3612680 | tf_op jit(solution)/shard_map/ppermute | solution.py:309

commit v4 on v3

--- a/solution.py
+++ b/solution.py
@@ -221,14 +221,45 @@
     other_ref[...] = part[pl.ds(pl.multiple_of((1 - kind) * half, half), half), :]
 
 
+def share(first, acts, d_pre, factors, gains, weight_ref, out_ref, act):
+    half, width = act.shape[1], d_pre.shape[1]
+    columns = pl.ds(first, half)
+    base = 0
+    for ref in acts:
+        act[pl.ds(base, ref.shape[0]), :] = ref[:, columns]
+        base += ref.shape[0]
+    left, right = factors
+    even = lax.dot_general(left[:, columns], right[...], (((0,), (0,)), ((), ())), preferred_element_type=f32)
+    total = even + lax.dot_general(act[...], d_pre[...], (((0,), (0,)), ((), ())), preferred_element_type=f32)
+    out_ref[:half, :] = total.astype(bf16)
+    weighed = total * weight_ref[columns, :].astype(f32)
+    lanes = weighed[:, :128]
+    for k in range(1, width // 128):
+        lanes = lanes + weighed[:, k * 128 : (k + 1) * 128]
+    gain_in = jnp.sum(lanes.T, axis=0, keepdims=True) / gains[:, columns]
+    none = jnp.zeros((1, width - half), f32)
+    return jnp.concatenate([none, gain_in] if first else [gain_in, none], axis=1)
+
+
+def terms(values):
+    parts = []
+    for rest in values:
+        for _ in range(3):
+            parts.append(rest.astype(bf16).astype(f32))
+            rest = rest - parts[-1]
+    return jnp.concatenate(parts + [jnp.zeros((16 - len(parts), rest.shape[1]), f32)], axis=0).astype(bf16)
+
+
 def back_kernel(seq, masks, *refs):
     grad_ref, gains_ref, weight_ref = refs[:3]
     groups = [refs[3 + 3 * g : 6 + 3 * g] for g in range(len(masks))]
-    out_ref, own_ref, act, d_pre, saved, spreads = refs[3 + 3 * len(masks) :]
+    out_ref, own_ref, d_pre, left, right, act, saved, spreads, own, sem = refs[3 + 3 * len(masks) :]
     me, core = number(), lax.axis_size("doc")
     places = [[place(me ^ m, core) for m in group] for group in masks]
-    own_ref[...] = grad_ref[pl.ds(place(me, core), 1), :]
-    width = gains_ref.shape[1]
+    own[...] = grad_ref[pl.ds(place(me, core), 1), :]
+    copy = pltpu.make_async_copy(own, own_ref, sem)
+    copy.start()
+    half = weight_ref.shape[0] // 2
     for (_, _, row_ref), group in zip(groups, places, strict=True):
         for d, at in enumerate(group):
             saved[at] = row_ref[d]
@@ -244,65 +275,107 @@
         * (1.0 / seq)
     )
     spreads[...] = spread
-    for (act_ref, tilt_ref, _), group in zip(groups, places, strict=True):
+    even = 0.5 * spread
+    sums_top, even_top = sums.astype(bf16), even.astype(bf16)
+    sums_low = (sums - sums_top.astype(f32)).astype(bf16)
+    even_low = (even - even_top.astype(f32)).astype(bf16)
+    left[...] = jnp.concatenate([sums_top, sums_top, sums_low], axis=0)
+    right[...] = jnp.concatenate([even_top, even_low, even_top], axis=0)
+    base = 0
+    for (_, tilt_ref, _), group in zip(groups, places, strict=True):
         for d, at in enumerate(group):
-            to = pl.ds(pl.multiple_of(at * seq, seq), seq)
-            act[to, :] = act_ref[d * seq : (d + 1) * seq, :]
-            d_pre[to, :] = (tilt_ref[d * seq : (d + 1) * seq, :] * spreads[pl.ds(at, 1), :]).astype(bf16)
-    even = 0.5 * spread
-    sums_top, half_top = sums.astype(bf16), even.astype(bf16)
-    sums_low = (sums - sums_top.astype(f32)).astype(bf16)
-    half_low = (even - half_top.astype(f32)).astype(bf16)
-    even = lax.dot_general(
-        jnp.concatenate([sums_top, sums_top, sums_low], axis=0),
-        jnp.concatenate([half_top, half_low, half_top], axis=0),
-        (((0,), (0,)), ((), ())),
-        preferred_element_type=f32,
-    )
-    total = even + lax.dot_general(act[...], d_pre[...], (((0,), (0,)), ((), ())), preferred_element_type=f32)
-    out_ref[:width, :] = total.astype(bf16)
-    weighed = total * weight_ref[...].astype(f32)
-    lanes = weighed[:, :128]
-    for k in range(1, width // 128):
-        lanes = lanes + weighed[:, k * 128 : (k + 1) * 128]
-    gain_in = jnp.sum(lanes.T, axis=0, keepdims=True) / gains_ref[0:1, :]
-    gain_out = jnp.sum(row * normed, axis=0, keepdims=True)
-    rest, terms = jnp.concatenate([gain_in, gain_out], axis=0), []
-    for _ in range(3):
-        terms.append(rest.astype(bf16).astype(f32))
-        rest = rest - terms[-1]
-    terms.append(jnp.zeros((16 - 2 * len(terms), width), f32))
-    out_ref[width:, :] = jnp.concatenate(terms, axis=0).astype(bf16)
-
-
-def final_kernel(steps, mine_ref, other_ref, weight_ref, gains_ref, total, sems):
-    rows = weight_ref.shape[0]
+            d_pre[pl.ds(base, seq), :] = (tilt_ref[d * seq : (d + 1) * seq, :] * spreads[pl.ds(at, 1), :]).astype(bf16)
+            base += seq
+    acts = [act_ref for act_ref, _, _ in groups]
+    gain_in = share(0, acts, d_pre, (left, right), gains_ref[0:1, :], weight_ref, out_ref, act)
+    out_ref[half:, :] = terms([jnp.sum(row * normed, axis=0, keepdims=True), gain_in])
+    copy.wait()
+
+
+def more_kernel(*refs):
+    (gains_ref, weight_ref, d_pre, left, right), acts, (out_ref, act) = refs[:5], refs[5:-2], refs[-2:]
+    half = weight_ref.shape[0] // 2
+    gain_in = share(half, acts, d_pre, (left, right), gains_ref[0:1, :], weight_ref, out_ref, act)
+    out_ref[half:, :] = terms([jnp.zeros_like(gain_in), gain_in])
+
+
+def back_calls(seq, masks, total, gains, weight, groups):
+    width, docs = weight.shape[0], sum(len(group) for group in masks)
+    half = width // 2
+    share_shape = jax.ShapeDtypeStruct((half + 16, width), bf16)
+    act, vmem = pltpu.VMEM((docs * seq, half), bf16), pl.BlockSpec(memory_space=pltpu.VMEM)
+    top, row_grad, *middle = pl.pallas_call(
+        functools.partial(back_kernel, seq, masks),
+        out_shape=[
+            share_shape,
+            jax.ShapeDtypeStruct((1, width), f32),
+            jax.ShapeDtypeStruct((docs * seq, width), bf16),
+            jax.ShapeDtypeStruct((3 * docs, width), bf16),
+            jax.ShapeDtypeStruct((3 * docs, width), bf16),
+        ],
+        out_specs=[vmem, pl.BlockSpec(memory_space=pltpu.HBM), vmem, vmem, vmem],
+        scratch_shapes=[
+            act,
+            pltpu.VMEM((docs, 8, width), f32),
+            pltpu.VMEM((docs, width), f32),
+            pltpu.VMEM((1, width), f32),
+            pltpu.SemaphoreType.DMA,
+        ],
+        compiler_params=pltpu.CompilerParams(vmem_limit_bytes=32 << 20),
+        name="back",
+    )(total, gains, weight, *[array for group in groups for array in group])
+    low = pl.pallas_call(
+        more_kernel,
+        out_shape=share_shape,
+        scratch_shapes=[act],
+        compiler_params=pltpu.CompilerParams(vmem_limit_bytes=24 << 20),
+        name="more",
+    )(gains, weight, *middle, *[group[0] for group in groups])
+    return top, low, row_grad
+
+
+def final_kernel(first, *refs):
+    (mine_ref, other_ref), weight_ref, (total, gains, sems) = refs[:2], refs[-4 - (first > 0)], refs[-3:]
+    rows, steps = total.shape[0], sems.shape[0] - 1
     span = rows // steps
     copies = []
+    if first:
+        gain_in = gain_out = 0.0
+        for pair in (refs[:2], refs[2:4]):
+            mine, other = pair[0][rows:, :].astype(f32), pair[1][rows:, :].astype(f32)
+            gain_out += (mine[0:1] + mine[1:2] + mine[2:3]) + (other[0:1] + other[1:2] + other[2:3])
+            gain_in += (mine[3:4] + mine[4:5] + mine[5:6]) + (other[3:4] + other[4:5] + other[5:6])
+        gains[...] = jnp.concatenate([gain_in, gain_out], axis=0)
+        copies.append(pltpu.make_async_copy(gains, refs[-4], sems.at[steps]))
+        copies[-1].start()
     for k in range(steps):
         part = pl.ds(k * span, span)
         total[part, :] = mine_ref[part, :].astype(f32) + other_ref[part, :].astype(f32)
-        copies.append(pltpu.make_async_copy(total.at[part, :], weight_ref.at[part, :], sems.at[k]))
+        copies.append(pltpu.make_async_copy(total.at[part, :], weight_ref.at[pl.ds(first + k * span, span), :], sems.at[k]))
         copies[-1].start()
-    mine, other = mine_ref[rows:, :].astype(f32), other_ref[rows:, :].astype(f32)
-    gains_ref[...] = (mine[0:2] + mine[2:4] + mine[4:6]) + (other[0:2] + other[2:4] + other[4:6])
     for copy in copies:
         copy.wait()
 
 
-def final_call(mine, other):
-    width = mine.shape[1]
-    steps = 8 if width % 128 == 0 else 1
+def final_call(first, shares, before=None):
+    rows, width = shares[0].shape[0] - 16, shares[0].shape[1]
+    steps = 4 if rows % 64 == 0 else 1
     vmem, hbm = pl.BlockSpec(memory_space=pltpu.VMEM), pl.BlockSpec(memory_space=pltpu.HBM)
+    extra = [] if before is None else [before]
     return pl.pallas_call(
-        functools.partial(final_kernel, steps),
-        out_shape=[jax.ShapeDtypeStruct((width, width), f32), jax.ShapeDtypeStruct((2, width), f32)],
-        in_specs=[vmem] * 2,
-        out_specs=[hbm, vmem],
-        scratch_shapes=[pltpu.VMEM((width, width), f32), pltpu.SemaphoreType.DMA((steps,))],
+        functools.partial(final_kernel, first),
+        out_shape=[jax.ShapeDtypeStruct((2 * rows, width), f32)] + [jax.ShapeDtypeStruct((2, width), f32)] * len(extra),
+        in_specs=[vmem] * len(shares) + [hbm] * len(extra),
+        out_specs=[hbm] * (1 + len(extra)),
+        input_output_aliases={len(shares): 0} if extra else {},
+        scratch_shapes=[
+            pltpu.VMEM((rows, width), f32),
+            pltpu.VMEM((2, width), f32),
+            pltpu.SemaphoreType.DMA((steps + 1,)),
+        ],
         compiler_params=pltpu.CompilerParams(vmem_limit_bytes=12 << 20),
         name="final",
-    )(mine, other)
+    )(*shares, *extra)
 
 
 def swap(value, mask, count):
@@ -409,27 +482,13 @@
     rest = docs_1[4:]
     tied = [encode_held(rest)] if rest else []
     total = add([total, hop(total, x)], tied)
-    tied = encode_held(docs_2)
-    total = add([total, hop(total, y)], [tied])
-    encode_held(docs_3)
-
-    operands = [array for group in groups for array in group]
-    part, row_grad = pl.pallas_call(
-        functools.partial(back_kernel, seq, masks),
-        out_shape=[
-            jax.ShapeDtypeStruct((width + 16, width), bf16),
-            jax.ShapeDtypeStruct((1, width), f32),
-        ],
-        scratch_shapes=[
-            pltpu.VMEM((half * seq, width), bf16),
-            pltpu.VMEM((half * seq, width), bf16),
-            pltpu.VMEM((half, 8, width), f32),
-            pltpu.VMEM((half, width), f32),
-        ],
-        compiler_params=pltpu.CompilerParams(vmem_limit_bytes=32 << 20),
-        name="back",
-    )(total, norm_gains, enc_weight, *operands)
-    weight_grad, gain_grads = final_call(part, hop(part, core))
+    tied = [encode_held(docs_2), encode_held(docs_3)]
+    total = add([total, hop(total, y)], tied)
+
+    top, low, row_grad = back_calls(seq, masks, total, norm_gains, enc_weight, groups)
+    other_top, other_low = hop(top, core), hop(low, core)
+    (weight_grad,) = final_call(0, [top, other_top])
+    weight_grad, gain_grads = final_call(width // 2, [low, other_low, top, other_top], weight_grad)
     return row_grad, weight_grad, gain_grads
 
 

time: 62 us -> 59.5 us (0.960)
  waiting for transfers between devices: 6.72 us -> 3.67 us
    ppermute x17 -> x18, waiting for transfers between devices: 6.72 us -> 3.67 us  [swap(): return lax.ppermute(value, AXES, [(i, i ^ mask) for i in range(count)])]
    ppermute x17 -> x18, starting transfers between devices: 23.5 us -> 24.1 us  [swap(): return lax.ppermute(value, AXES, [(i, i ^ mask) for i in range(count)])]
    pallas_call x2 -> x4, Pallas kernels: 6.85 us -> 6.8 us  [the longest x1 2.92 us: back_calls(): pl.pallas_call(functools.partial(back_kernel, seq, masks), out_shape=[sha...]
  transfers between devices with their start and end apart: 17 -> 18, of which waited for: 7 -> 6; matrix products, arithmetic and copies ran while one was open for 0% -> 0% of each run, Pallas kernels for 15% -> 22%
where the time goes in v4:
time: 59.5 us; the launch traced here: 59.3 us
  starting transfers between devices  24.1 us (41%)
  Pallas kernels  16.9 us (28%)
  blocking collectives  10.2 us (17%)
  waiting for transfers between devices  3.67 us (6%)
  local copies, waits for them, and re-layouts  3.56 us (6%)
  between operations  0.81 us (1%)
    ppermute x18, starting transfers between devices, swap(): return lax.ppermute(value, AXES, [(i, i ^ mask) for i in range(count)])  24.1 us
    all_to_all x1, blocking collectives, gathered(): lax.all_to_all(copies, AXES, split_axis=0, concat_axis=0, tiled=True, axi...  10.2 us
    pallas_call x5, Pallas kernels, encode_call(): pl.pallas_call(functools.partial(encode_kernel, layout), out_shape=encode...  7.92 us
    ppermute x18, waiting for transfers between devices, swap(): return lax.ppermute(value, AXES, [(i, i ^ mask) for i in range(count)])  3.67 us
    unnamed x16, local copies, waits for them, and re-layouts  3.56 us
    pallas_call x1, Pallas kernels, back_calls(): pl.pallas_call(functools.partial(back_kernel, seq, masks), out_shape=[sha...  2.92 us
    pallas_call x2, Pallas kernels, final_call(): pl.pallas_call(functools.partial(final_kernel, first), out_shape=[jax.Sha...  2.18 us
    pallas_call x1, Pallas kernels, back_calls(): pl.pallas_call(more_kernel, out_shape=share_shape, scratch_shapes=[act],...  1.69 us
  transfers between devices with their start and end apart: 18, of which 6 were waited for; matrix products, arithmetic and copies ran while one was open for 0% of the time, Pallas kernels for 22%

profile of v4, /device:TPU:0, one launch (start us, length us, event | category | flops | bytes accessed | tf_op | source)
XLA Modules:
  0.0 59.3 jit_solution(17722802342715628692)
XLA Ops:
  0.6 4.1 %collective-permute-start.2 = (bf16[128,768]{1,0:T(8,128)(2,1)}, bf16[128,768]{1,0:T(8,128)(2,1)S(1)}, u32[]{:S(2)}, u32[]{:S(2)}) collective-permute-start(bf16[128,768]{1,0:T(8,128)(2,1)} %bitcast.1), channel_id=1, source_target_pairs={{0,16},{1,17},{2,18},{3,19},{4,20},{5,21},{6,22},{7,23},{8,24},{9,... | collective-permute-start | bytes 589832 | tf_op jit(solution)/shard_map/ppermute | solution.py:382
  4.7 1.5 %collective-permute-start.5 = (bf16[128,768]{1,0:T(8,128)(2,1)}, bf16[128,768]{1,0:T(8,128)(2,1)S(1)}, u32[]{:S(2)}, u32[]{:S(2)}) collective-permute-start(bf16[128,768]{1,0:T(8,128)(2,1)} %bitcast.2), channel_id=1, source_target_pairs={{0,4},{1,5},{2,6},{3,7},{4,0},{5,1},{6,2},{7,3},{8,12},{9,13},{10,... | collective-permute-start | bytes 589832 | tf_op jit(solution)/shard_map/ppermute | solution.py:382
  6.2 1.6 %collective-permute-start.3 = (bf16[128,768]{1,0:T(8,128)(2,1)}, bf16[128,768]{1,0:T(8,128)(2,1)S(1)}, u32[]{:S(2)}, u32[]{:S(2)}) collective-permute-start(bf16[128,768]{1,0:T(8,128)(2,1)} %bitcast.3), channel_id=1, source_target_pairs={{0,8},{1,9},{2,10},{3,11},{4,12},{5,13},{6,14},{7,15},{8,0},{9,1},... | collective-permute-start | bytes 589832 | tf_op jit(solution)/shard_map/ppermute | solution.py:382
  7.8 1.5 %collective-permute-start.4 = (bf16[128,768]{1,0:T(8,128)(2,1)}, bf16[128,768]{1,0:T(8,128)(2,1)S(1)}, u32[]{:S(2)}, u32[]{:S(2)}) collective-permute-start(bf16[128,768]{1,0:T(8,128)(2,1)} %bitcast.4), channel_id=1, source_target_pairs={{0,1},{1,0},{2,3},{3,2},{4,5},{5,4},{6,7},{7,6},{8,9},{9,8},{10,11... | collective-permute-start | bytes 589832 | tf_op jit(solution)/shard_map/ppermute | solution.py:382
  9.3 1.3 %copy-done = bf16[768,768]{1,0:T(8,128)(2,1)S(1)} copy-done((bf16[768,768]{1,0:T(8,128)(2,1)S(1)}, bf16[768,768]{1,0:T(8,128)(2,1)}, u32[]{:S(2)}) %copy-start) | copy-done | bytes 1179672
  10.6 0.7 %copy-done.3 = f32[2,768]{1,0:T(2,128)S(1)} copy-done((f32[2,768]{1,0:T(2,128)S(1)}, f32[2,768]{1,0:T(2,128)}, u32[]{:S(2)}) %copy-start.3) | copy-done | bytes 6168
  11.3 0.9 %copy-done.5 = bf16[1,128,768]{2,1,0:T(8,128)(2,1)S(1)} copy-done((bf16[1,128,768]{2,1,0:T(8,128)(2,1)S(1)}, bf16[1,128,768]{2,1,0:T(8,128)(2,1)}, u32[]{:S(2)}) %copy-start.5) | copy-done | bytes 196632
  12.2 0.7 %copy-done.7 = s32[1,8]{1,0:T(1,128)S(1)} copy-done((s32[1,8]{1,0:T(1,128)S(1)}, s32[1,8]{1,0:T(1,128)}, u32[]{:S(2)}) %copy-start.7) | copy-done | bytes 56
  12.9 1.3 %first.1 = (bf16[128,768]{1,0:T(8,128)(2,1)S(1)}, f32[128,768]{1,0:T(8,128)S(1)}, f32[1,8,768]{2,1,0:T(8,128)S(1)}, bf16[32,8,128]{2,1,0:T(8,128)(2,1)S(1)}) custom-call(bf16[128,768]{1,0:T(8,128)(2,1)S(1)} %bitcast.5, f32[2,768]{1,0:T(2,128)S(1)} %copy-done.3, bf16[768,768]{1,0:T(8,128)(2,1)S(1)} %copy-done, s32[1,8]{1,0:T(1,128)S(1)} %copy-done.7), custom_call_target="tpu_custom_call" | custom-call | tf_op jit(solution)/shard_map/first/pallas_call | solution.py:120
  14.2 1.4 %collective-permute-done.3.refs_1_.refs_0_ = bf16[128,768]{1,0:T(8,128)(2,1)S(1)} collective-permute-done((bf16[128,768]{1,0:T(8,128)(2,1)}, bf16[128,768]{1,0:T(8,128)(2,1)S(1)}, u32[]{:S(2)}, u32[]{:S(2)}) %collective-permute-start.3) | collective-permute-done | bytes 196640 | tf_op jit(solution)/shard_map/ppermute | solution.py:382
  15.6 1.6 %collective-permute-start.7 = (bf16[320,768]{1,0:T(8,128)(2,1)S(1)}, bf16[320,768]{1,0:T(8,128)(2,1)S(1)}, u32[]{:S(2)}, u32[]{:S(2)}) collective-permute-start(bf16[320,768]{1,0:T(8,128)(2,1)S(1)} %join.7), channel_id=1, source_target_pairs={{0,1},{1,0},{2,3},{3,2},{4,5},{5,4},{6,7},{7,6},{8,9},{9,8},{10,11... | collective-permute-start | bytes 1474568 | tf_op jit(solution)/shard_map/ppermute | solution.py:382
  17.9 1.2 %collective-permute-start.10 = (bf16[128,768]{1,0:T(8,128)(2,1)S(1)}, bf16[128,768]{1,0:T(8,128)(2,1)S(1)}, u32[]{:S(2)}, u32[]{:S(2)}) collective-permute-start(bf16[128,768]{1,0:T(8,128)(2,1)S(1)} %join.9), channel_id=1, source_target_pairs={{0,8},{1,9},{2,10},{3,11},{4,12},{5,13},{6,14},{7,15},{8,0},{9,1},... | collective-permute-start | bytes 589832 | tf_op jit(solution)/shard_map/ppermute | solution.py:382
  19.1 10.2 %all_to_all.5.rows_ref = bf16[32,8,128]{2,1,0:T(8,128)(2,1)S(1)} all-to-all(bf16[32,8,128]{2,1,0:T(8,128)(2,1)S(1)} %get-tuple-element.31), channel_id=1, replica_groups={{0,1,4,5,8,9,12,13,16,17,20,21,24,25,28,29,2,3,6,7,10,11,14,15,18,19,22..., dimensions={0} | all-to-all | bytes 131072 | tf_op jit(solution)/shard_map/all_to_all | solution.py:452
  29.4 0.7 %head.1 = (f32[16,768]{1,0:T(8,128)S(1)}, f32[16,768]{1,0:T(8,128)S(1)}) custom-call(bf16[32,8,128]{2,1,0:T(8,128)(2,1)S(1)} %all_to_all.5.rows_ref, bf16[512,768]{1,0:T(8,128)(2,1)S(1)} %copy-done.2, bf16[512]{0:T(512)(128)(2,1)S(1)} %copy-done.6), custom_call_target="tpu_custom_call" | custom-call | tf_op jit(solution)/shard_map/head/pallas_call | solution.py:465
  30.2 1.2 %collective-permute-done.refs_1_ = f32[16,768]{1,0:T(8,128)S(1)} collective-permute-done((f32[16,768]{1,0:T(8,128)S(1)}, f32[16,768]{1,0:T(8,128)S(1)}, u32[]{:S(2)}, u32[]{:S(2)}) %collective-permute-start) | collective-permute-done | bytes 49184 | tf_op jit(solution)/shard_map/ppermute | solution.py:382
  31.5 0.9 %collective-permute-start.13 = (bf16[256,768]{1,0:T(8,128)(2,1)S(1)}, bf16[256,768]{1,0:T(8,128)(2,1)S(1)}, u32[]{:S(2)}, u32[]{:S(2)}) collective-permute-start(bf16[256,768]{1,0:T(8,128)(2,1)S(1)} %join.11), channel_id=1, source_target_pairs={{0,4},{1,5},{2,6},{3,7},{4,0},{5,1},{6,2},{7,3},{8,12},{9,13},{10,... | collective-permute-start | bytes 1179656 | tf_op jit(solution)/shard_map/ppermute | solution.py:382
  32.4 1.2 %collective-permute-start.12 = (bf16[256,768]{1,0:T(8,128)(2,1)S(1)}, bf16[256,768]{1,0:T(8,128)(2,1)S(1)}, u32[]{:S(2)}, u32[]{:S(2)}) collective-permute-start(bf16[256,768]{1,0:T(8,128)(2,1)S(1)} %join.10), channel_id=1, source_target_pairs={{0,1},{1,0},{2,3},{3,2},{4,5},{5,4},{6,7},{7,6},{8,9},{9,8},{10,11... | collective-permute-start | bytes 1179656 | tf_op jit(solution)/shard_map/ppermute | solution.py:382
  33.6 1.8 %collective-permute-start.1 = (f32[16,768]{1,0:T(8,128)S(1)}, f32[16,768]{1,0:T(8,128)S(1)}, u32[]{:S(2)}, u32[]{:S(2)}) collective-permute-start(f32[16,768]{1,0:T(8,128)S(1)} %add.5.refs_0_.refs_2_), channel_id=1, source_target_pairs={{0,8},{1,9},{2,10},{3,11},{4,12},{5,13},{6,14},{7,15},{8,0},{9,1},... | collective-permute-start | bytes 147464 | tf_op jit(solution)/shard_map/ppermute | solution.py:382
  35.4 2.0 %encode.5 = (bf16[512,768]{1,0:T(8,128)(2,1)S(1)}, f32[512,768]{1,0:T(8,128)S(1)}, f32[4,8,768]{2,1,0:T(8,128)S(1)}) custom-call(bf16[128,768]{1,0:T(8,128)(2,1)S(1)} %collective-permute-done.2.refs_0_.refs_1_, bf16[128,768]{1,0:T(8,128)(2,1)S(1)} %collective-permute-done.3.refs_1_.refs_0_, bf16[128,768]{1,0:T(8,128)(2,1)S(1)} %collective-permute-done.4.refs_2_, ...), custom_call_target="tpu_custom_call" | custom-call | tf_op jit(solution)/shard_map/encode/pallas_call | solution.py:133
  37.7 3.1 %collective-permute-start.6 = (f32[16,768]{1,0:T(8,128)S(1)}, f32[16,768]{1,0:T(8,128)S(1)}, u32[]{:S(2)}, u32[]{:S(2)}) collective-permute-start(f32[16,768]{1,0:T(8,128)S(1)} %add.6.refs_0_), channel_id=1, source_target_pairs={{0,16},{1,17},{2,18},{3,19},{4,20},{5,21},{6,22},{7,23},{8,24},{9,... | collective-permute-start | bytes 147464 | tf_op jit(solution)/shard_map/ppermute | solution.py:382
  40.8 2.0 %encode.6 = (bf16[512,768]{1,0:T(8,128)(2,1)S(1)}, f32[512,768]{1,0:T(8,128)S(1)}, f32[4,8,768]{2,1,0:T(8,128)S(1)}) custom-call(bf16[320,768]{1,0:T(8,128)(2,1)S(1)} %collective-permute-done.7.refs_0_.refs_1_, bf16[320,768]{1,0:T(8,128)(2,1)S(1)} %collective-permute-done.8.refs_1_.refs_0_, f32[2,768]{1,0:T(2,128)S(1)} %copy-done.4, ...), custom_call_target="tpu_custom_call" | custom-call | tf_op jit(solution)/shard_map/encode/pallas_call | solution.py:133
  42.9 0.8 %collective-permute-start.9 = (f32[16,768]{1,0:T(8,128)S(1)}, f32[16,768]{1,0:T(8,128)S(1)}, u32[]{:S(2)}, u32[]{:S(2)}) collective-permute-start(f32[16,768]{1,0:T(8,128)S(1)} %add.7.refs_0_.refs_1_), channel_id=1, source_target_pairs={{0,1},{1,0},{2,3},{3,2},{4,5},{5,4},{6,7},{7,6},{8,9},{9,8},{10,11... | collective-permute-start | bytes 147464 | tf_op jit(solution)/shard_map/ppermute | solution.py:382
  43.7 1.4 %collective-permute-start.14 = (bf16[64,768]{1,0:T(8,128)(2,1)S(1)}, bf16[64,768]{1,0:T(8,128)(2,1)S(1)}, u32[]{:S(2)}, u32[]{:S(2)}) collective-permute-start(bf16[64,768]{1,0:T(8,128)(2,1)S(1)} %join.12), channel_id=1, source_target_pairs={{0,1},{1,0},{2,3},{3,2},{4,5},{5,4},{6,7},{7,6},{8,9},{9,8},{10,11... | collective-permute-start | bytes 294920 | tf_op jit(solution)/shard_map/ppermute | solution.py:382
  45.1 0.7 %collective-permute-start.15 = (bf16[64,768]{1,0:T(8,128)(2,1)S(1)}, bf16[64,768]{1,0:T(8,128)(2,1)S(1)}, u32[]{:S(2)}, u32[]{:S(2)}) collective-permute-start(bf16[64,768]{1,0:T(8,128)(2,1)S(1)} %join.13), channel_id=1, source_target_pairs={{0,4},{1,5},{2,6},{3,7},{4,0},{5,1},{6,2},{7,3},{8,12},{9,13},{10,... | collective-permute-start | bytes 294920 | tf_op jit(solution)/shard_map/ppermute | solution.py:382
  45.8 1.1 %encode.7 = (bf16[256,768]{1,0:T(8,128)(2,1)S(1)}, f32[256,768]{1,0:T(8,128)S(1)}, f32[2,8,768]{2,1,0:T(8,128)S(1)}) custom-call(bf16[320,768]{1,0:T(8,128)(2,1)S(1)} %collective-permute-done.8.refs_1_.refs_0_, bf16[128,768]{1,0:T(8,128)(2,1)S(1)} %collective-permute-done.10.refs_1_.refs_0_, f32[2,768]{1,0:T(2,128)S(1)} %copy-done.4, ...), custom_call_target="tpu_custom_call" | custom-call | tf_op jit(solution)/shard_map/encode/pallas_call | solution.py:133
  47.1 1.3 %collective-permute-start.11 = (f32[16,768]{1,0:T(8,128)S(1)}, f32[16,768]{1,0:T(8,128)S(1)}, u32[]{:S(2)}, u32[]{:S(2)}) collective-permute-start(f32[16,768]{1,0:T(8,128)S(1)} %add.8.refs_0_), channel_id=1, source_target_pairs={{0,4},{1,5},{2,6},{3,7},{4,0},{5,1},{6,2},{7,3},{8,12},{9,13},{10,... | collective-permute-start | bytes 147464 | tf_op jit(solution)/shard_map/ppermute | solution.py:382
  48.4 2.0 %encode.8 = (bf16[512,768]{1,0:T(8,128)(2,1)S(1)}, f32[512,768]{1,0:T(8,128)S(1)}, f32[4,8,768]{2,1,0:T(8,128)S(1)}) custom-call(bf16[256,768]{1,0:T(8,128)(2,1)S(1)} %collective-permute-done.12.refs_0_, bf16[256,768]{1,0:T(8,128)(2,1)S(1)} %collective-permute-done.13.refs_1_.refs_0_, f32[2,768]{1,0:T(2,128)S(1)} %copy-done.4, bf16[768,768]{1,0:T(8,128)(2,1)S(1)} %copy-done.1), custom_call_target="tpu_custom_call" | custom-call | tf_op jit(solution)/shard_map/encode/pallas_call | solution.py:133
  50.4 0.8 %encode.9 = (bf16[128,768]{1,0:T(8,128)(2,1)S(1)}, f32[128,768]{1,0:T(8,128)S(1)}, f32[1,8,768]{2,1,0:T(8,128)S(1)}) custom-call(bf16[64,768]{1,0:T(8,128)(2,1)S(1)} %collective-permute-done.14.refs_0_, bf16[64,768]{1,0:T(8,128)(2,1)S(1)} %collective-permute-done.15.refs_1_, f32[2,768]{1,0:T(2,128)S(1)} %copy-done.4, bf16[768,768]{1,0:T(8,128)(2,1)S(1)} %copy-done.1), custom_call_target="tpu_custom_call" | custom-call | tf_op jit(solution)/shard_map/encode/pallas_call | solution.py:133
  51.2 2.9 %back.1 = (bf16[400,768]{1,0:T(8,128)(2,1)S(1)}, f32[1,768]{1,0:T(1,128)}, bf16[2048,768]{1,0:T(8,128)(2,1)S(1)}, bf16[48,768]{1,0:T(8,128)(2,1)S(1)}, bf16[48,768]{1,0:T(8,128)(2,1)S(1)}) custom-call(f32[16,768]{1,0:T(8,128)S(1)} %add.9.refs_0_, f32[2,768]{1,0:T(2,128)S(1)} %copy-done.4, bf16[768,768]{1,0:T(8,128)(2,1)S(1)} %copy-done.1, ...), custom_call_target="tpu_custom_call" | custom-call | tf_op jit(solution)/shard_map/back/pallas_call | solution.py:307
  54.2 1.7 %more.1.refs_0_ = bf16[400,768]{1,0:T(8,128)(2,1)S(1)} custom-call(f32[2,768]{1,0:T(2,128)S(1)} %copy-done.4, bf16[768,768]{1,0:T(8,128)(2,1)S(1)} %copy-done.1, bf16[2048,768]{1,0:T(8,128)(2,1)S(1)} %get-tuple-element.53.refs_2_, bf16[48,768]{1,0:T(8,128)(2,1)S(1)} %get-tuple-element.54.refs_3_, bf16[48,768]{1,0:T(8,128)(2,1)S(1)} %get-tuple-element.55.refs_4_, ...), custom_call_target="tpu_custom_call" | custom-call | tf_op jit(solution)/shard_map/more/pallas_call | solution.py:327
  56.5 1.1 %final.2.refs_4_ = f32[768,768]{1,0:T(8,128)} custom-call(bf16[400,768]{1,0:T(8,128)(2,1)S(1)} %get-tuple-element.56.refs_0_.refs_2_, bf16[400,768]{1,0:T(8,128)(2,1)S(1)} %collective-permute-done.17.refs_1_.refs_3_), custom_call_target="tpu_custom_call" | custom-call | tf_op jit(solution)/shard_map/final/pallas_call | solution.py:365
  58.2 1.1 %final.3 = (f32[768,768]{1,0:T(8,128)}, f32[2,768]{1,0:T(2,128)}) custom-call(bf16[400,768]{1,0:T(8,128)(2,1)S(1)} %more.1.refs_0_, bf16[400,768]{1,0:T(8,128)(2,1)S(1)} %collective-permute-done.16.refs_1_, bf16[400,768]{1,0:T(8,128)(2,1)S(1)} %get-tuple-element.56.refs_0_.refs_2_, ...), custom_call_target="tpu_custom_call", output_to_operand_aliasing={{0}: (4, {})} | custom-call | tf_op jit(solution)/shard_map/final/pallas_call | solution.py:365
  (45 shorter events, 2.6 us)
Async XLA Ops:
  0.6 13.6 %collective-permute-start.2 = (bf16[128,768]{1,0:T(8,128)(2,1)}, bf16[128,768]{1,0:T(8,128)(2,1)S(1)}, u32[]{:S(2)}, u32[]{:S(2)}) collective-permute-start(bf16[128,768]{1,0:T(8,128)(2,1)} %bitcast.1), channel_id=1, source_target_pairs={{0,16},{1,17},{2,18},{3,19},{4,20},{5,21},{6,22},{7,23},{8,24},{9,... | collective-permute-start | bytes 589832 | tf_op jit(solution)/shard_map/ppermute | solution.py:382
  4.7 9.5 %collective-permute-start.5 = (bf16[128,768]{1,0:T(8,128)(2,1)}, bf16[128,768]{1,0:T(8,128)(2,1)S(1)}, u32[]{:S(2)}, u32[]{:S(2)}) collective-permute-start(bf16[128,768]{1,0:T(8,128)(2,1)} %bitcast.2), channel_id=1, source_target_pairs={{0,4},{1,5},{2,6},{3,7},{4,0},{5,1},{6,2},{7,3},{8,12},{9,13},{10,... | collective-permute-start | bytes 589832 | tf_op jit(solution)/shard_map/ppermute | solution.py:382
  6.2 9.3 %collective-permute-start.3 = (bf16[128,768]{1,0:T(8,128)(2,1)}, bf16[128,768]{1,0:T(8,128)(2,1)S(1)}, u32[]{:S(2)}, u32[]{:S(2)}) collective-permute-start(bf16[128,768]{1,0:T(8,128)(2,1)} %bitcast.3), channel_id=1, source_target_pairs={{0,8},{1,9},{2,10},{3,11},{4,12},{5,13},{6,14},{7,15},{8,0},{9,1},... | collective-permute-start | bytes 589832 | tf_op jit(solution)/shard_map/ppermute | solution.py:382
  7.8 9.4 %collective-permute-start.4 = (bf16[128,768]{1,0:T(8,128)(2,1)}, bf16[128,768]{1,0:T(8,128)(2,1)S(1)}, u32[]{:S(2)}, u32[]{:S(2)}) collective-permute-start(bf16[128,768]{1,0:T(8,128)(2,1)} %bitcast.4), channel_id=1, source_target_pairs={{0,1},{1,0},{2,3},{3,2},{4,5},{5,4},{6,7},{7,6},{8,9},{9,8},{10,11... | collective-permute-start | bytes 589832 | tf_op jit(solution)/shard_map/ppermute | solution.py:382
  9.3 1.3 %copy-start = (bf16[768,768]{1,0:T(8,128)(2,1)S(1)}, bf16[768,768]{1,0:T(8,128)(2,1)}, u32[]{:S(2)}) copy-start(bf16[768,768]{1,0:T(8,128)(2,1)} %refs_1_.5) | copy-start | bytes 3538948
  10.6 0.7 %copy-start.3 = (f32[2,768]{1,0:T(2,128)S(1)}, f32[2,768]{1,0:T(2,128)}, u32[]{:S(2)}) copy-start(f32[2,768]{1,0:T(2,128)} %refs_0_.1) | copy-start | bytes 18436
  11.3 0.9 %copy-start.5 = (bf16[1,128,768]{2,1,0:T(8,128)(2,1)S(1)}, bf16[1,128,768]{2,1,0:T(8,128)(2,1)}, u32[]{:S(2)}) copy-start(bf16[1,128,768]{2,1,0:T(8,128)(2,1)} %param.6) | copy-start | bytes 589828
  12.2 0.7 %copy-start.7 = (s32[1,8]{1,0:T(1,128)S(1)}, s32[1,8]{1,0:T(1,128)}, u32[]{:S(2)}) copy-start(s32[1,8]{1,0:T(1,128)} %refs_3_.5) | copy-start | bytes 100
  14.2 15.2 %copy-start.2 = (bf16[512,768]{1,0:T(8,128)(2,1)S(1)}, bf16[512,768]{1,0:T(8,128)(2,1)}, u32[]{:S(2)}) copy-start(bf16[512,768]{1,0:T(8,128)(2,1)} %weight_ref.1) | copy-start | bytes 2359300
  14.2 15.2 %copy-start.6 = (bf16[512]{0:T(512)(128)(2,1)S(1)}, bf16[512]{0:T(512)(128)(2,1)}, u32[]{:S(2)}) copy-start(bf16[512]{0:T(512)(128)(2,1)} %bias_ref.1) | copy-start | bytes 3076
  15.6 15.8 %collective-permute-start.7 = (bf16[320,768]{1,0:T(8,128)(2,1)S(1)}, bf16[320,768]{1,0:T(8,128)(2,1)S(1)}, u32[]{:S(2)}, u32[]{:S(2)}) collective-permute-start(bf16[320,768]{1,0:T(8,128)(2,1)S(1)} %join.7), channel_id=1, source_target_pairs={{0,1},{1,0},{2,3},{3,2},{4,5},{5,4},{6,7},{7,6},{8,9},{9,8},{10,11... | collective-permute-start | bytes 1474568 | tf_op jit(solution)/shard_map/ppermute | solution.py:382
  17.3 15.1 %collective-permute-start.8 = (bf16[320,768]{1,0:T(8,128)(2,1)S(1)}, bf16[320,768]{1,0:T(8,128)(2,1)S(1)}, u32[]{:S(2)}, u32[]{:S(2)}) collective-permute-start(bf16[320,768]{1,0:T(8,128)(2,1)S(1)} %join.8), channel_id=1, source_target_pairs={{0,4},{1,5},{2,6},{3,7},{4,0},{5,1},{6,2},{7,3},{8,12},{9,13},{10,... | collective-permute-start | bytes 1474568 | tf_op jit(solution)/shard_map/ppermute | solution.py:382
  17.9 13.5 %collective-permute-start.10 = (bf16[128,768]{1,0:T(8,128)(2,1)S(1)}, bf16[128,768]{1,0:T(8,128)(2,1)S(1)}, u32[]{:S(2)}, u32[]{:S(2)}) collective-permute-start(bf16[128,768]{1,0:T(8,128)(2,1)S(1)} %join.9), channel_id=1, source_target_pairs={{0,8},{1,9},{2,10},{3,11},{4,12},{5,13},{6,14},{7,15},{8,0},{9,1},... | collective-permute-start | bytes 589832 | tf_op jit(solution)/shard_map/ppermute | solution.py:382
  29.4 6.0 %copy-start.1 = (bf16[768,768]{1,0:T(8,128)(2,1)S(1)}, bf16[768,768]{1,0:T(8,128)(2,1)}, u32[]{:S(2)}) copy-start(bf16[768,768]{1,0:T(8,128)(2,1)} %refs_1_.5) | copy-start | bytes 3538948
  29.4 6.0 %copy-start.4 = (f32[2,768]{1,0:T(2,128)S(1)}, f32[2,768]{1,0:T(2,128)}, u32[]{:S(2)}) copy-start(f32[2,768]{1,0:T(2,128)} %refs_0_.1) | copy-start | bytes 18436
  30.1 1.3 %collective-permute-start = (f32[16,768]{1,0:T(8,128)S(1)}, f32[16,768]{1,0:T(8,128)S(1)}, u32[]{:S(2)}, u32[]{:S(2)}) collective-permute-start(f32[16,768]{1,0:T(8,128)S(1)} %get-tuple-element.33), channel_id=1, source_target_pairs={{0,2},{1,3},{2,0},{3,1},{4,6},{5,7},{6,4},{7,5},{8,10},{9,11},{10,... | collective-permute-start | bytes 147464 | tf_op jit(solution)/shard_map/ppermute | solution.py:382
  31.5 12.2 %collective-permute-start.13 = (bf16[256,768]{1,0:T(8,128)(2,1)S(1)}, bf16[256,768]{1,0:T(8,128)(2,1)S(1)}, u32[]{:S(2)}, u32[]{:S(2)}) collective-permute-start(bf16[256,768]{1,0:T(8,128)(2,1)S(1)} %join.11), channel_id=1, source_target_pairs={{0,4},{1,5},{2,6},{3,7},{4,0},{5,1},{6,2},{7,3},{8,12},{9,13},{10,... | collective-permute-start | bytes 1179656 | tf_op jit(solution)/shard_map/ppermute | solution.py:382
  32.4 12.7 %collective-permute-start.12 = (bf16[256,768]{1,0:T(8,128)(2,1)S(1)}, bf16[256,768]{1,0:T(8,128)(2,1)S(1)}, u32[]{:S(2)}, u32[]{:S(2)}) collective-permute-start(bf16[256,768]{1,0:T(8,128)(2,1)S(1)} %join.10), channel_id=1, source_target_pairs={{0,1},{1,0},{2,3},{3,2},{4,5},{5,4},{6,7},{7,6},{8,9},{9,8},{10,11... | collective-permute-start | bytes 1179656 | tf_op jit(solution)/shard_map/ppermute | solution.py:382
  33.6 4.1 %collective-permute-start.1 = (f32[16,768]{1,0:T(8,128)S(1)}, f32[16,768]{1,0:T(8,128)S(1)}, u32[]{:S(2)}, u32[]{:S(2)}) collective-permute-start(f32[16,768]{1,0:T(8,128)S(1)} %add.5.refs_0_.refs_2_), channel_id=1, source_target_pairs={{0,8},{1,9},{2,10},{3,11},{4,12},{5,13},{6,14},{7,15},{8,0},{9,1},... | collective-permute-start | bytes 147464 | tf_op jit(solution)/shard_map/ppermute | solution.py:382
  37.7 5.2 %collective-permute-start.6 = (f32[16,768]{1,0:T(8,128)S(1)}, f32[16,768]{1,0:T(8,128)S(1)}, u32[]{:S(2)}, u32[]{:S(2)}) collective-permute-start(f32[16,768]{1,0:T(8,128)S(1)} %add.6.refs_0_), channel_id=1, source_target_pairs={{0,16},{1,17},{2,18},{3,19},{4,20},{5,21},{6,22},{7,23},{8,24},{9,... | collective-permute-start | bytes 147464 | tf_op jit(solution)/shard_map/ppermute | solution.py:382
  42.9 4.2 %collective-permute-start.9 = (f32[16,768]{1,0:T(8,128)S(1)}, f32[16,768]{1,0:T(8,128)S(1)}, u32[]{:S(2)}, u32[]{:S(2)}) collective-permute-start(f32[16,768]{1,0:T(8,128)S(1)} %add.7.refs_0_.refs_1_), channel_id=1, source_target_pairs={{0,1},{1,0},{2,3},{3,2},{4,5},{5,4},{6,7},{7,6},{8,9},{9,8},{10,11... | collective-permute-start | bytes 147464 | tf_op jit(solution)/shard_map/ppermute | solution.py:382
  43.7 6.7 %collective-permute-start.14 = (bf16[64,768]{1,0:T(8,128)(2,1)S(1)}, bf16[64,768]{1,0:T(8,128)(2,1)S(1)}, u32[]{:S(2)}, u32[]{:S(2)}) collective-permute-start(bf16[64,768]{1,0:T(8,128)(2,1)S(1)} %join.12), channel_id=1, source_target_pairs={{0,1},{1,0},{2,3},{3,2},{4,5},{5,4},{6,7},{7,6},{8,9},{9,8},{10,11... | collective-permute-start | bytes 294920 | tf_op jit(solution)/shard_map/ppermute | solution.py:382
  45.1 5.3 %collective-permute-start.15 = (bf16[64,768]{1,0:T(8,128)(2,1)S(1)}, bf16[64,768]{1,0:T(8,128)(2,1)S(1)}, u32[]{:S(2)}, u32[]{:S(2)}) collective-permute-start(bf16[64,768]{1,0:T(8,128)(2,1)S(1)} %join.13), channel_id=1, source_target_pairs={{0,4},{1,5},{2,6},{3,7},{4,0},{5,1},{6,2},{7,3},{8,12},{9,13},{10,... | collective-permute-start | bytes 294920 | tf_op jit(solution)/shard_map/ppermute | solution.py:382
  47.1 4.1 %collective-permute-start.11 = (f32[16,768]{1,0:T(8,128)S(1)}, f32[16,768]{1,0:T(8,128)S(1)}, u32[]{:S(2)}, u32[]{:S(2)}) collective-permute-start(f32[16,768]{1,0:T(8,128)S(1)} %add.8.refs_0_), channel_id=1, source_target_pairs={{0,4},{1,5},{2,6},{3,7},{4,0},{5,1},{6,2},{7,3},{8,12},{9,13},{10,... | collective-permute-start | bytes 147464 | tf_op jit(solution)/shard_map/ppermute | solution.py:382
  54.2 2.3 %collective-permute-start.17 = (bf16[400,768]{1,0:T(8,128)(2,1)S(1)}, bf16[400,768]{1,0:T(8,128)(2,1)S(1)}, u32[]{:S(2)}, u32[]{:S(2)}) collective-permute-start(bf16[400,768]{1,0:T(8,128)(2,1)S(1)} %get-tuple-element.56.refs_0_.refs_2_), channel_id=1, source_target_pairs={{0,2},{1,3},{2,0},{3,1},{4,6},{5,7},{6,4},{7,5},{8,10},{9,11},{10,... | collective-permute-start | bytes 1843208 | tf_op jit(solution)/shard_map/ppermute | solution.py:382
  55.9 2.2 %collective-permute-start.16 = (bf16[400,768]{1,0:T(8,128)(2,1)S(1)}, bf16[400,768]{1,0:T(8,128)(2,1)S(1)}, u32[]{:S(2)}, u32[]{:S(2)}) collective-permute-start(bf16[400,768]{1,0:T(8,128)(2,1)S(1)} %more.1.refs_0_), channel_id=1, source_target_pairs={{0,2},{1,3},{2,0},{3,1},{4,6},{5,7},{6,4},{7,5},{8,10},{9,11},{10,... | collective-permute-start | bytes 1843208 | tf_op jit(solution)/shard_map/ppermute | solution.py:382

commit v5 on v4

--- a/solution.py
+++ b/solution.py
@@ -458,7 +458,7 @@
             y: wanted + [(x | doc, h, seq) for doc in corners],
         }
 
-    early = mark([held[far][0][0]])
+    early = mark([held[far][0][0], held[z][0][0]])
     plan = spread([z, far], [0])
     plan[z] = [(far, 0, seq)]
     docs_1, _ = exchange(plan, [groups[0][2], early])
@@ -475,11 +475,11 @@
     docs_2, _ = exchange(plan, [total])
     tied = encode_held(docs_0)
     total = add([total, hop(total, z)], [tied])
-    tied = encode_held(docs_1[:4])
+    tied = encode_held(docs_1[:5])
     total = add([total, hop(total, far)], [tied])
     plan = spread([], [z | far])
     docs_3, _ = exchange(plan, [total])
-    rest = docs_1[4:]
+    rest = docs_1[5:]
     tied = [encode_held(rest)] if rest else []
     total = add([total, hop(total, x)], tied)
     tied = [encode_held(docs_2), encode_held(docs_3)]

time: 59.5 us -> 59.1 us (level)
  starting transfers between devices: 24.1 us -> 23.3 us
    ppermute x18, starting transfers between devices: 24.1 us -> 23.3 us  [swap(): return lax.ppermute(value, AXES, [(i, i ^ mask) for i in range(count)])]
where the time goes in v5:
time: 59.1 us; the launch traced here: 58.8 us
  starting transfers between devices  23.3 us (39%)
  Pallas kernels  17 us (29%)
  blocking collectives  10.1 us (17%)
  waiting for transfers between devices  4.11 us (7%)
  local copies, waits for them, and re-layouts  3.56 us (6%)
  between operations  0.8 us (1%)
    ppermute x18, starting transfers between devices, swap(): return lax.ppermute(value, AXES, [(i, i ^ mask) for i in range(count)])  23.3 us
    all_to_all x1, blocking collectives, gathered(): lax.all_to_all(copies, AXES, split_axis=0, concat_axis=0, tiled=True, axi...  10.1 us
    pallas_call x5, Pallas kernels, encode_call(): pl.pallas_call(functools.partial(encode_kernel, layout), out_shape=encode...  7.98 us
    ppermute x18, waiting for transfers between devices, swap(): return lax.ppermute(value, AXES, [(i, i ^ mask) for i in range(count)])  4.11 us
    unnamed x16, local copies, waits for them, and re-layouts  3.56 us
    pallas_call x1, Pallas kernels, back_calls(): pl.pallas_call(functools.partial(back_kernel, seq, masks), out_shape=[sha...  2.94 us
    pallas_call x2, Pallas kernels, final_call(): pl.pallas_call(functools.partial(final_kernel, first), out_shape=[jax.Sha...  2.18 us
    pallas_call x1, Pallas kernels, back_calls(): pl.pallas_call(more_kernel, out_shape=share_shape, scratch_shapes=[act],...  1.69 us
  transfers between devices with their start and end apart: 18, of which 6 were waited for; matrix products, arithmetic and copies ran while one was open for 0% of the time, Pallas kernels for 22%

profile of v5, /device:TPU:0, one launch (start us, length us, event | category | flops | bytes accessed | tf_op | source)
XLA Modules:
  0.0 58.8 jit_solution(14447432167571652964)
XLA Ops:
  0.6 3.1 %collective-permute-start.3 = (bf16[128,768]{1,0:T(8,128)(2,1)}, bf16[128,768]{1,0:T(8,128)(2,1)S(1)}, u32[]{:S(2)}, u32[]{:S(2)}) collective-permute-start(bf16[128,768]{1,0:T(8,128)(2,1)} %bitcast.1), channel_id=1, source_target_pairs={{0,8},{1,9},{2,10},{3,11},{4,12},{5,13},{6,14},{7,15},{8,0},{9,1},... | collective-permute-start | bytes 589832 | tf_op jit(solution)/shard_map/ppermute | solution.py:382
  3.7 2.6 %collective-permute-start.2 = (bf16[128,768]{1,0:T(8,128)(2,1)}, bf16[128,768]{1,0:T(8,128)(2,1)S(1)}, u32[]{:S(2)}, u32[]{:S(2)}) collective-permute-start(bf16[128,768]{1,0:T(8,128)(2,1)} %bitcast.2), channel_id=1, source_target_pairs={{0,16},{1,17},{2,18},{3,19},{4,20},{5,21},{6,22},{7,23},{8,24},{9,... | collective-permute-start | bytes 589832 | tf_op jit(solution)/shard_map/ppermute | solution.py:382
  6.3 1.5 %collective-permute-start.5 = (bf16[128,768]{1,0:T(8,128)(2,1)}, bf16[128,768]{1,0:T(8,128)(2,1)S(1)}, u32[]{:S(2)}, u32[]{:S(2)}) collective-permute-start(bf16[128,768]{1,0:T(8,128)(2,1)} %bitcast.3), channel_id=1, source_target_pairs={{0,4},{1,5},{2,6},{3,7},{4,0},{5,1},{6,2},{7,3},{8,12},{9,13},{10,... | collective-permute-start | bytes 589832 | tf_op jit(solution)/shard_map/ppermute | solution.py:382
  7.8 1.5 %collective-permute-start.4 = (bf16[128,768]{1,0:T(8,128)(2,1)}, bf16[128,768]{1,0:T(8,128)(2,1)S(1)}, u32[]{:S(2)}, u32[]{:S(2)}) collective-permute-start(bf16[128,768]{1,0:T(8,128)(2,1)} %bitcast.4), channel_id=1, source_target_pairs={{0,1},{1,0},{2,3},{3,2},{4,5},{5,4},{6,7},{7,6},{8,9},{9,8},{10,11... | collective-permute-start | bytes 589832 | tf_op jit(solution)/shard_map/ppermute | solution.py:382
  9.3 1.3 %copy-done = bf16[768,768]{1,0:T(8,128)(2,1)S(1)} copy-done((bf16[768,768]{1,0:T(8,128)(2,1)S(1)}, bf16[768,768]{1,0:T(8,128)(2,1)}, u32[]{:S(2)}) %copy-start) | copy-done | bytes 1179672
  10.6 0.7 %copy-done.3 = f32[2,768]{1,0:T(2,128)S(1)} copy-done((f32[2,768]{1,0:T(2,128)S(1)}, f32[2,768]{1,0:T(2,128)}, u32[]{:S(2)}) %copy-start.3) | copy-done | bytes 6168
  11.3 0.9 %copy-done.5 = bf16[1,128,768]{2,1,0:T(8,128)(2,1)S(1)} copy-done((bf16[1,128,768]{2,1,0:T(8,128)(2,1)S(1)}, bf16[1,128,768]{2,1,0:T(8,128)(2,1)}, u32[]{:S(2)}) %copy-start.5) | copy-done | bytes 196632
  12.2 0.7 %copy-done.7 = s32[1,8]{1,0:T(1,128)S(1)} copy-done((s32[1,8]{1,0:T(1,128)S(1)}, s32[1,8]{1,0:T(1,128)}, u32[]{:S(2)}) %copy-start.7) | copy-done | bytes 56
  12.9 1.3 %first.1 = (bf16[128,768]{1,0:T(8,128)(2,1)S(1)}, f32[128,768]{1,0:T(8,128)S(1)}, f32[1,8,768]{2,1,0:T(8,128)S(1)}, bf16[32,8,128]{2,1,0:T(8,128)(2,1)S(1)}) custom-call(bf16[128,768]{1,0:T(8,128)(2,1)S(1)} %bitcast.5, f32[2,768]{1,0:T(2,128)S(1)} %copy-done.3, bf16[768,768]{1,0:T(8,128)(2,1)S(1)} %copy-done, s32[1,8]{1,0:T(1,128)S(1)} %copy-done.7), custom_call_target="tpu_custom_call" | custom-call | tf_op jit(solution)/shard_map/first/pallas_call | solution.py:120
  14.2 1.3 %collective-permute-done.2.refs_0_.refs_1_ = bf16[128,768]{1,0:T(8,128)(2,1)S(1)} collective-permute-done((bf16[128,768]{1,0:T(8,128)(2,1)}, bf16[128,768]{1,0:T(8,128)(2,1)S(1)}, u32[]{:S(2)}, u32[]{:S(2)}) %collective-permute-start.2) | collective-permute-done | bytes 196640 | tf_op jit(solution)/shard_map/ppermute | solution.py:382
  15.5 1.6 %collective-permute-start.7 = (bf16[320,768]{1,0:T(8,128)(2,1)S(1)}, bf16[320,768]{1,0:T(8,128)(2,1)S(1)}, u32[]{:S(2)}, u32[]{:S(2)}) collective-permute-start(bf16[320,768]{1,0:T(8,128)(2,1)S(1)} %join.7), channel_id=1, source_target_pairs={{0,1},{1,0},{2,3},{3,2},{4,5},{5,4},{6,7},{7,6},{8,9},{9,8},{10,11... | collective-permute-start | bytes 1474568 | tf_op jit(solution)/shard_map/ppermute | solution.py:382
  17.2 1.6 %collective-permute-start.8 = (bf16[320,768]{1,0:T(8,128)(2,1)S(1)}, bf16[320,768]{1,0:T(8,128)(2,1)S(1)}, u32[]{:S(2)}, u32[]{:S(2)}) collective-permute-start(bf16[320,768]{1,0:T(8,128)(2,1)S(1)} %join.8), channel_id=1, source_target_pairs={{0,4},{1,5},{2,6},{3,7},{4,0},{5,1},{6,2},{7,3},{8,12},{9,13},{10,... | collective-permute-start | bytes 1474568 | tf_op jit(solution)/shard_map/ppermute | solution.py:382
  19.2 10.1 %all_to_all.5.rows_ref = bf16[32,8,128]{2,1,0:T(8,128)(2,1)S(1)} all-to-all(bf16[32,8,128]{2,1,0:T(8,128)(2,1)S(1)} %get-tuple-element.31), channel_id=1, replica_groups={{0,1,4,5,8,9,12,13,16,17,20,21,24,25,28,29,2,3,6,7,10,11,14,15,18,19,22..., dimensions={0} | all-to-all | bytes 131072 | tf_op jit(solution)/shard_map/all_to_all | solution.py:452
  29.3 0.7 %head.1 = (f32[16,768]{1,0:T(8,128)S(1)}, f32[16,768]{1,0:T(8,128)S(1)}) custom-call(bf16[32,8,128]{2,1,0:T(8,128)(2,1)S(1)} %all_to_all.5.rows_ref, bf16[512,768]{1,0:T(8,128)(2,1)S(1)} %copy-done.2, bf16[512]{0:T(512)(128)(2,1)S(1)} %copy-done.6), custom_call_target="tpu_custom_call" | custom-call | tf_op jit(solution)/shard_map/head/pallas_call | solution.py:465
  30.1 1.2 %collective-permute-done.refs_1_ = f32[16,768]{1,0:T(8,128)S(1)} collective-permute-done((f32[16,768]{1,0:T(8,128)S(1)}, f32[16,768]{1,0:T(8,128)S(1)}, u32[]{:S(2)}, u32[]{:S(2)}) %collective-permute-start) | collective-permute-done | bytes 49184 | tf_op jit(solution)/shard_map/ppermute | solution.py:382
  31.4 0.9 %collective-permute-start.13 = (bf16[256,768]{1,0:T(8,128)(2,1)S(1)}, bf16[256,768]{1,0:T(8,128)(2,1)S(1)}, u32[]{:S(2)}, u32[]{:S(2)}) collective-permute-start(bf16[256,768]{1,0:T(8,128)(2,1)S(1)} %join.11), channel_id=1, source_target_pairs={{0,4},{1,5},{2,6},{3,7},{4,0},{5,1},{6,2},{7,3},{8,12},{9,13},{10,... | collective-permute-start | bytes 1179656 | tf_op jit(solution)/shard_map/ppermute | solution.py:382
  32.9 2.4 %collective-permute-start.1 = (f32[16,768]{1,0:T(8,128)S(1)}, f32[16,768]{1,0:T(8,128)S(1)}, u32[]{:S(2)}, u32[]{:S(2)}) collective-permute-start(f32[16,768]{1,0:T(8,128)S(1)} %add.5.refs_0_.refs_2_), channel_id=1, source_target_pairs={{0,8},{1,9},{2,10},{3,11},{4,12},{5,13},{6,14},{7,15},{8,0},{9,1},... | collective-permute-start | bytes 147464 | tf_op jit(solution)/shard_map/ppermute | solution.py:382
  35.3 2.0 %encode.5 = (bf16[512,768]{1,0:T(8,128)(2,1)S(1)}, f32[512,768]{1,0:T(8,128)S(1)}, f32[4,8,768]{2,1,0:T(8,128)S(1)}) custom-call(bf16[128,768]{1,0:T(8,128)(2,1)S(1)} %collective-permute-done.2.refs_0_.refs_1_, bf16[128,768]{1,0:T(8,128)(2,1)S(1)} %collective-permute-done.3.refs_1_.refs_0_, bf16[128,768]{1,0:T(8,128)(2,1)S(1)} %collective-permute-done.4.refs_2_, ...), custom_call_target="tpu_custom_call" | custom-call | tf_op jit(solution)/shard_map/encode/pallas_call | solution.py:133
  37.4 2.0 %collective-permute-start.6 = (f32[16,768]{1,0:T(8,128)S(1)}, f32[16,768]{1,0:T(8,128)S(1)}, u32[]{:S(2)}, u32[]{:S(2)}) collective-permute-start(f32[16,768]{1,0:T(8,128)S(1)} %add.6.refs_0_), channel_id=1, source_target_pairs={{0,16},{1,17},{2,18},{3,19},{4,20},{5,21},{6,22},{7,23},{8,24},{9,... | collective-permute-start | bytes 147464 | tf_op jit(solution)/shard_map/ppermute | solution.py:382
  39.4 2.4 %encode.6 = (bf16[640,768]{1,0:T(8,128)(2,1)S(1)}, f32[640,768]{1,0:T(8,128)S(1)}, f32[5,8,768]{2,1,0:T(8,128)S(1)}) custom-call(bf16[320,768]{1,0:T(8,128)(2,1)S(1)} %collective-permute-done.7.refs_0_.refs_1_, bf16[320,768]{1,0:T(8,128)(2,1)S(1)} %collective-permute-done.8.refs_1_, f32[2,768]{1,0:T(2,128)S(1)} %copy-done.4, bf16[768,768]{1,0:T(8,128)(2,1)S(1)} %copy-done.1), custom_call_target="tpu_custom_call" | custom-call | tf_op jit(solution)/shard_map/encode/pallas_call | solution.py:133
  41.8 0.7 %collective-permute-done.6.refs_1_ = f32[16,768]{1,0:T(8,128)S(1)} collective-permute-done((f32[16,768]{1,0:T(8,128)S(1)}, f32[16,768]{1,0:T(8,128)S(1)}, u32[]{:S(2)}, u32[]{:S(2)}) %collective-permute-start.6) | collective-permute-done | bytes 49184 | tf_op jit(solution)/shard_map/ppermute | solution.py:382
  42.5 1.2 %collective-permute-start.9 = (f32[16,768]{1,0:T(8,128)S(1)}, f32[16,768]{1,0:T(8,128)S(1)}, u32[]{:S(2)}, u32[]{:S(2)}) collective-permute-start(f32[16,768]{1,0:T(8,128)S(1)} %add.7.refs_0_.refs_1_), channel_id=1, source_target_pairs={{0,1},{1,0},{2,3},{3,2},{4,5},{5,4},{6,7},{7,6},{8,9},{9,8},{10,11... | collective-permute-start | bytes 147464 | tf_op jit(solution)/shard_map/ppermute | solution.py:382
  43.7 1.0 %collective-permute-start.14 = (bf16[64,768]{1,0:T(8,128)(2,1)S(1)}, bf16[64,768]{1,0:T(8,128)(2,1)S(1)}, u32[]{:S(2)}, u32[]{:S(2)}) collective-permute-start(bf16[64,768]{1,0:T(8,128)(2,1)S(1)} %join.12), channel_id=1, source_target_pairs={{0,1},{1,0},{2,3},{3,2},{4,5},{5,4},{6,7},{7,6},{8,9},{9,8},{10,11... | collective-permute-start | bytes 294920 | tf_op jit(solution)/shard_map/ppermute | solution.py:382
  44.6 1.1 %collective-permute-start.15 = (bf16[64,768]{1,0:T(8,128)(2,1)S(1)}, bf16[64,768]{1,0:T(8,128)(2,1)S(1)}, u32[]{:S(2)}, u32[]{:S(2)}) collective-permute-start(bf16[64,768]{1,0:T(8,128)(2,1)S(1)} %join.13), channel_id=1, source_target_pairs={{0,4},{1,5},{2,6},{3,7},{4,0},{5,1},{6,2},{7,3},{8,12},{9,13},{10,... | collective-permute-start | bytes 294920 | tf_op jit(solution)/shard_map/ppermute | solution.py:382
  45.8 0.8 %encode.7 = (bf16[128,768]{1,0:T(8,128)(2,1)S(1)}, f32[128,768]{1,0:T(8,128)S(1)}, f32[1,8,768]{2,1,0:T(8,128)S(1)}) custom-call(bf16[128,768]{1,0:T(8,128)(2,1)S(1)} %collective-permute-done.10.refs_0_, f32[2,768]{1,0:T(2,128)S(1)} %copy-done.4, bf16[768,768]{1,0:T(8,128)(2,1)S(1)} %copy-done.1), custom_call_target="tpu_custom_call" | custom-call | tf_op jit(solution)/shard_map/encode/pallas_call | solution.py:133
  46.6 1.1 %collective-permute-start.11 = (f32[16,768]{1,0:T(8,128)S(1)}, f32[16,768]{1,0:T(8,128)S(1)}, u32[]{:S(2)}, u32[]{:S(2)}) collective-permute-start(f32[16,768]{1,0:T(8,128)S(1)} %add.8.refs_0_), channel_id=1, source_target_pairs={{0,4},{1,5},{2,6},{3,7},{4,0},{5,1},{6,2},{7,3},{8,12},{9,13},{10,... | collective-permute-start | bytes 147464 | tf_op jit(solution)/shard_map/ppermute | solution.py:382
  47.7 2.0 %encode.8 = (bf16[512,768]{1,0:T(8,128)(2,1)S(1)}, f32[512,768]{1,0:T(8,128)S(1)}, f32[4,8,768]{2,1,0:T(8,128)S(1)}) custom-call(bf16[256,768]{1,0:T(8,128)(2,1)S(1)} %collective-permute-done.12.refs_0_, bf16[256,768]{1,0:T(8,128)(2,1)S(1)} %collective-permute-done.13.refs_1_.refs_0_, f32[2,768]{1,0:T(2,128)S(1)} %copy-done.4, bf16[768,768]{1,0:T(8,128)(2,1)S(1)} %copy-done.1), custom_call_target="tpu_custom_call" | custom-call | tf_op jit(solution)/shard_map/encode/pallas_call | solution.py:133
  49.8 0.8 %encode.9 = (bf16[128,768]{1,0:T(8,128)(2,1)S(1)}, f32[128,768]{1,0:T(8,128)S(1)}, f32[1,8,768]{2,1,0:T(8,128)S(1)}) custom-call(bf16[64,768]{1,0:T(8,128)(2,1)S(1)} %collective-permute-done.14.refs_0_, bf16[64,768]{1,0:T(8,128)(2,1)S(1)} %collective-permute-done.15.refs_1_, f32[2,768]{1,0:T(2,128)S(1)} %copy-done.4, bf16[768,768]{1,0:T(8,128)(2,1)S(1)} %copy-done.1), custom_call_target="tpu_custom_call" | custom-call | tf_op jit(solution)/shard_map/encode/pallas_call | solution.py:133
  50.8 2.9 %back.1 = (bf16[400,768]{1,0:T(8,128)(2,1)S(1)}, f32[1,768]{1,0:T(1,128)}, bf16[2048,768]{1,0:T(8,128)(2,1)S(1)}, bf16[48,768]{1,0:T(8,128)(2,1)S(1)}, bf16[48,768]{1,0:T(8,128)(2,1)S(1)}) custom-call(f32[16,768]{1,0:T(8,128)S(1)} %add.9.refs_0_, f32[2,768]{1,0:T(2,128)S(1)} %copy-done.4, bf16[768,768]{1,0:T(8,128)(2,1)S(1)} %copy-done.1, ...), custom_call_target="tpu_custom_call" | custom-call | tf_op jit(solution)/shard_map/back/pallas_call | solution.py:307
  53.8 1.7 %more.1.refs_0_ = bf16[400,768]{1,0:T(8,128)(2,1)S(1)} custom-call(f32[2,768]{1,0:T(2,128)S(1)} %copy-done.4, bf16[768,768]{1,0:T(8,128)(2,1)S(1)} %copy-done.1, bf16[2048,768]{1,0:T(8,128)(2,1)S(1)} %get-tuple-element.53.refs_2_, bf16[48,768]{1,0:T(8,128)(2,1)S(1)} %get-tuple-element.54.refs_3_, bf16[48,768]{1,0:T(8,128)(2,1)S(1)} %get-tuple-element.55.refs_4_, ...), custom_call_target="tpu_custom_call" | custom-call | tf_op jit(solution)/shard_map/more/pallas_call | solution.py:327
  56.1 1.1 %final.2.refs_4_ = f32[768,768]{1,0:T(8,128)} custom-call(bf16[400,768]{1,0:T(8,128)(2,1)S(1)} %get-tuple-element.56.refs_0_.refs_2_, bf16[400,768]{1,0:T(8,128)(2,1)S(1)} %collective-permute-done.17.refs_1_.refs_3_), custom_call_target="tpu_custom_call" | custom-call | tf_op jit(solution)/shard_map/final/pallas_call | solution.py:365
  57.7 1.1 %final.3 = (f32[768,768]{1,0:T(8,128)}, f32[2,768]{1,0:T(2,128)}) custom-call(bf16[400,768]{1,0:T(8,128)(2,1)S(1)} %more.1.refs_0_, bf16[400,768]{1,0:T(8,128)(2,1)S(1)} %collective-permute-done.16.refs_1_, bf16[400,768]{1,0:T(8,128)(2,1)S(1)} %get-tuple-element.56.refs_0_.refs_2_, ...), custom_call_target="tpu_custom_call", output_to_operand_aliasing={{0}: (4, {})} | custom-call | tf_op jit(solution)/shard_map/final/pallas_call | solution.py:365
  (45 shorter events, 3.0 us)
Async XLA Ops:
  0.6 28.7 %copy-start.6 = (bf16[512]{0:T(512)(128)(2,1)S(1)}, bf16[512]{0:T(512)(128)(2,1)}, u32[]{:S(2)}) copy-start(bf16[512]{0:T(512)(128)(2,1)} %bias_ref.1) | copy-start | bytes 3076
  0.6 13.5 %collective-permute-start.3 = (bf16[128,768]{1,0:T(8,128)(2,1)}, bf16[128,768]{1,0:T(8,128)(2,1)S(1)}, u32[]{:S(2)}, u32[]{:S(2)}) collective-permute-start(bf16[128,768]{1,0:T(8,128)(2,1)} %bitcast.1), channel_id=1, source_target_pairs={{0,8},{1,9},{2,10},{3,11},{4,12},{5,13},{6,14},{7,15},{8,0},{9,1},... | collective-permute-start | bytes 589832 | tf_op jit(solution)/shard_map/ppermute | solution.py:382
  3.7 11.7 %collective-permute-start.2 = (bf16[128,768]{1,0:T(8,128)(2,1)}, bf16[128,768]{1,0:T(8,128)(2,1)S(1)}, u32[]{:S(2)}, u32[]{:S(2)}) collective-permute-start(bf16[128,768]{1,0:T(8,128)(2,1)} %bitcast.2), channel_id=1, source_target_pairs={{0,16},{1,17},{2,18},{3,19},{4,20},{5,21},{6,22},{7,23},{8,24},{9,... | collective-permute-start | bytes 589832 | tf_op jit(solution)/shard_map/ppermute | solution.py:382
  6.3 9.2 %collective-permute-start.5 = (bf16[128,768]{1,0:T(8,128)(2,1)}, bf16[128,768]{1,0:T(8,128)(2,1)S(1)}, u32[]{:S(2)}, u32[]{:S(2)}) collective-permute-start(bf16[128,768]{1,0:T(8,128)(2,1)} %bitcast.3), channel_id=1, source_target_pairs={{0,4},{1,5},{2,6},{3,7},{4,0},{5,1},{6,2},{7,3},{8,12},{9,13},{10,... | collective-permute-start | bytes 589832 | tf_op jit(solution)/shard_map/ppermute | solution.py:382
  7.8 9.3 %collective-permute-start.4 = (bf16[128,768]{1,0:T(8,128)(2,1)}, bf16[128,768]{1,0:T(8,128)(2,1)S(1)}, u32[]{:S(2)}, u32[]{:S(2)}) collective-permute-start(bf16[128,768]{1,0:T(8,128)(2,1)} %bitcast.4), channel_id=1, source_target_pairs={{0,1},{1,0},{2,3},{3,2},{4,5},{5,4},{6,7},{7,6},{8,9},{9,8},{10,11... | collective-permute-start | bytes 589832 | tf_op jit(solution)/shard_map/ppermute | solution.py:382
  9.3 1.3 %copy-start = (bf16[768,768]{1,0:T(8,128)(2,1)S(1)}, bf16[768,768]{1,0:T(8,128)(2,1)}, u32[]{:S(2)}) copy-start(bf16[768,768]{1,0:T(8,128)(2,1)} %refs_1_.7) | copy-start | bytes 3538948
  10.6 0.7 %copy-start.3 = (f32[2,768]{1,0:T(2,128)S(1)}, f32[2,768]{1,0:T(2,128)}, u32[]{:S(2)}) copy-start(f32[2,768]{1,0:T(2,128)} %refs_0_.1) | copy-start | bytes 18436
  11.3 0.9 %copy-start.5 = (bf16[1,128,768]{2,1,0:T(8,128)(2,1)S(1)}, bf16[1,128,768]{2,1,0:T(8,128)(2,1)}, u32[]{:S(2)}) copy-start(bf16[1,128,768]{2,1,0:T(8,128)(2,1)} %param.6) | copy-start | bytes 589828
  12.2 0.7 %copy-start.7 = (s32[1,8]{1,0:T(1,128)S(1)}, s32[1,8]{1,0:T(1,128)}, u32[]{:S(2)}) copy-start(s32[1,8]{1,0:T(1,128)} %refs_3_.4) | copy-start | bytes 100
  12.9 16.4 %copy-start.2 = (bf16[512,768]{1,0:T(8,128)(2,1)S(1)}, bf16[512,768]{1,0:T(8,128)(2,1)}, u32[]{:S(2)}) copy-start(bf16[512,768]{1,0:T(8,128)(2,1)} %weight_ref.1) | copy-start | bytes 2359300
  15.5 15.8 %collective-permute-start.7 = (bf16[320,768]{1,0:T(8,128)(2,1)S(1)}, bf16[320,768]{1,0:T(8,128)(2,1)S(1)}, u32[]{:S(2)}, u32[]{:S(2)}) collective-permute-start(bf16[320,768]{1,0:T(8,128)(2,1)S(1)} %join.7), channel_id=1, source_target_pairs={{0,1},{1,0},{2,3},{3,2},{4,5},{5,4},{6,7},{7,6},{8,9},{9,8},{10,11... | collective-permute-start | bytes 1474568 | tf_op jit(solution)/shard_map/ppermute | solution.py:382
  17.1 18.2 %copy-start.1 = (bf16[768,768]{1,0:T(8,128)(2,1)S(1)}, bf16[768,768]{1,0:T(8,128)(2,1)}, u32[]{:S(2)}) copy-start(bf16[768,768]{1,0:T(8,128)(2,1)} %refs_1_.7) | copy-start | bytes 3538948
  17.2 18.2 %copy-start.4 = (f32[2,768]{1,0:T(2,128)S(1)}, f32[2,768]{1,0:T(2,128)}, u32[]{:S(2)}) copy-start(f32[2,768]{1,0:T(2,128)} %refs_0_.1) | copy-start | bytes 18436
  17.2 15.1 %collective-permute-start.8 = (bf16[320,768]{1,0:T(8,128)(2,1)S(1)}, bf16[320,768]{1,0:T(8,128)(2,1)S(1)}, u32[]{:S(2)}, u32[]{:S(2)}) collective-permute-start(bf16[320,768]{1,0:T(8,128)(2,1)S(1)} %join.8), channel_id=1, source_target_pairs={{0,4},{1,5},{2,6},{3,7},{4,0},{5,1},{6,2},{7,3},{8,12},{9,13},{10,... | collective-permute-start | bytes 1474568 | tf_op jit(solution)/shard_map/ppermute | solution.py:382
  18.7 12.6 %collective-permute-start.10 = (bf16[128,768]{1,0:T(8,128)(2,1)S(1)}, bf16[128,768]{1,0:T(8,128)(2,1)S(1)}, u32[]{:S(2)}, u32[]{:S(2)}) collective-permute-start(bf16[128,768]{1,0:T(8,128)(2,1)S(1)} %join.9), channel_id=1, source_target_pairs={{0,8},{1,9},{2,10},{3,11},{4,12},{5,13},{6,14},{7,15},{8,0},{9,1},... | collective-permute-start | bytes 589832 | tf_op jit(solution)/shard_map/ppermute | solution.py:382
  30.0 1.3 %collective-permute-start = (f32[16,768]{1,0:T(8,128)S(1)}, f32[16,768]{1,0:T(8,128)S(1)}, u32[]{:S(2)}, u32[]{:S(2)}) collective-permute-start(f32[16,768]{1,0:T(8,128)S(1)} %get-tuple-element.33), channel_id=1, source_target_pairs={{0,2},{1,3},{2,0},{3,1},{4,6},{5,7},{6,4},{7,5},{8,10},{9,11},{10,... | collective-permute-start | bytes 147464 | tf_op jit(solution)/shard_map/ppermute | solution.py:382
  31.4 12.2 %collective-permute-start.13 = (bf16[256,768]{1,0:T(8,128)(2,1)S(1)}, bf16[256,768]{1,0:T(8,128)(2,1)S(1)}, u32[]{:S(2)}, u32[]{:S(2)}) collective-permute-start(bf16[256,768]{1,0:T(8,128)(2,1)S(1)} %join.11), channel_id=1, source_target_pairs={{0,4},{1,5},{2,6},{3,7},{4,0},{5,1},{6,2},{7,3},{8,12},{9,13},{10,... | collective-permute-start | bytes 1179656 | tf_op jit(solution)/shard_map/ppermute | solution.py:382
  32.3 12.3 %collective-permute-start.12 = (bf16[256,768]{1,0:T(8,128)(2,1)S(1)}, bf16[256,768]{1,0:T(8,128)(2,1)S(1)}, u32[]{:S(2)}, u32[]{:S(2)}) collective-permute-start(bf16[256,768]{1,0:T(8,128)(2,1)S(1)} %join.10), channel_id=1, source_target_pairs={{0,1},{1,0},{2,3},{3,2},{4,5},{5,4},{6,7},{7,6},{8,9},{9,8},{10,11... | collective-permute-start | bytes 1179656 | tf_op jit(solution)/shard_map/ppermute | solution.py:382
  32.9 4.5 %collective-permute-start.1 = (f32[16,768]{1,0:T(8,128)S(1)}, f32[16,768]{1,0:T(8,128)S(1)}, u32[]{:S(2)}, u32[]{:S(2)}) collective-permute-start(f32[16,768]{1,0:T(8,128)S(1)} %add.5.refs_0_.refs_2_), channel_id=1, source_target_pairs={{0,8},{1,9},{2,10},{3,11},{4,12},{5,13},{6,14},{7,15},{8,0},{9,1},... | collective-permute-start | bytes 147464 | tf_op jit(solution)/shard_map/ppermute | solution.py:382
  37.4 5.0 %collective-permute-start.6 = (f32[16,768]{1,0:T(8,128)S(1)}, f32[16,768]{1,0:T(8,128)S(1)}, u32[]{:S(2)}, u32[]{:S(2)}) collective-permute-start(f32[16,768]{1,0:T(8,128)S(1)} %add.6.refs_0_), channel_id=1, source_target_pairs={{0,16},{1,17},{2,18},{3,19},{4,20},{5,21},{6,22},{7,23},{8,24},{9,... | collective-permute-start | bytes 147464 | tf_op jit(solution)/shard_map/ppermute | solution.py:382
  42.5 4.2 %collective-permute-start.9 = (f32[16,768]{1,0:T(8,128)S(1)}, f32[16,768]{1,0:T(8,128)S(1)}, u32[]{:S(2)}, u32[]{:S(2)}) collective-permute-start(f32[16,768]{1,0:T(8,128)S(1)} %add.7.refs_0_.refs_1_), channel_id=1, source_target_pairs={{0,1},{1,0},{2,3},{3,2},{4,5},{5,4},{6,7},{7,6},{8,9},{9,8},{10,11... | collective-permute-start | bytes 147464 | tf_op jit(solution)/shard_map/ppermute | solution.py:382
  43.7 6.1 %collective-permute-start.14 = (bf16[64,768]{1,0:T(8,128)(2,1)S(1)}, bf16[64,768]{1,0:T(8,128)(2,1)S(1)}, u32[]{:S(2)}, u32[]{:S(2)}) collective-permute-start(bf16[64,768]{1,0:T(8,128)(2,1)S(1)} %join.12), channel_id=1, source_target_pairs={{0,1},{1,0},{2,3},{3,2},{4,5},{5,4},{6,7},{7,6},{8,9},{9,8},{10,11... | collective-permute-start | bytes 294920 | tf_op jit(solution)/shard_map/ppermute | solution.py:382
  44.6 5.1 %collective-permute-start.15 = (bf16[64,768]{1,0:T(8,128)(2,1)S(1)}, bf16[64,768]{1,0:T(8,128)(2,1)S(1)}, u32[]{:S(2)}, u32[]{:S(2)}) collective-permute-start(bf16[64,768]{1,0:T(8,128)(2,1)S(1)} %join.13), channel_id=1, source_target_pairs={{0,4},{1,5},{2,6},{3,7},{4,0},{5,1},{6,2},{7,3},{8,12},{9,13},{10,... | collective-permute-start | bytes 294920 | tf_op jit(solution)/shard_map/ppermute | solution.py:382
  46.6 4.2 %collective-permute-start.11 = (f32[16,768]{1,0:T(8,128)S(1)}, f32[16,768]{1,0:T(8,128)S(1)}, u32[]{:S(2)}, u32[]{:S(2)}) collective-permute-start(f32[16,768]{1,0:T(8,128)S(1)} %add.8.refs_0_), channel_id=1, source_target_pairs={{0,4},{1,5},{2,6},{3,7},{4,0},{5,1},{6,2},{7,3},{8,12},{9,13},{10,... | collective-permute-start | bytes 147464 | tf_op jit(solution)/shard_map/ppermute | solution.py:382
  53.7 2.3 %collective-permute-start.17 = (bf16[400,768]{1,0:T(8,128)(2,1)S(1)}, bf16[400,768]{1,0:T(8,128)(2,1)S(1)}, u32[]{:S(2)}, u32[]{:S(2)}) collective-permute-start(bf16[400,768]{1,0:T(8,128)(2,1)S(1)} %get-tuple-element.56.refs_0_.refs_2_), channel_id=1, source_target_pairs={{0,2},{1,3},{2,0},{3,1},{4,6},{5,7},{6,4},{7,5},{8,10},{9,11},{10,... | collective-permute-start | bytes 1843208 | tf_op jit(solution)/shard_map/ppermute | solution.py:382
  55.5 2.2 %collective-permute-start.16 = (bf16[400,768]{1,0:T(8,128)(2,1)S(1)}, bf16[400,768]{1,0:T(8,128)(2,1)S(1)}, u32[]{:S(2)}, u32[]{:S(2)}) collective-permute-start(bf16[400,768]{1,0:T(8,128)(2,1)S(1)} %more.1.refs_0_), channel_id=1, source_target_pairs={{0,2},{1,3},{2,0},{3,1},{4,6},{5,7},{6,4},{7,5},{8,10},{9,11},{10,... | collective-permute-start | bytes 1843208 | tf_op jit(solution)/shard_map/ppermute | solution.py:382

commit v6 on v5

--- a/solution.py
+++ b/solution.py
@@ -221,16 +221,23 @@
     other_ref[...] = part[pl.ds(pl.multiple_of((1 - kind) * half, half), half), :]
 
 
-def share(first, acts, d_pre, factors, gains, weight_ref, out_ref, act):
+def share(first, acts, d_pre, factors, gains, weight_ref, out_ref, act, fill=None):
     half, width = act.shape[1], d_pre.shape[1]
     columns = pl.ds(first, half)
-    base = 0
-    for ref in acts:
+    left, right = factors
+    total = lax.dot_general(left[:, columns], right[...], (((0,), (0,)), ((), ())), preferred_element_type=f32)
+    base = cut = 0
+    for k, ref in enumerate(acts):
+        if fill is not None:
+            fill(k)
         act[pl.ds(base, ref.shape[0]), :] = ref[:, columns]
         base += ref.shape[0]
-    left, right = factors
-    even = lax.dot_general(left[:, columns], right[...], (((0,), (0,)), ((), ())), preferred_element_type=f32)
-    total = even + lax.dot_general(act[...], d_pre[...], (((0,), (0,)), ((), ())), preferred_element_type=f32)
+        if base - cut >= act.shape[0] // 2 or base == act.shape[0]:
+            part = pl.ds(cut, base - cut)
+            total = total + lax.dot_general(
+                act[part, :], d_pre[part, :], (((0,), (0,)), ((), ())), preferred_element_type=f32
+            )
+            cut = base
     out_ref[:half, :] = total.astype(bf16)
     weighed = total * weight_ref[columns, :].astype(f32)
     lanes = weighed[:, :128]
@@ -281,13 +288,16 @@
     even_low = (even - even_top.astype(f32)).astype(bf16)
     left[...] = jnp.concatenate([sums_top, sums_top, sums_low], axis=0)
     right[...] = jnp.concatenate([even_top, even_low, even_top], axis=0)
-    base = 0
-    for (_, tilt_ref, _), group in zip(groups, places, strict=True):
-        for d, at in enumerate(group):
-            d_pre[pl.ds(base, seq), :] = (tilt_ref[d * seq : (d + 1) * seq, :] * spreads[pl.ds(at, 1), :]).astype(bf16)
-            base += seq
+    starts = [seq * sum(len(group) for group in masks[:g]) for g in range(len(masks))]
+
+    def fill(g):
+        tilt_ref = groups[g][1]
+        for d, at in enumerate(places[g]):
+            rows = pl.ds(d * seq, seq)
+            d_pre[pl.ds(starts[g] + d * seq, seq), :] = (tilt_ref[rows, :] * spreads[pl.ds(at, 1), :]).astype(bf16)
+
     acts = [act_ref for act_ref, _, _ in groups]
-    gain_in = share(0, acts, d_pre, (left, right), gains_ref[0:1, :], weight_ref, out_ref, act)
+    gain_in = share(0, acts, d_pre, (left, right), gains_ref[0:1, :], weight_ref, out_ref, act, fill)
     out_ref[half:, :] = terms([jnp.sum(row * normed, axis=0, keepdims=True), gain_in])
     copy.wait()
 

time: 59.1 us -> 59 us (level)
  no operation moved by 1% of the time
where the time goes in v6:
time: 59 us; the launch traced here: 58.8 us
  starting transfers between devices  23.3 us (39%)
  Pallas kernels  17 us (29%)
  blocking collectives  10.1 us (17%)
  waiting for transfers between devices  4.11 us (7%)
  local copies, waits for them, and re-layouts  3.56 us (6%)
  between operations  0.8 us (1%)
    ppermute x18, starting transfers between devices, swap(): return lax.ppermute(value, AXES, [(i, i ^ mask) for i in range(count)])  23.3 us
    all_to_all x1, blocking collectives, gathered(): lax.all_to_all(copies, AXES, split_axis=0, concat_axis=0, tiled=True, axi...  10.1 us
    pallas_call x5, Pallas kernels, encode_call(): pl.pallas_call(functools.partial(encode_kernel, layout), out_shape=encode...  7.98 us
    ppermute x18, waiting for transfers between devices, swap(): return lax.ppermute(value, AXES, [(i, i ^ mask) for i in range(count)])  4.11 us
    unnamed x16, local copies, waits for them, and re-layouts  3.56 us
    pallas_call x1, Pallas kernels, back_calls(): pl.pallas_call(functools.partial(back_kernel, seq, masks), out_shape=[sha...  2.87 us
    pallas_call x2, Pallas kernels, final_call(): pl.pallas_call(functools.partial(final_kernel, first), out_shape=[jax.Sha...  2.18 us
    pallas_call x1, Pallas kernels, back_calls(): pl.pallas_call(more_kernel, out_shape=share_shape, scratch_shapes=[act],...  1.73 us
  transfers between devices with their start and end apart: 18, of which 6 were waited for; matrix products, arithmetic and copies ran while one was open for 0% of the time, Pallas kernels for 22%

profile of v6, /device:TPU:0, one launch (start us, length us, event | category | flops | bytes accessed | tf_op | source)
XLA Modules:
  0.0 58.8 jit_solution(879393259762862607)
XLA Ops:
  0.6 3.1 %collective-permute-start.3 = (bf16[128,768]{1,0:T(8,128)(2,1)}, bf16[128,768]{1,0:T(8,128)(2,1)S(1)}, u32[]{:S(2)}, u32[]{:S(2)}) collective-permute-start(bf16[128,768]{1,0:T(8,128)(2,1)} %bitcast.1), channel_id=1, source_target_pairs={{0,8},{1,9},{2,10},{3,11},{4,12},{5,13},{6,14},{7,15},{8,0},{9,1},... | collective-permute-start | bytes 589832 | tf_op jit(solution)/shard_map/ppermute | solution.py:392
  3.7 2.6 %collective-permute-start.2 = (bf16[128,768]{1,0:T(8,128)(2,1)}, bf16[128,768]{1,0:T(8,128)(2,1)S(1)}, u32[]{:S(2)}, u32[]{:S(2)}) collective-permute-start(bf16[128,768]{1,0:T(8,128)(2,1)} %bitcast.2), channel_id=1, source_target_pairs={{0,16},{1,17},{2,18},{3,19},{4,20},{5,21},{6,22},{7,23},{8,24},{9,... | collective-permute-start | bytes 589832 | tf_op jit(solution)/shard_map/ppermute | solution.py:392
  6.3 1.5 %collective-permute-start.5 = (bf16[128,768]{1,0:T(8,128)(2,1)}, bf16[128,768]{1,0:T(8,128)(2,1)S(1)}, u32[]{:S(2)}, u32[]{:S(2)}) collective-permute-start(bf16[128,768]{1,0:T(8,128)(2,1)} %bitcast.3), channel_id=1, source_target_pairs={{0,4},{1,5},{2,6},{3,7},{4,0},{5,1},{6,2},{7,3},{8,12},{9,13},{10,... | collective-permute-start | bytes 589832 | tf_op jit(solution)/shard_map/ppermute | solution.py:392
  7.8 1.5 %collective-permute-start.4 = (bf16[128,768]{1,0:T(8,128)(2,1)}, bf16[128,768]{1,0:T(8,128)(2,1)S(1)}, u32[]{:S(2)}, u32[]{:S(2)}) collective-permute-start(bf16[128,768]{1,0:T(8,128)(2,1)} %bitcast.4), channel_id=1, source_target_pairs={{0,1},{1,0},{2,3},{3,2},{4,5},{5,4},{6,7},{7,6},{8,9},{9,8},{10,11... | collective-permute-start | bytes 589832 | tf_op jit(solution)/shard_map/ppermute | solution.py:392
  9.3 1.3 %copy-done = bf16[768,768]{1,0:T(8,128)(2,1)S(1)} copy-done((bf16[768,768]{1,0:T(8,128)(2,1)S(1)}, bf16[768,768]{1,0:T(8,128)(2,1)}, u32[]{:S(2)}) %copy-start) | copy-done | bytes 1179672
  10.6 0.7 %copy-done.3 = f32[2,768]{1,0:T(2,128)S(1)} copy-done((f32[2,768]{1,0:T(2,128)S(1)}, f32[2,768]{1,0:T(2,128)}, u32[]{:S(2)}) %copy-start.3) | copy-done | bytes 6168
  11.3 0.9 %copy-done.5 = bf16[1,128,768]{2,1,0:T(8,128)(2,1)S(1)} copy-done((bf16[1,128,768]{2,1,0:T(8,128)(2,1)S(1)}, bf16[1,128,768]{2,1,0:T(8,128)(2,1)}, u32[]{:S(2)}) %copy-start.5) | copy-done | bytes 196632
  12.2 0.7 %copy-done.7 = s32[1,8]{1,0:T(1,128)S(1)} copy-done((s32[1,8]{1,0:T(1,128)S(1)}, s32[1,8]{1,0:T(1,128)}, u32[]{:S(2)}) %copy-start.7) | copy-done | bytes 56
  12.9 1.3 %first.1 = (bf16[128,768]{1,0:T(8,128)(2,1)S(1)}, f32[128,768]{1,0:T(8,128)S(1)}, f32[1,8,768]{2,1,0:T(8,128)S(1)}, bf16[32,8,128]{2,1,0:T(8,128)(2,1)S(1)}) custom-call(bf16[128,768]{1,0:T(8,128)(2,1)S(1)} %bitcast.5, f32[2,768]{1,0:T(2,128)S(1)} %copy-done.3, bf16[768,768]{1,0:T(8,128)(2,1)S(1)} %copy-done, s32[1,8]{1,0:T(1,128)S(1)} %copy-done.7), custom_call_target="tpu_custom_call" | custom-call | tf_op jit(solution)/shard_map/first/pallas_call | solution.py:120
  14.2 1.3 %collective-permute-done.2.refs_0_.refs_1_ = bf16[128,768]{1,0:T(8,128)(2,1)S(1)} collective-permute-done((bf16[128,768]{1,0:T(8,128)(2,1)}, bf16[128,768]{1,0:T(8,128)(2,1)S(1)}, u32[]{:S(2)}, u32[]{:S(2)}) %collective-permute-start.2) | collective-permute-done | bytes 196640 | tf_op jit(solution)/shard_map/ppermute | solution.py:392
  15.5 1.6 %collective-permute-start.7 = (bf16[320,768]{1,0:T(8,128)(2,1)S(1)}, bf16[320,768]{1,0:T(8,128)(2,1)S(1)}, u32[]{:S(2)}, u32[]{:S(2)}) collective-permute-start(bf16[320,768]{1,0:T(8,128)(2,1)S(1)} %join.7), channel_id=1, source_target_pairs={{0,1},{1,0},{2,3},{3,2},{4,5},{5,4},{6,7},{7,6},{8,9},{9,8},{10,11... | collective-permute-start | bytes 1474568 | tf_op jit(solution)/shard_map/ppermute | solution.py:392
  17.2 1.6 %collective-permute-start.8 = (bf16[320,768]{1,0:T(8,128)(2,1)S(1)}, bf16[320,768]{1,0:T(8,128)(2,1)S(1)}, u32[]{:S(2)}, u32[]{:S(2)}) collective-permute-start(bf16[320,768]{1,0:T(8,128)(2,1)S(1)} %join.8), channel_id=1, source_target_pairs={{0,4},{1,5},{2,6},{3,7},{4,0},{5,1},{6,2},{7,3},{8,12},{9,13},{10,... | collective-permute-start | bytes 1474568 | tf_op jit(solution)/shard_map/ppermute | solution.py:392
  19.2 10.1 %all_to_all.5.rows_ref = bf16[32,8,128]{2,1,0:T(8,128)(2,1)S(1)} all-to-all(bf16[32,8,128]{2,1,0:T(8,128)(2,1)S(1)} %get-tuple-element.31), channel_id=1, replica_groups={{0,1,4,5,8,9,12,13,16,17,20,21,24,25,28,29,2,3,6,7,10,11,14,15,18,19,22..., dimensions={0} | all-to-all | bytes 131072 | tf_op jit(solution)/shard_map/all_to_all | solution.py:462
  29.3 0.7 %head.1 = (f32[16,768]{1,0:T(8,128)S(1)}, f32[16,768]{1,0:T(8,128)S(1)}) custom-call(bf16[32,8,128]{2,1,0:T(8,128)(2,1)S(1)} %all_to_all.5.rows_ref, bf16[512,768]{1,0:T(8,128)(2,1)S(1)} %copy-done.2, bf16[512]{0:T(512)(128)(2,1)S(1)} %copy-done.6), custom_call_target="tpu_custom_call" | custom-call | tf_op jit(solution)/shard_map/head/pallas_call | solution.py:475
  30.1 1.2 %collective-permute-done.refs_1_ = f32[16,768]{1,0:T(8,128)S(1)} collective-permute-done((f32[16,768]{1,0:T(8,128)S(1)}, f32[16,768]{1,0:T(8,128)S(1)}, u32[]{:S(2)}, u32[]{:S(2)}) %collective-permute-start) | collective-permute-done | bytes 49184 | tf_op jit(solution)/shard_map/ppermute | solution.py:392
  31.4 0.9 %collective-permute-start.13 = (bf16[256,768]{1,0:T(8,128)(2,1)S(1)}, bf16[256,768]{1,0:T(8,128)(2,1)S(1)}, u32[]{:S(2)}, u32[]{:S(2)}) collective-permute-start(bf16[256,768]{1,0:T(8,128)(2,1)S(1)} %join.11), channel_id=1, source_target_pairs={{0,4},{1,5},{2,6},{3,7},{4,0},{5,1},{6,2},{7,3},{8,12},{9,13},{10,... | collective-permute-start | bytes 1179656 | tf_op jit(solution)/shard_map/ppermute | solution.py:392
  32.9 2.4 %collective-permute-start.1 = (f32[16,768]{1,0:T(8,128)S(1)}, f32[16,768]{1,0:T(8,128)S(1)}, u32[]{:S(2)}, u32[]{:S(2)}) collective-permute-start(f32[16,768]{1,0:T(8,128)S(1)} %add.5.refs_0_.refs_2_), channel_id=1, source_target_pairs={{0,8},{1,9},{2,10},{3,11},{4,12},{5,13},{6,14},{7,15},{8,0},{9,1},... | collective-permute-start | bytes 147464 | tf_op jit(solution)/shard_map/ppermute | solution.py:392
  35.3 2.0 %encode.5 = (bf16[512,768]{1,0:T(8,128)(2,1)S(1)}, f32[512,768]{1,0:T(8,128)S(1)}, f32[4,8,768]{2,1,0:T(8,128)S(1)}) custom-call(bf16[128,768]{1,0:T(8,128)(2,1)S(1)} %collective-permute-done.2.refs_0_.refs_1_, bf16[128,768]{1,0:T(8,128)(2,1)S(1)} %collective-permute-done.3.refs_1_.refs_0_, bf16[128,768]{1,0:T(8,128)(2,1)S(1)} %collective-permute-done.4.refs_2_, ...), custom_call_target="tpu_custom_call" | custom-call | tf_op jit(solution)/shard_map/encode/pallas_call | solution.py:133
  37.4 2.0 %collective-permute-start.6 = (f32[16,768]{1,0:T(8,128)S(1)}, f32[16,768]{1,0:T(8,128)S(1)}, u32[]{:S(2)}, u32[]{:S(2)}) collective-permute-start(f32[16,768]{1,0:T(8,128)S(1)} %add.6.refs_0_), channel_id=1, source_target_pairs={{0,16},{1,17},{2,18},{3,19},{4,20},{5,21},{6,22},{7,23},{8,24},{9,... | collective-permute-start | bytes 147464 | tf_op jit(solution)/shard_map/ppermute | solution.py:392
  39.4 2.4 %encode.6 = (bf16[640,768]{1,0:T(8,128)(2,1)S(1)}, f32[640,768]{1,0:T(8,128)S(1)}, f32[5,8,768]{2,1,0:T(8,128)S(1)}) custom-call(bf16[320,768]{1,0:T(8,128)(2,1)S(1)} %collective-permute-done.7.refs_0_.refs_1_, bf16[320,768]{1,0:T(8,128)(2,1)S(1)} %collective-permute-done.8.refs_1_, f32[2,768]{1,0:T(2,128)S(1)} %copy-done.4, bf16[768,768]{1,0:T(8,128)(2,1)S(1)} %copy-done.1), custom_call_target="tpu_custom_call" | custom-call | tf_op jit(solution)/shard_map/encode/pallas_call | solution.py:133
  41.8 0.7 %collective-permute-done.6.refs_1_ = f32[16,768]{1,0:T(8,128)S(1)} collective-permute-done((f32[16,768]{1,0:T(8,128)S(1)}, f32[16,768]{1,0:T(8,128)S(1)}, u32[]{:S(2)}, u32[]{:S(2)}) %collective-permute-start.6) | collective-permute-done | bytes 49184 | tf_op jit(solution)/shard_map/ppermute | solution.py:392
  42.5 1.2 %collective-permute-start.9 = (f32[16,768]{1,0:T(8,128)S(1)}, f32[16,768]{1,0:T(8,128)S(1)}, u32[]{:S(2)}, u32[]{:S(2)}) collective-permute-start(f32[16,768]{1,0:T(8,128)S(1)} %add.7.refs_0_.refs_1_), channel_id=1, source_target_pairs={{0,1},{1,0},{2,3},{3,2},{4,5},{5,4},{6,7},{7,6},{8,9},{9,8},{10,11... | collective-permute-start | bytes 147464 | tf_op jit(solution)/shard_map/ppermute | solution.py:392
  43.7 1.0 %collective-permute-start.14 = (bf16[64,768]{1,0:T(8,128)(2,1)S(1)}, bf16[64,768]{1,0:T(8,128)(2,1)S(1)}, u32[]{:S(2)}, u32[]{:S(2)}) collective-permute-start(bf16[64,768]{1,0:T(8,128)(2,1)S(1)} %join.12), channel_id=1, source_target_pairs={{0,1},{1,0},{2,3},{3,2},{4,5},{5,4},{6,7},{7,6},{8,9},{9,8},{10,11... | collective-permute-start | bytes 294920 | tf_op jit(solution)/shard_map/ppermute | solution.py:392
  44.6 1.1 %collective-permute-start.15 = (bf16[64,768]{1,0:T(8,128)(2,1)S(1)}, bf16[64,768]{1,0:T(8,128)(2,1)S(1)}, u32[]{:S(2)}, u32[]{:S(2)}) collective-permute-start(bf16[64,768]{1,0:T(8,128)(2,1)S(1)} %join.13), channel_id=1, source_target_pairs={{0,4},{1,5},{2,6},{3,7},{4,0},{5,1},{6,2},{7,3},{8,12},{9,13},{10,... | collective-permute-start | bytes 294920 | tf_op jit(solution)/shard_map/ppermute | solution.py:392
  45.8 0.8 %encode.7 = (bf16[128,768]{1,0:T(8,128)(2,1)S(1)}, f32[128,768]{1,0:T(8,128)S(1)}, f32[1,8,768]{2,1,0:T(8,128)S(1)}) custom-call(bf16[128,768]{1,0:T(8,128)(2,1)S(1)} %collective-permute-done.10.refs_0_, f32[2,768]{1,0:T(2,128)S(1)} %copy-done.4, bf16[768,768]{1,0:T(8,128)(2,1)S(1)} %copy-done.1), custom_call_target="tpu_custom_call" | custom-call | tf_op jit(solution)/shard_map/encode/pallas_call | solution.py:133
  46.6 1.1 %collective-permute-start.11 = (f32[16,768]{1,0:T(8,128)S(1)}, f32[16,768]{1,0:T(8,128)S(1)}, u32[]{:S(2)}, u32[]{:S(2)}) collective-permute-start(f32[16,768]{1,0:T(8,128)S(1)} %add.8.refs_0_), channel_id=1, source_target_pairs={{0,4},{1,5},{2,6},{3,7},{4,0},{5,1},{6,2},{7,3},{8,12},{9,13},{10,... | collective-permute-start | bytes 147464 | tf_op jit(solution)/shard_map/ppermute | solution.py:392
  47.7 2.0 %encode.8 = (bf16[512,768]{1,0:T(8,128)(2,1)S(1)}, f32[512,768]{1,0:T(8,128)S(1)}, f32[4,8,768]{2,1,0:T(8,128)S(1)}) custom-call(bf16[256,768]{1,0:T(8,128)(2,1)S(1)} %collective-permute-done.12.refs_0_, bf16[256,768]{1,0:T(8,128)(2,1)S(1)} %collective-permute-done.13.refs_1_.refs_0_, f32[2,768]{1,0:T(2,128)S(1)} %copy-done.4, bf16[768,768]{1,0:T(8,128)(2,1)S(1)} %copy-done.1), custom_call_target="tpu_custom_call" | custom-call | tf_op jit(solution)/shard_map/encode/pallas_call | solution.py:133
  49.8 0.8 %encode.9 = (bf16[128,768]{1,0:T(8,128)(2,1)S(1)}, f32[128,768]{1,0:T(8,128)S(1)}, f32[1,8,768]{2,1,0:T(8,128)S(1)}) custom-call(bf16[64,768]{1,0:T(8,128)(2,1)S(1)} %collective-permute-done.14.refs_0_, bf16[64,768]{1,0:T(8,128)(2,1)S(1)} %collective-permute-done.15.refs_1_, f32[2,768]{1,0:T(2,128)S(1)} %copy-done.4, bf16[768,768]{1,0:T(8,128)(2,1)S(1)} %copy-done.1), custom_call_target="tpu_custom_call" | custom-call | tf_op jit(solution)/shard_map/encode/pallas_call | solution.py:133
  50.8 2.9 %back.1 = (bf16[400,768]{1,0:T(8,128)(2,1)S(1)}, f32[1,768]{1,0:T(1,128)}, bf16[2048,768]{1,0:T(8,128)(2,1)S(1)}, bf16[48,768]{1,0:T(8,128)(2,1)S(1)}, bf16[48,768]{1,0:T(8,128)(2,1)S(1)}) custom-call(f32[16,768]{1,0:T(8,128)S(1)} %add.9.refs_0_, f32[2,768]{1,0:T(2,128)S(1)} %copy-done.4, bf16[768,768]{1,0:T(8,128)(2,1)S(1)} %copy-done.1, ...), custom_call_target="tpu_custom_call" | custom-call | tf_op jit(solution)/shard_map/back/pallas_call | solution.py:317
  53.7 1.7 %more.1.refs_0_ = bf16[400,768]{1,0:T(8,128)(2,1)S(1)} custom-call(f32[2,768]{1,0:T(2,128)S(1)} %copy-done.4, bf16[768,768]{1,0:T(8,128)(2,1)S(1)} %copy-done.1, bf16[2048,768]{1,0:T(8,128)(2,1)S(1)} %get-tuple-element.53.refs_2_, bf16[48,768]{1,0:T(8,128)(2,1)S(1)} %get-tuple-element.54.refs_3_, bf16[48,768]{1,0:T(8,128)(2,1)S(1)} %get-tuple-element.55.refs_4_, ...), custom_call_target="tpu_custom_call" | custom-call | tf_op jit(solution)/shard_map/more/pallas_call | solution.py:337
  56.0 1.1 %final.2.refs_4_ = f32[768,768]{1,0:T(8,128)} custom-call(bf16[400,768]{1,0:T(8,128)(2,1)S(1)} %get-tuple-element.56.refs_0_.refs_2_, bf16[400,768]{1,0:T(8,128)(2,1)S(1)} %collective-permute-done.17.refs_1_.refs_3_), custom_call_target="tpu_custom_call" | custom-call | tf_op jit(solution)/shard_map/final/pallas_call | solution.py:375
  57.7 1.1 %final.3 = (f32[768,768]{1,0:T(8,128)}, f32[2,768]{1,0:T(2,128)}) custom-call(bf16[400,768]{1,0:T(8,128)(2,1)S(1)} %more.1.refs_0_, bf16[400,768]{1,0:T(8,128)(2,1)S(1)} %collective-permute-done.16.refs_1_, bf16[400,768]{1,0:T(8,128)(2,1)S(1)} %get-tuple-element.56.refs_0_.refs_2_, ...), custom_call_target="tpu_custom_call", output_to_operand_aliasing={{0}: (4, {})} | custom-call | tf_op jit(solution)/shard_map/final/pallas_call | solution.py:375
  (45 shorter events, 3.0 us)
Async XLA Ops:
  0.6 28.7 %copy-start.6 = (bf16[512]{0:T(512)(128)(2,1)S(1)}, bf16[512]{0:T(512)(128)(2,1)}, u32[]{:S(2)}) copy-start(bf16[512]{0:T(512)(128)(2,1)} %bias_ref.1) | copy-start | bytes 3076
  0.6 13.5 %collective-permute-start.3 = (bf16[128,768]{1,0:T(8,128)(2,1)}, bf16[128,768]{1,0:T(8,128)(2,1)S(1)}, u32[]{:S(2)}, u32[]{:S(2)}) collective-permute-start(bf16[128,768]{1,0:T(8,128)(2,1)} %bitcast.1), channel_id=1, source_target_pairs={{0,8},{1,9},{2,10},{3,11},{4,12},{5,13},{6,14},{7,15},{8,0},{9,1},... | collective-permute-start | bytes 589832 | tf_op jit(solution)/shard_map/ppermute | solution.py:392
  3.7 11.7 %collective-permute-start.2 = (bf16[128,768]{1,0:T(8,128)(2,1)}, bf16[128,768]{1,0:T(8,128)(2,1)S(1)}, u32[]{:S(2)}, u32[]{:S(2)}) collective-permute-start(bf16[128,768]{1,0:T(8,128)(2,1)} %bitcast.2), channel_id=1, source_target_pairs={{0,16},{1,17},{2,18},{3,19},{4,20},{5,21},{6,22},{7,23},{8,24},{9,... | collective-permute-start | bytes 589832 | tf_op jit(solution)/shard_map/ppermute | solution.py:392
  6.3 9.2 %collective-permute-start.5 = (bf16[128,768]{1,0:T(8,128)(2,1)}, bf16[128,768]{1,0:T(8,128)(2,1)S(1)}, u32[]{:S(2)}, u32[]{:S(2)}) collective-permute-start(bf16[128,768]{1,0:T(8,128)(2,1)} %bitcast.3), channel_id=1, source_target_pairs={{0,4},{1,5},{2,6},{3,7},{4,0},{5,1},{6,2},{7,3},{8,12},{9,13},{10,... | collective-permute-start | bytes 589832 | tf_op jit(solution)/shard_map/ppermute | solution.py:392
  7.8 9.3 %collective-permute-start.4 = (bf16[128,768]{1,0:T(8,128)(2,1)}, bf16[128,768]{1,0:T(8,128)(2,1)S(1)}, u32[]{:S(2)}, u32[]{:S(2)}) collective-permute-start(bf16[128,768]{1,0:T(8,128)(2,1)} %bitcast.4), channel_id=1, source_target_pairs={{0,1},{1,0},{2,3},{3,2},{4,5},{5,4},{6,7},{7,6},{8,9},{9,8},{10,11... | collective-permute-start | bytes 589832 | tf_op jit(solution)/shard_map/ppermute | solution.py:392
  9.3 1.3 %copy-start = (bf16[768,768]{1,0:T(8,128)(2,1)S(1)}, bf16[768,768]{1,0:T(8,128)(2,1)}, u32[]{:S(2)}) copy-start(bf16[768,768]{1,0:T(8,128)(2,1)} %refs_1_.7) | copy-start | bytes 3538948
  10.6 0.7 %copy-start.3 = (f32[2,768]{1,0:T(2,128)S(1)}, f32[2,768]{1,0:T(2,128)}, u32[]{:S(2)}) copy-start(f32[2,768]{1,0:T(2,128)} %refs_0_.1) | copy-start | bytes 18436
  11.3 0.9 %copy-start.5 = (bf16[1,128,768]{2,1,0:T(8,128)(2,1)S(1)}, bf16[1,128,768]{2,1,0:T(8,128)(2,1)}, u32[]{:S(2)}) copy-start(bf16[1,128,768]{2,1,0:T(8,128)(2,1)} %param.6) | copy-start | bytes 589828
  12.2 0.7 %copy-start.7 = (s32[1,8]{1,0:T(1,128)S(1)}, s32[1,8]{1,0:T(1,128)}, u32[]{:S(2)}) copy-start(s32[1,8]{1,0:T(1,128)} %refs_3_.4) | copy-start | bytes 100
  12.9 16.4 %copy-start.2 = (bf16[512,768]{1,0:T(8,128)(2,1)S(1)}, bf16[512,768]{1,0:T(8,128)(2,1)}, u32[]{:S(2)}) copy-start(bf16[512,768]{1,0:T(8,128)(2,1)} %weight_ref.1) | copy-start | bytes 2359300
  15.5 15.8 %collective-permute-start.7 = (bf16[320,768]{1,0:T(8,128)(2,1)S(1)}, bf16[320,768]{1,0:T(8,128)(2,1)S(1)}, u32[]{:S(2)}, u32[]{:S(2)}) collective-permute-start(bf16[320,768]{1,0:T(8,128)(2,1)S(1)} %join.7), channel_id=1, source_target_pairs={{0,1},{1,0},{2,3},{3,2},{4,5},{5,4},{6,7},{7,6},{8,9},{9,8},{10,11... | collective-permute-start | bytes 1474568 | tf_op jit(solution)/shard_map/ppermute | solution.py:392
  17.1 18.2 %copy-start.1 = (bf16[768,768]{1,0:T(8,128)(2,1)S(1)}, bf16[768,768]{1,0:T(8,128)(2,1)}, u32[]{:S(2)}) copy-start(bf16[768,768]{1,0:T(8,128)(2,1)} %refs_1_.7) | copy-start | bytes 3538948
  17.2 18.2 %copy-start.4 = (f32[2,768]{1,0:T(2,128)S(1)}, f32[2,768]{1,0:T(2,128)}, u32[]{:S(2)}) copy-start(f32[2,768]{1,0:T(2,128)} %refs_0_.1) | copy-start | bytes 18436
  17.2 15.1 %collective-permute-start.8 = (bf16[320,768]{1,0:T(8,128)(2,1)S(1)}, bf16[320,768]{1,0:T(8,128)(2,1)S(1)}, u32[]{:S(2)}, u32[]{:S(2)}) collective-permute-start(bf16[320,768]{1,0:T(8,128)(2,1)S(1)} %join.8), channel_id=1, source_target_pairs={{0,4},{1,5},{2,6},{3,7},{4,0},{5,1},{6,2},{7,3},{8,12},{9,13},{10,... | collective-permute-start | bytes 1474568 | tf_op jit(solution)/shard_map/ppermute | solution.py:392
  18.7 12.6 %collective-permute-start.10 = (bf16[128,768]{1,0:T(8,128)(2,1)S(1)}, bf16[128,768]{1,0:T(8,128)(2,1)S(1)}, u32[]{:S(2)}, u32[]{:S(2)}) collective-permute-start(bf16[128,768]{1,0:T(8,128)(2,1)S(1)} %join.9), channel_id=1, source_target_pairs={{0,8},{1,9},{2,10},{3,11},{4,12},{5,13},{6,14},{7,15},{8,0},{9,1},... | collective-permute-start | bytes 589832 | tf_op jit(solution)/shard_map/ppermute | solution.py:392
  30.0 1.3 %collective-permute-start = (f32[16,768]{1,0:T(8,128)S(1)}, f32[16,768]{1,0:T(8,128)S(1)}, u32[]{:S(2)}, u32[]{:S(2)}) collective-permute-start(f32[16,768]{1,0:T(8,128)S(1)} %get-tuple-element.33), channel_id=1, source_target_pairs={{0,2},{1,3},{2,0},{3,1},{4,6},{5,7},{6,4},{7,5},{8,10},{9,11},{10,... | collective-permute-start | bytes 147464 | tf_op jit(solution)/shard_map/ppermute | solution.py:392
  31.4 12.2 %collective-permute-start.13 = (bf16[256,768]{1,0:T(8,128)(2,1)S(1)}, bf16[256,768]{1,0:T(8,128)(2,1)S(1)}, u32[]{:S(2)}, u32[]{:S(2)}) collective-permute-start(bf16[256,768]{1,0:T(8,128)(2,1)S(1)} %join.11), channel_id=1, source_target_pairs={{0,4},{1,5},{2,6},{3,7},{4,0},{5,1},{6,2},{7,3},{8,12},{9,13},{10,... | collective-permute-start | bytes 1179656 | tf_op jit(solution)/shard_map/ppermute | solution.py:392
  32.3 12.3 %collective-permute-start.12 = (bf16[256,768]{1,0:T(8,128)(2,1)S(1)}, bf16[256,768]{1,0:T(8,128)(2,1)S(1)}, u32[]{:S(2)}, u32[]{:S(2)}) collective-permute-start(bf16[256,768]{1,0:T(8,128)(2,1)S(1)} %join.10), channel_id=1, source_target_pairs={{0,1},{1,0},{2,3},{3,2},{4,5},{5,4},{6,7},{7,6},{8,9},{9,8},{10,11... | collective-permute-start | bytes 1179656 | tf_op jit(solution)/shard_map/ppermute | solution.py:392
  32.9 4.5 %collective-permute-start.1 = (f32[16,768]{1,0:T(8,128)S(1)}, f32[16,768]{1,0:T(8,128)S(1)}, u32[]{:S(2)}, u32[]{:S(2)}) collective-permute-start(f32[16,768]{1,0:T(8,128)S(1)} %add.5.refs_0_.refs_2_), channel_id=1, source_target_pairs={{0,8},{1,9},{2,10},{3,11},{4,12},{5,13},{6,14},{7,15},{8,0},{9,1},... | collective-permute-start | bytes 147464 | tf_op jit(solution)/shard_map/ppermute | solution.py:392
  37.4 5.0 %collective-permute-start.6 = (f32[16,768]{1,0:T(8,128)S(1)}, f32[16,768]{1,0:T(8,128)S(1)}, u32[]{:S(2)}, u32[]{:S(2)}) collective-permute-start(f32[16,768]{1,0:T(8,128)S(1)} %add.6.refs_0_), channel_id=1, source_target_pairs={{0,16},{1,17},{2,18},{3,19},{4,20},{5,21},{6,22},{7,23},{8,24},{9,... | collective-permute-start | bytes 147464 | tf_op jit(solution)/shard_map/ppermute | solution.py:392
  42.5 4.2 %collective-permute-start.9 = (f32[16,768]{1,0:T(8,128)S(1)}, f32[16,768]{1,0:T(8,128)S(1)}, u32[]{:S(2)}, u32[]{:S(2)}) collective-permute-start(f32[16,768]{1,0:T(8,128)S(1)} %add.7.refs_0_.refs_1_), channel_id=1, source_target_pairs={{0,1},{1,0},{2,3},{3,2},{4,5},{5,4},{6,7},{7,6},{8,9},{9,8},{10,11... | collective-permute-start | bytes 147464 | tf_op jit(solution)/shard_map/ppermute | solution.py:392
  43.7 6.1 %collective-permute-start.14 = (bf16[64,768]{1,0:T(8,128)(2,1)S(1)}, bf16[64,768]{1,0:T(8,128)(2,1)S(1)}, u32[]{:S(2)}, u32[]{:S(2)}) collective-permute-start(bf16[64,768]{1,0:T(8,128)(2,1)S(1)} %join.12), channel_id=1, source_target_pairs={{0,1},{1,0},{2,3},{3,2},{4,5},{5,4},{6,7},{7,6},{8,9},{9,8},{10,11... | collective-permute-start | bytes 294920 | tf_op jit(solution)/shard_map/ppermute | solution.py:392
  44.6 5.1 %collective-permute-start.15 = (bf16[64,768]{1,0:T(8,128)(2,1)S(1)}, bf16[64,768]{1,0:T(8,128)(2,1)S(1)}, u32[]{:S(2)}, u32[]{:S(2)}) collective-permute-start(bf16[64,768]{1,0:T(8,128)(2,1)S(1)} %join.13), channel_id=1, source_target_pairs={{0,4},{1,5},{2,6},{3,7},{4,0},{5,1},{6,2},{7,3},{8,12},{9,13},{10,... | collective-permute-start | bytes 294920 | tf_op jit(solution)/shard_map/ppermute | solution.py:392
  46.6 4.2 %collective-permute-start.11 = (f32[16,768]{1,0:T(8,128)S(1)}, f32[16,768]{1,0:T(8,128)S(1)}, u32[]{:S(2)}, u32[]{:S(2)}) collective-permute-start(f32[16,768]{1,0:T(8,128)S(1)} %add.8.refs_0_), channel_id=1, source_target_pairs={{0,4},{1,5},{2,6},{3,7},{4,0},{5,1},{6,2},{7,3},{8,12},{9,13},{10,... | collective-permute-start | bytes 147464 | tf_op jit(solution)/shard_map/ppermute | solution.py:392
  53.7 2.4 %collective-permute-start.17 = (bf16[400,768]{1,0:T(8,128)(2,1)S(1)}, bf16[400,768]{1,0:T(8,128)(2,1)S(1)}, u32[]{:S(2)}, u32[]{:S(2)}) collective-permute-start(bf16[400,768]{1,0:T(8,128)(2,1)S(1)} %get-tuple-element.56.refs_0_.refs_2_), channel_id=1, source_target_pairs={{0,2},{1,3},{2,0},{3,1},{4,6},{5,7},{6,4},{7,5},{8,10},{9,11},{10,... | collective-permute-start | bytes 1843208 | tf_op jit(solution)/shard_map/ppermute | solution.py:392
  55.5 2.2 %collective-permute-start.16 = (bf16[400,768]{1,0:T(8,128)(2,1)S(1)}, bf16[400,768]{1,0:T(8,128)(2,1)S(1)}, u32[]{:S(2)}, u32[]{:S(2)}) collective-permute-start(bf16[400,768]{1,0:T(8,128)(2,1)S(1)} %more.1.refs_0_), channel_id=1, source_target_pairs={{0,2},{1,3},{2,0},{3,1},{4,6},{5,7},{6,4},{7,5},{8,10},{9,11},{10,... | collective-permute-start | bytes 1843208 | tf_op jit(solution)/shard_map/ppermute | solution.py:392

commit v7 on v5

--- a/solution.py
+++ b/solution.py
@@ -359,7 +359,7 @@
 
 def final_call(first, shares, before=None):
     rows, width = shares[0].shape[0] - 16, shares[0].shape[1]
-    steps = 4 if rows % 64 == 0 else 1
+    steps = 8 if rows % 128 == 0 else 1
     vmem, hbm = pl.BlockSpec(memory_space=pltpu.VMEM), pl.BlockSpec(memory_space=pltpu.HBM)
     extra = [] if before is None else [before]
     return pl.pallas_call(

time: 59.1 us -> 59.1 us (level)
  no operation moved by 1% of the time
where the time goes in v7:
time: 59.1 us; the launch traced here: 58.8 us
  starting transfers between devices  23.3 us (39%)
  Pallas kernels  17 us (29%)
  blocking collectives  10.1 us (17%)
  waiting for transfers between devices  4.09 us (7%)
  local copies, waits for them, and re-layouts  3.56 us (6%)
  between operations  0.8 us (1%)
    ppermute x18, starting transfers between devices, swap(): return lax.ppermute(value, AXES, [(i, i ^ mask) for i in range(count)])  23.3 us
    all_to_all x1, blocking collectives, gathered(): lax.all_to_all(copies, AXES, split_axis=0, concat_axis=0, tiled=True, axi...  10.1 us
    pallas_call x5, Pallas kernels, encode_call(): pl.pallas_call(functools.partial(encode_kernel, layout), out_shape=encode...  7.98 us
    ppermute x18, waiting for transfers between devices, swap(): return lax.ppermute(value, AXES, [(i, i ^ mask) for i in range(count)])  4.09 us
    unnamed x16, local copies, waits for them, and re-layouts  3.56 us
    pallas_call x1, Pallas kernels, back_calls(): pl.pallas_call(functools.partial(back_kernel, seq, masks), out_shape=[sha...  2.94 us
    pallas_call x2, Pallas kernels, final_call(): pl.pallas_call(functools.partial(final_kernel, first), out_shape=[jax.Sha...  2.21 us
    pallas_call x1, Pallas kernels, back_calls(): pl.pallas_call(more_kernel, out_shape=share_shape, scratch_shapes=[act],...  1.69 us
  transfers between devices with their start and end apart: 18, of which 6 were waited for; matrix products, arithmetic and copies ran while one was open for 0% of the time, Pallas kernels for 22%

profile of v7, /device:TPU:0, one launch (start us, length us, event | category | flops | bytes accessed | tf_op | source)
XLA Modules:
  0.0 58.8 jit_solution(1562012268273923145)
XLA Ops:
  0.6 3.1 %collective-permute-start.3 = (bf16[128,768]{1,0:T(8,128)(2,1)}, bf16[128,768]{1,0:T(8,128)(2,1)S(1)}, u32[]{:S(2)}, u32[]{:S(2)}) collective-permute-start(bf16[128,768]{1,0:T(8,128)(2,1)} %bitcast.1), channel_id=1, source_target_pairs={{0,8},{1,9},{2,10},{3,11},{4,12},{5,13},{6,14},{7,15},{8,0},{9,1},... | collective-permute-start | bytes 589832 | tf_op jit(solution)/shard_map/ppermute | solution.py:382
  3.7 2.6 %collective-permute-start.2 = (bf16[128,768]{1,0:T(8,128)(2,1)}, bf16[128,768]{1,0:T(8,128)(2,1)S(1)}, u32[]{:S(2)}, u32[]{:S(2)}) collective-permute-start(bf16[128,768]{1,0:T(8,128)(2,1)} %bitcast.2), channel_id=1, source_target_pairs={{0,16},{1,17},{2,18},{3,19},{4,20},{5,21},{6,22},{7,23},{8,24},{9,... | collective-permute-start | bytes 589832 | tf_op jit(solution)/shard_map/ppermute | solution.py:382
  6.3 1.5 %collective-permute-start.5 = (bf16[128,768]{1,0:T(8,128)(2,1)}, bf16[128,768]{1,0:T(8,128)(2,1)S(1)}, u32[]{:S(2)}, u32[]{:S(2)}) collective-permute-start(bf16[128,768]{1,0:T(8,128)(2,1)} %bitcast.3), channel_id=1, source_target_pairs={{0,4},{1,5},{2,6},{3,7},{4,0},{5,1},{6,2},{7,3},{8,12},{9,13},{10,... | collective-permute-start | bytes 589832 | tf_op jit(solution)/shard_map/ppermute | solution.py:382
  7.8 1.5 %collective-permute-start.4 = (bf16[128,768]{1,0:T(8,128)(2,1)}, bf16[128,768]{1,0:T(8,128)(2,1)S(1)}, u32[]{:S(2)}, u32[]{:S(2)}) collective-permute-start(bf16[128,768]{1,0:T(8,128)(2,1)} %bitcast.4), channel_id=1, source_target_pairs={{0,1},{1,0},{2,3},{3,2},{4,5},{5,4},{6,7},{7,6},{8,9},{9,8},{10,11... | collective-permute-start | bytes 589832 | tf_op jit(solution)/shard_map/ppermute | solution.py:382
  9.3 1.3 %copy-done = bf16[768,768]{1,0:T(8,128)(2,1)S(1)} copy-done((bf16[768,768]{1,0:T(8,128)(2,1)S(1)}, bf16[768,768]{1,0:T(8,128)(2,1)}, u32[]{:S(2)}) %copy-start) | copy-done | bytes 1179672
  10.6 0.7 %copy-done.3 = f32[2,768]{1,0:T(2,128)S(1)} copy-done((f32[2,768]{1,0:T(2,128)S(1)}, f32[2,768]{1,0:T(2,128)}, u32[]{:S(2)}) %copy-start.3) | copy-done | bytes 6168
  11.3 0.9 %copy-done.5 = bf16[1,128,768]{2,1,0:T(8,128)(2,1)S(1)} copy-done((bf16[1,128,768]{2,1,0:T(8,128)(2,1)S(1)}, bf16[1,128,768]{2,1,0:T(8,128)(2,1)}, u32[]{:S(2)}) %copy-start.5) | copy-done | bytes 196632
  12.2 0.7 %copy-done.7 = s32[1,8]{1,0:T(1,128)S(1)} copy-done((s32[1,8]{1,0:T(1,128)S(1)}, s32[1,8]{1,0:T(1,128)}, u32[]{:S(2)}) %copy-start.7) | copy-done | bytes 56
  12.9 1.3 %first.1 = (bf16[128,768]{1,0:T(8,128)(2,1)S(1)}, f32[128,768]{1,0:T(8,128)S(1)}, f32[1,8,768]{2,1,0:T(8,128)S(1)}, bf16[32,8,128]{2,1,0:T(8,128)(2,1)S(1)}) custom-call(bf16[128,768]{1,0:T(8,128)(2,1)S(1)} %bitcast.5, f32[2,768]{1,0:T(2,128)S(1)} %copy-done.3, bf16[768,768]{1,0:T(8,128)(2,1)S(1)} %copy-done, s32[1,8]{1,0:T(1,128)S(1)} %copy-done.7), custom_call_target="tpu_custom_call" | custom-call | tf_op jit(solution)/shard_map/first/pallas_call | solution.py:120
  14.2 1.3 %collective-permute-done.2.refs_0_.refs_1_ = bf16[128,768]{1,0:T(8,128)(2,1)S(1)} collective-permute-done((bf16[128,768]{1,0:T(8,128)(2,1)}, bf16[128,768]{1,0:T(8,128)(2,1)S(1)}, u32[]{:S(2)}, u32[]{:S(2)}) %collective-permute-start.2) | collective-permute-done | bytes 196640 | tf_op jit(solution)/shard_map/ppermute | solution.py:382
  15.5 1.6 %collective-permute-start.7 = (bf16[320,768]{1,0:T(8,128)(2,1)S(1)}, bf16[320,768]{1,0:T(8,128)(2,1)S(1)}, u32[]{:S(2)}, u32[]{:S(2)}) collective-permute-start(bf16[320,768]{1,0:T(8,128)(2,1)S(1)} %join.7), channel_id=1, source_target_pairs={{0,1},{1,0},{2,3},{3,2},{4,5},{5,4},{6,7},{7,6},{8,9},{9,8},{10,11... | collective-permute-start | bytes 1474568 | tf_op jit(solution)/shard_map/ppermute | solution.py:382
  17.2 1.6 %collective-permute-start.8 = (bf16[320,768]{1,0:T(8,128)(2,1)S(1)}, bf16[320,768]{1,0:T(8,128)(2,1)S(1)}, u32[]{:S(2)}, u32[]{:S(2)}) collective-permute-start(bf16[320,768]{1,0:T(8,128)(2,1)S(1)} %join.8), channel_id=1, source_target_pairs={{0,4},{1,5},{2,6},{3,7},{4,0},{5,1},{6,2},{7,3},{8,12},{9,13},{10,... | collective-permute-start | bytes 1474568 | tf_op jit(solution)/shard_map/ppermute | solution.py:382
  19.2 10.1 %all_to_all.5.rows_ref = bf16[32,8,128]{2,1,0:T(8,128)(2,1)S(1)} all-to-all(bf16[32,8,128]{2,1,0:T(8,128)(2,1)S(1)} %get-tuple-element.31), channel_id=1, replica_groups={{0,1,4,5,8,9,12,13,16,17,20,21,24,25,28,29,2,3,6,7,10,11,14,15,18,19,22..., dimensions={0} | all-to-all | bytes 131072 | tf_op jit(solution)/shard_map/all_to_all | solution.py:452
  29.3 0.7 %head.1 = (f32[16,768]{1,0:T(8,128)S(1)}, f32[16,768]{1,0:T(8,128)S(1)}) custom-call(bf16[32,8,128]{2,1,0:T(8,128)(2,1)S(1)} %all_to_all.5.rows_ref, bf16[512,768]{1,0:T(8,128)(2,1)S(1)} %copy-done.2, bf16[512]{0:T(512)(128)(2,1)S(1)} %copy-done.6), custom_call_target="tpu_custom_call" | custom-call | tf_op jit(solution)/shard_map/head/pallas_call | solution.py:465
  30.1 1.2 %collective-permute-done.refs_1_ = f32[16,768]{1,0:T(8,128)S(1)} collective-permute-done((f32[16,768]{1,0:T(8,128)S(1)}, f32[16,768]{1,0:T(8,128)S(1)}, u32[]{:S(2)}, u32[]{:S(2)}) %collective-permute-start) | collective-permute-done | bytes 49184 | tf_op jit(solution)/shard_map/ppermute | solution.py:382
  31.4 0.9 %collective-permute-start.13 = (bf16[256,768]{1,0:T(8,128)(2,1)S(1)}, bf16[256,768]{1,0:T(8,128)(2,1)S(1)}, u32[]{:S(2)}, u32[]{:S(2)}) collective-permute-start(bf16[256,768]{1,0:T(8,128)(2,1)S(1)} %join.11), channel_id=1, source_target_pairs={{0,4},{1,5},{2,6},{3,7},{4,0},{5,1},{6,2},{7,3},{8,12},{9,13},{10,... | collective-permute-start | bytes 1179656 | tf_op jit(solution)/shard_map/ppermute | solution.py:382
  32.9 2.4 %collective-permute-start.1 = (f32[16,768]{1,0:T(8,128)S(1)}, f32[16,768]{1,0:T(8,128)S(1)}, u32[]{:S(2)}, u32[]{:S(2)}) collective-permute-start(f32[16,768]{1,0:T(8,128)S(1)} %add.5.refs_0_.refs_2_), channel_id=1, source_target_pairs={{0,8},{1,9},{2,10},{3,11},{4,12},{5,13},{6,14},{7,15},{8,0},{9,1},... | collective-permute-start | bytes 147464 | tf_op jit(solution)/shard_map/ppermute | solution.py:382
  35.3 2.0 %encode.5 = (bf16[512,768]{1,0:T(8,128)(2,1)S(1)}, f32[512,768]{1,0:T(8,128)S(1)}, f32[4,8,768]{2,1,0:T(8,128)S(1)}) custom-call(bf16[128,768]{1,0:T(8,128)(2,1)S(1)} %collective-permute-done.2.refs_0_.refs_1_, bf16[128,768]{1,0:T(8,128)(2,1)S(1)} %collective-permute-done.3.refs_1_.refs_0_, bf16[128,768]{1,0:T(8,128)(2,1)S(1)} %collective-permute-done.4.refs_2_, ...), custom_call_target="tpu_custom_call" | custom-call | tf_op jit(solution)/shard_map/encode/pallas_call | solution.py:133
  37.4 2.0 %collective-permute-start.6 = (f32[16,768]{1,0:T(8,128)S(1)}, f32[16,768]{1,0:T(8,128)S(1)}, u32[]{:S(2)}, u32[]{:S(2)}) collective-permute-start(f32[16,768]{1,0:T(8,128)S(1)} %add.6.refs_0_), channel_id=1, source_target_pairs={{0,16},{1,17},{2,18},{3,19},{4,20},{5,21},{6,22},{7,23},{8,24},{9,... | collective-permute-start | bytes 147464 | tf_op jit(solution)/shard_map/ppermute | solution.py:382
  39.4 2.4 %encode.6 = (bf16[640,768]{1,0:T(8,128)(2,1)S(1)}, f32[640,768]{1,0:T(8,128)S(1)}, f32[5,8,768]{2,1,0:T(8,128)S(1)}) custom-call(bf16[320,768]{1,0:T(8,128)(2,1)S(1)} %collective-permute-done.7.refs_0_.refs_1_, bf16[320,768]{1,0:T(8,128)(2,1)S(1)} %collective-permute-done.8.refs_1_, f32[2,768]{1,0:T(2,128)S(1)} %copy-done.4, bf16[768,768]{1,0:T(8,128)(2,1)S(1)} %copy-done.1), custom_call_target="tpu_custom_call" | custom-call | tf_op jit(solution)/shard_map/encode/pallas_call | solution.py:133
  41.8 0.7 %collective-permute-done.6.refs_1_ = f32[16,768]{1,0:T(8,128)S(1)} collective-permute-done((f32[16,768]{1,0:T(8,128)S(1)}, f32[16,768]{1,0:T(8,128)S(1)}, u32[]{:S(2)}, u32[]{:S(2)}) %collective-permute-start.6) | collective-permute-done | bytes 49184 | tf_op jit(solution)/shard_map/ppermute | solution.py:382
  42.5 1.2 %collective-permute-start.9 = (f32[16,768]{1,0:T(8,128)S(1)}, f32[16,768]{1,0:T(8,128)S(1)}, u32[]{:S(2)}, u32[]{:S(2)}) collective-permute-start(f32[16,768]{1,0:T(8,128)S(1)} %add.7.refs_0_.refs_1_), channel_id=1, source_target_pairs={{0,1},{1,0},{2,3},{3,2},{4,5},{5,4},{6,7},{7,6},{8,9},{9,8},{10,11... | collective-permute-start | bytes 147464 | tf_op jit(solution)/shard_map/ppermute | solution.py:382
  43.7 1.0 %collective-permute-start.14 = (bf16[64,768]{1,0:T(8,128)(2,1)S(1)}, bf16[64,768]{1,0:T(8,128)(2,1)S(1)}, u32[]{:S(2)}, u32[]{:S(2)}) collective-permute-start(bf16[64,768]{1,0:T(8,128)(2,1)S(1)} %join.12), channel_id=1, source_target_pairs={{0,1},{1,0},{2,3},{3,2},{4,5},{5,4},{6,7},{7,6},{8,9},{9,8},{10,11... | collective-permute-start | bytes 294920 | tf_op jit(solution)/shard_map/ppermute | solution.py:382
  44.6 1.1 %collective-permute-start.15 = (bf16[64,768]{1,0:T(8,128)(2,1)S(1)}, bf16[64,768]{1,0:T(8,128)(2,1)S(1)}, u32[]{:S(2)}, u32[]{:S(2)}) collective-permute-start(bf16[64,768]{1,0:T(8,128)(2,1)S(1)} %join.13), channel_id=1, source_target_pairs={{0,4},{1,5},{2,6},{3,7},{4,0},{5,1},{6,2},{7,3},{8,12},{9,13},{10,... | collective-permute-start | bytes 294920 | tf_op jit(solution)/shard_map/ppermute | solution.py:382
  45.8 0.8 %encode.7 = (bf16[128,768]{1,0:T(8,128)(2,1)S(1)}, f32[128,768]{1,0:T(8,128)S(1)}, f32[1,8,768]{2,1,0:T(8,128)S(1)}) custom-call(bf16[128,768]{1,0:T(8,128)(2,1)S(1)} %collective-permute-done.10.refs_0_, f32[2,768]{1,0:T(2,128)S(1)} %copy-done.4, bf16[768,768]{1,0:T(8,128)(2,1)S(1)} %copy-done.1), custom_call_target="tpu_custom_call" | custom-call | tf_op jit(solution)/shard_map/encode/pallas_call | solution.py:133
  46.6 1.1 %collective-permute-start.11 = (f32[16,768]{1,0:T(8,128)S(1)}, f32[16,768]{1,0:T(8,128)S(1)}, u32[]{:S(2)}, u32[]{:S(2)}) collective-permute-start(f32[16,768]{1,0:T(8,128)S(1)} %add.8.refs_0_), channel_id=1, source_target_pairs={{0,4},{1,5},{2,6},{3,7},{4,0},{5,1},{6,2},{7,3},{8,12},{9,13},{10,... | collective-permute-start | bytes 147464 | tf_op jit(solution)/shard_map/ppermute | solution.py:382
  47.7 2.0 %encode.8 = (bf16[512,768]{1,0:T(8,128)(2,1)S(1)}, f32[512,768]{1,0:T(8,128)S(1)}, f32[4,8,768]{2,1,0:T(8,128)S(1)}) custom-call(bf16[256,768]{1,0:T(8,128)(2,1)S(1)} %collective-permute-done.12.refs_0_, bf16[256,768]{1,0:T(8,128)(2,1)S(1)} %collective-permute-done.13.refs_1_.refs_0_, f32[2,768]{1,0:T(2,128)S(1)} %copy-done.4, bf16[768,768]{1,0:T(8,128)(2,1)S(1)} %copy-done.1), custom_call_target="tpu_custom_call" | custom-call | tf_op jit(solution)/shard_map/encode/pallas_call | solution.py:133
  49.8 0.8 %encode.9 = (bf16[128,768]{1,0:T(8,128)(2,1)S(1)}, f32[128,768]{1,0:T(8,128)S(1)}, f32[1,8,768]{2,1,0:T(8,128)S(1)}) custom-call(bf16[64,768]{1,0:T(8,128)(2,1)S(1)} %collective-permute-done.14.refs_0_, bf16[64,768]{1,0:T(8,128)(2,1)S(1)} %collective-permute-done.15.refs_1_, f32[2,768]{1,0:T(2,128)S(1)} %copy-done.4, bf16[768,768]{1,0:T(8,128)(2,1)S(1)} %copy-done.1), custom_call_target="tpu_custom_call" | custom-call | tf_op jit(solution)/shard_map/encode/pallas_call | solution.py:133
  50.8 2.9 %back.1 = (bf16[400,768]{1,0:T(8,128)(2,1)S(1)}, f32[1,768]{1,0:T(1,128)}, bf16[2048,768]{1,0:T(8,128)(2,1)S(1)}, bf16[48,768]{1,0:T(8,128)(2,1)S(1)}, bf16[48,768]{1,0:T(8,128)(2,1)S(1)}) custom-call(f32[16,768]{1,0:T(8,128)S(1)} %add.9.refs_0_, f32[2,768]{1,0:T(2,128)S(1)} %copy-done.4, bf16[768,768]{1,0:T(8,128)(2,1)S(1)} %copy-done.1, ...), custom_call_target="tpu_custom_call" | custom-call | tf_op jit(solution)/shard_map/back/pallas_call | solution.py:307
  53.8 1.7 %more.1.refs_0_ = bf16[400,768]{1,0:T(8,128)(2,1)S(1)} custom-call(f32[2,768]{1,0:T(2,128)S(1)} %copy-done.4, bf16[768,768]{1,0:T(8,128)(2,1)S(1)} %copy-done.1, bf16[2048,768]{1,0:T(8,128)(2,1)S(1)} %get-tuple-element.53.refs_2_, bf16[48,768]{1,0:T(8,128)(2,1)S(1)} %get-tuple-element.54.refs_3_, bf16[48,768]{1,0:T(8,128)(2,1)S(1)} %get-tuple-element.55.refs_4_, ...), custom_call_target="tpu_custom_call" | custom-call | tf_op jit(solution)/shard_map/more/pallas_call | solution.py:327
  56.1 1.1 %final.2.refs_4_ = f32[768,768]{1,0:T(8,128)} custom-call(bf16[400,768]{1,0:T(8,128)(2,1)S(1)} %get-tuple-element.56.refs_0_.refs_2_, bf16[400,768]{1,0:T(8,128)(2,1)S(1)} %collective-permute-done.17.refs_1_.refs_3_), custom_call_target="tpu_custom_call" | custom-call | tf_op jit(solution)/shard_map/final/pallas_call | solution.py:365
  57.7 1.1 %final.3 = (f32[768,768]{1,0:T(8,128)}, f32[2,768]{1,0:T(2,128)}) custom-call(bf16[400,768]{1,0:T(8,128)(2,1)S(1)} %more.1.refs_0_, bf16[400,768]{1,0:T(8,128)(2,1)S(1)} %collective-permute-done.16.refs_1_, bf16[400,768]{1,0:T(8,128)(2,1)S(1)} %get-tuple-element.56.refs_0_.refs_2_, ...), custom_call_target="tpu_custom_call", output_to_operand_aliasing={{0}: (4, {})} | custom-call | tf_op jit(solution)/shard_map/final/pallas_call | solution.py:365
  (45 shorter events, 2.9 us)
Async XLA Ops:
  0.6 28.7 %copy-start.6 = (bf16[512]{0:T(512)(128)(2,1)S(1)}, bf16[512]{0:T(512)(128)(2,1)}, u32[]{:S(2)}) copy-start(bf16[512]{0:T(512)(128)(2,1)} %bias_ref.1) | copy-start | bytes 3076
  0.6 13.5 %collective-permute-start.3 = (bf16[128,768]{1,0:T(8,128)(2,1)}, bf16[128,768]{1,0:T(8,128)(2,1)S(1)}, u32[]{:S(2)}, u32[]{:S(2)}) collective-permute-start(bf16[128,768]{1,0:T(8,128)(2,1)} %bitcast.1), channel_id=1, source_target_pairs={{0,8},{1,9},{2,10},{3,11},{4,12},{5,13},{6,14},{7,15},{8,0},{9,1},... | collective-permute-start | bytes 589832 | tf_op jit(solution)/shard_map/ppermute | solution.py:382
  3.7 11.7 %collective-permute-start.2 = (bf16[128,768]{1,0:T(8,128)(2,1)}, bf16[128,768]{1,0:T(8,128)(2,1)S(1)}, u32[]{:S(2)}, u32[]{:S(2)}) collective-permute-start(bf16[128,768]{1,0:T(8,128)(2,1)} %bitcast.2), channel_id=1, source_target_pairs={{0,16},{1,17},{2,18},{3,19},{4,20},{5,21},{6,22},{7,23},{8,24},{9,... | collective-permute-start | bytes 589832 | tf_op jit(solution)/shard_map/ppermute | solution.py:382
  6.3 9.2 %collective-permute-start.5 = (bf16[128,768]{1,0:T(8,128)(2,1)}, bf16[128,768]{1,0:T(8,128)(2,1)S(1)}, u32[]{:S(2)}, u32[]{:S(2)}) collective-permute-start(bf16[128,768]{1,0:T(8,128)(2,1)} %bitcast.3), channel_id=1, source_target_pairs={{0,4},{1,5},{2,6},{3,7},{4,0},{5,1},{6,2},{7,3},{8,12},{9,13},{10,... | collective-permute-start | bytes 589832 | tf_op jit(solution)/shard_map/ppermute | solution.py:382
  7.8 9.3 %collective-permute-start.4 = (bf16[128,768]{1,0:T(8,128)(2,1)}, bf16[128,768]{1,0:T(8,128)(2,1)S(1)}, u32[]{:S(2)}, u32[]{:S(2)}) collective-permute-start(bf16[128,768]{1,0:T(8,128)(2,1)} %bitcast.4), channel_id=1, source_target_pairs={{0,1},{1,0},{2,3},{3,2},{4,5},{5,4},{6,7},{7,6},{8,9},{9,8},{10,11... | collective-permute-start | bytes 589832 | tf_op jit(solution)/shard_map/ppermute | solution.py:382
  9.3 1.3 %copy-start = (bf16[768,768]{1,0:T(8,128)(2,1)S(1)}, bf16[768,768]{1,0:T(8,128)(2,1)}, u32[]{:S(2)}) copy-start(bf16[768,768]{1,0:T(8,128)(2,1)} %refs_1_.7) | copy-start | bytes 3538948
  10.6 0.7 %copy-start.3 = (f32[2,768]{1,0:T(2,128)S(1)}, f32[2,768]{1,0:T(2,128)}, u32[]{:S(2)}) copy-start(f32[2,768]{1,0:T(2,128)} %refs_0_.1) | copy-start | bytes 18436
  11.3 0.9 %copy-start.5 = (bf16[1,128,768]{2,1,0:T(8,128)(2,1)S(1)}, bf16[1,128,768]{2,1,0:T(8,128)(2,1)}, u32[]{:S(2)}) copy-start(bf16[1,128,768]{2,1,0:T(8,128)(2,1)} %param.6) | copy-start | bytes 589828
  12.2 0.7 %copy-start.7 = (s32[1,8]{1,0:T(1,128)S(1)}, s32[1,8]{1,0:T(1,128)}, u32[]{:S(2)}) copy-start(s32[1,8]{1,0:T(1,128)} %refs_3_.4) | copy-start | bytes 100
  12.9 16.4 %copy-start.2 = (bf16[512,768]{1,0:T(8,128)(2,1)S(1)}, bf16[512,768]{1,0:T(8,128)(2,1)}, u32[]{:S(2)}) copy-start(bf16[512,768]{1,0:T(8,128)(2,1)} %weight_ref.1) | copy-start | bytes 2359300
  15.5 15.8 %collective-permute-start.7 = (bf16[320,768]{1,0:T(8,128)(2,1)S(1)}, bf16[320,768]{1,0:T(8,128)(2,1)S(1)}, u32[]{:S(2)}, u32[]{:S(2)}) collective-permute-start(bf16[320,768]{1,0:T(8,128)(2,1)S(1)} %join.7), channel_id=1, source_target_pairs={{0,1},{1,0},{2,3},{3,2},{4,5},{5,4},{6,7},{7,6},{8,9},{9,8},{10,11... | collective-permute-start | bytes 1474568 | tf_op jit(solution)/shard_map/ppermute | solution.py:382
  17.1 18.2 %copy-start.1 = (bf16[768,768]{1,0:T(8,128)(2,1)S(1)}, bf16[768,768]{1,0:T(8,128)(2,1)}, u32[]{:S(2)}) copy-start(bf16[768,768]{1,0:T(8,128)(2,1)} %refs_1_.7) | copy-start | bytes 3538948
  17.2 18.2 %copy-start.4 = (f32[2,768]{1,0:T(2,128)S(1)}, f32[2,768]{1,0:T(2,128)}, u32[]{:S(2)}) copy-start(f32[2,768]{1,0:T(2,128)} %refs_0_.1) | copy-start | bytes 18436
  17.2 15.1 %collective-permute-start.8 = (bf16[320,768]{1,0:T(8,128)(2,1)S(1)}, bf16[320,768]{1,0:T(8,128)(2,1)S(1)}, u32[]{:S(2)}, u32[]{:S(2)}) collective-permute-start(bf16[320,768]{1,0:T(8,128)(2,1)S(1)} %join.8), channel_id=1, source_target_pairs={{0,4},{1,5},{2,6},{3,7},{4,0},{5,1},{6,2},{7,3},{8,12},{9,13},{10,... | collective-permute-start | bytes 1474568 | tf_op jit(solution)/shard_map/ppermute | solution.py:382
  18.7 12.6 %collective-permute-start.10 = (bf16[128,768]{1,0:T(8,128)(2,1)S(1)}, bf16[128,768]{1,0:T(8,128)(2,1)S(1)}, u32[]{:S(2)}, u32[]{:S(2)}) collective-permute-start(bf16[128,768]{1,0:T(8,128)(2,1)S(1)} %join.9), channel_id=1, source_target_pairs={{0,8},{1,9},{2,10},{3,11},{4,12},{5,13},{6,14},{7,15},{8,0},{9,1},... | collective-permute-start | bytes 589832 | tf_op jit(solution)/shard_map/ppermute | solution.py:382
  30.0 1.3 %collective-permute-start = (f32[16,768]{1,0:T(8,128)S(1)}, f32[16,768]{1,0:T(8,128)S(1)}, u32[]{:S(2)}, u32[]{:S(2)}) collective-permute-start(f32[16,768]{1,0:T(8,128)S(1)} %get-tuple-element.33), channel_id=1, source_target_pairs={{0,2},{1,3},{2,0},{3,1},{4,6},{5,7},{6,4},{7,5},{8,10},{9,11},{10,... | collective-permute-start | bytes 147464 | tf_op jit(solution)/shard_map/ppermute | solution.py:382
  31.4 12.2 %collective-permute-start.13 = (bf16[256,768]{1,0:T(8,128)(2,1)S(1)}, bf16[256,768]{1,0:T(8,128)(2,1)S(1)}, u32[]{:S(2)}, u32[]{:S(2)}) collective-permute-start(bf16[256,768]{1,0:T(8,128)(2,1)S(1)} %join.11), channel_id=1, source_target_pairs={{0,4},{1,5},{2,6},{3,7},{4,0},{5,1},{6,2},{7,3},{8,12},{9,13},{10,... | collective-permute-start | bytes 1179656 | tf_op jit(solution)/shard_map/ppermute | solution.py:382
  32.3 12.3 %collective-permute-start.12 = (bf16[256,768]{1,0:T(8,128)(2,1)S(1)}, bf16[256,768]{1,0:T(8,128)(2,1)S(1)}, u32[]{:S(2)}, u32[]{:S(2)}) collective-permute-start(bf16[256,768]{1,0:T(8,128)(2,1)S(1)} %join.10), channel_id=1, source_target_pairs={{0,1},{1,0},{2,3},{3,2},{4,5},{5,4},{6,7},{7,6},{8,9},{9,8},{10,11... | collective-permute-start | bytes 1179656 | tf_op jit(solution)/shard_map/ppermute | solution.py:382
  32.9 4.5 %collective-permute-start.1 = (f32[16,768]{1,0:T(8,128)S(1)}, f32[16,768]{1,0:T(8,128)S(1)}, u32[]{:S(2)}, u32[]{:S(2)}) collective-permute-start(f32[16,768]{1,0:T(8,128)S(1)} %add.5.refs_0_.refs_2_), channel_id=1, source_target_pairs={{0,8},{1,9},{2,10},{3,11},{4,12},{5,13},{6,14},{7,15},{8,0},{9,1},... | collective-permute-start | bytes 147464 | tf_op jit(solution)/shard_map/ppermute | solution.py:382
  37.4 5.0 %collective-permute-start.6 = (f32[16,768]{1,0:T(8,128)S(1)}, f32[16,768]{1,0:T(8,128)S(1)}, u32[]{:S(2)}, u32[]{:S(2)}) collective-permute-start(f32[16,768]{1,0:T(8,128)S(1)} %add.6.refs_0_), channel_id=1, source_target_pairs={{0,16},{1,17},{2,18},{3,19},{4,20},{5,21},{6,22},{7,23},{8,24},{9,... | collective-permute-start | bytes 147464 | tf_op jit(solution)/shard_map/ppermute | solution.py:382
  42.5 4.2 %collective-permute-start.9 = (f32[16,768]{1,0:T(8,128)S(1)}, f32[16,768]{1,0:T(8,128)S(1)}, u32[]{:S(2)}, u32[]{:S(2)}) collective-permute-start(f32[16,768]{1,0:T(8,128)S(1)} %add.7.refs_0_.refs_1_), channel_id=1, source_target_pairs={{0,1},{1,0},{2,3},{3,2},{4,5},{5,4},{6,7},{7,6},{8,9},{9,8},{10,11... | collective-permute-start | bytes 147464 | tf_op jit(solution)/shard_map/ppermute | solution.py:382
  43.7 6.1 %collective-permute-start.14 = (bf16[64,768]{1,0:T(8,128)(2,1)S(1)}, bf16[64,768]{1,0:T(8,128)(2,1)S(1)}, u32[]{:S(2)}, u32[]{:S(2)}) collective-permute-start(bf16[64,768]{1,0:T(8,128)(2,1)S(1)} %join.12), channel_id=1, source_target_pairs={{0,1},{1,0},{2,3},{3,2},{4,5},{5,4},{6,7},{7,6},{8,9},{9,8},{10,11... | collective-permute-start | bytes 294920 | tf_op jit(solution)/shard_map/ppermute | solution.py:382
  44.6 5.1 %collective-permute-start.15 = (bf16[64,768]{1,0:T(8,128)(2,1)S(1)}, bf16[64,768]{1,0:T(8,128)(2,1)S(1)}, u32[]{:S(2)}, u32[]{:S(2)}) collective-permute-start(bf16[64,768]{1,0:T(8,128)(2,1)S(1)} %join.13), channel_id=1, source_target_pairs={{0,4},{1,5},{2,6},{3,7},{4,0},{5,1},{6,2},{7,3},{8,12},{9,13},{10,... | collective-permute-start | bytes 294920 | tf_op jit(solution)/shard_map/ppermute | solution.py:382
  46.6 4.2 %collective-permute-start.11 = (f32[16,768]{1,0:T(8,128)S(1)}, f32[16,768]{1,0:T(8,128)S(1)}, u32[]{:S(2)}, u32[]{:S(2)}) collective-permute-start(f32[16,768]{1,0:T(8,128)S(1)} %add.8.refs_0_), channel_id=1, source_target_pairs={{0,4},{1,5},{2,6},{3,7},{4,0},{5,1},{6,2},{7,3},{8,12},{9,13},{10,... | collective-permute-start | bytes 147464 | tf_op jit(solution)/shard_map/ppermute | solution.py:382
  53.7 2.3 %collective-permute-start.17 = (bf16[400,768]{1,0:T(8,128)(2,1)S(1)}, bf16[400,768]{1,0:T(8,128)(2,1)S(1)}, u32[]{:S(2)}, u32[]{:S(2)}) collective-permute-start(bf16[400,768]{1,0:T(8,128)(2,1)S(1)} %get-tuple-element.56.refs_0_.refs_2_), channel_id=1, source_target_pairs={{0,2},{1,3},{2,0},{3,1},{4,6},{5,7},{6,4},{7,5},{8,10},{9,11},{10,... | collective-permute-start | bytes 1843208 | tf_op jit(solution)/shard_map/ppermute | solution.py:382
  55.5 2.2 %collective-permute-start.16 = (bf16[400,768]{1,0:T(8,128)(2,1)S(1)}, bf16[400,768]{1,0:T(8,128)(2,1)S(1)}, u32[]{:S(2)}, u32[]{:S(2)}) collective-permute-start(bf16[400,768]{1,0:T(8,128)(2,1)S(1)} %more.1.refs_0_), channel_id=1, source_target_pairs={{0,2},{1,3},{2,0},{3,1},{4,6},{5,7},{6,4},{7,5},{8,10},{9,11},{10,... | collective-permute-start | bytes 1843208 | tf_op jit(solution)/shard_map/ppermute | solution.py:382
